TPU v7x, 32 devices: a whole 2x2x4 slice. The times are simulated.
32 devices in a mesh: dp: 8 (over y, x, core), tensor: 4 (over z).
Axes of the slice: x: 2, y: 2, z: 4, core: 2. Of those that a mesh axis runs over, the one named last changes fastest.
Arguments:
- block_input: bfloat16 [4096, 1024], P(('dp', 'tensor')), may hold values from -6 to 6
- output_cotangent: bfloat16 [4096, 1024], P(('dp', 'tensor')), may hold values from -6 to 6
- first_gain: bfloat16 [1024], replicated, may hold values from 0.5 to 1.5
- first_shift: bfloat16 [1024], replicated, may hold values from -4 to 4
- project_in: bfloat16 [1024, 3, 1024], P('dp', None, 'tensor'), may hold values from -0.1875 to 0.1875
- query_value_bias: bfloat16 [2, 1024], P(None, 'tensor'), may hold values from -4 to 4
- project_out: bfloat16 [1024, 1024], P('tensor', 'dp'), may hold values from -0.5 to 0.5
- project_out_bias: bfloat16 [1024], replicated, may hold values from -4 to 4
- second_gain: bfloat16 [1024], replicated, may hold values from 0.5 to 1.5
- second_shift: bfloat16 [1024], replicated, may hold values from -4 to 4
- expand_weight: bfloat16 [1024, 4096], P('dp', 'tensor'), may hold values from -0.1875 to 0.1875
- expand_bias: bfloat16 [4096], P('tensor'), may hold values from -4 to 4
- shrink_weight: bfloat16 [4096, 1024], P('tensor', 'dp'), may hold values from -0.125 to 0.125
- shrink_bias: bfloat16 [1024], replicated, may hold values from -4 to 4
Outputs:
- block_output: bfloat16 [4096, 1024], P(('dp', 'tensor'))
- input_grad: bfloat16 [4096, 1024], P(('dp', 'tensor'))
- first_gain_grad: float32 [1024], replicated
- first_shift_grad: float32 [1024], replicated
- project_in_grad: float32 [1024, 3, 1024], P('dp', None, 'tensor')
- query_value_bias_grad: float32 [2, 1024], P(None, 'tensor')
- project_out_grad: float32 [1024, 1024], P('tensor', 'dp')
- project_out_bias_grad: float32 [1024], replicated
- second_gain_grad: float32 [1024], replicated
- second_shift_grad: float32 [1024], replicated
- expand_weight_grad: float32 [1024, 4096], P('dp', 'tensor')
- expand_bias_grad: float32 [4096], P('tensor')
- shrink_weight_grad: float32 [4096, 1024], P('tensor', 'dp')
- shrink_bias_grad: float32 [1024], replicated
All inputs are finite; a program needn't handle non-finite values.
Results may differ from a plain program's by a relative error of at most 0.019.
Values may be sent and summed in bfloat16 or wider, within the bound.
No kernel may reach another device: no remote copies, remote signals or barrier semaphores. Data moves between devices by JAX's collectives and lax.ppermute only.
A program may use at most 64 MiB of HBM per device.

v0:
```python
import jax
import jax.numpy as jnp
from jax import lax
from jax.sharding import PartitionSpec as P

HEADS = 16
HEAD = 64


def layer_norm(values, norm_gain, norm_shift):
    average = jnp.mean(values, axis=-1, keepdims=True)
    centered = values - average
    variance = jnp.mean(centered * centered, axis=-1, keepdims=True)
    return centered * lax.rsqrt(variance + 1e-05) * norm_gain + norm_shift


def gelu_local(hidden):
    return jax.nn.gelu(hidden, approximate=True)


def score_block(queries, keys_all, first_head):
    seq_len = queries.shape[0]
    heads_local = queries.shape[1]
    product = jnp.einsum("qhd,khd->hqk", queries, keys_all, preferred_element_type=jnp.float32)
    position = jnp.arange(seq_len)
    distance = (position[:, None] - position[None, :]).astype(jnp.float32)
    head_ids = (first_head + jnp.arange(heads_local) + 1).astype(jnp.float32)
    slopes = jnp.exp2(-8.0 * head_ids / HEADS)
    scores = product * HEAD ** (-0.5) - slopes[:, None, None] * distance[None]
    return jnp.where(distance[None] >= 0, scores, -1e30)


def body(
    block_input,
    output_cotangent,
    first_gain,
    first_shift,
    project_in,
    query_value_bias,
    project_out,
    project_out_bias,
    second_gain,
    second_shift,
    expand_weight,
    expand_bias,
    shrink_weight,
    shrink_bias,
):
    single = jnp.float32
    rows_in = block_input.astype(single)
    gain_one = first_gain.astype(single)
    shift_one = first_shift.astype(single)
    gain_two = second_gain.astype(single)
    shift_two = second_shift.astype(single)
    bias_qv = query_value_bias.astype(single)
    bias_out = project_out_bias.astype(single)
    bias_expand = expand_bias.astype(single)
    bias_shrink = shrink_bias.astype(single)
    full_in, full_out, full_expand, full_shrink = (
        lax.all_gather(project_in, "dp", axis=0, tiled=True),
        lax.all_gather(project_out, "dp", axis=1, tiled=True),
        lax.all_gather(expand_weight, "dp", axis=0, tiled=True),
        lax.all_gather(shrink_weight, "dp", axis=1, tiled=True),
    )
    normed_one, pull_one = jax.vjp(layer_norm, rows_in, gain_one, shift_one)
    normed_all = lax.all_gather(normed_one.astype(jnp.bfloat16), "tensor", axis=0, tiled=True)
    seq_len = normed_all.shape[0]
    dim_local = project_out.shape[0]
    heads_local = dim_local // HEAD
    first_head = lax.axis_index("tensor") * heads_local
    mixed = jnp.einsum("sd,dcf->scf", normed_all, full_in, preferred_element_type=single)
    bias_full = jnp.stack([bias_qv[0], jnp.zeros_like(bias_qv[0]), bias_qv[1]])
    mixed_low = (mixed + bias_full).astype(jnp.bfloat16)
    shaped = mixed_low.reshape(seq_len, 3, heads_local, HEAD)
    queries = shaped[:, 0]
    keys_all = shaped[:, 1]
    values_all = shaped[:, 2]
    scores = score_block(queries, keys_all, first_head)
    top_score = jnp.max(scores, axis=-1, keepdims=True)
    log_total = top_score + jnp.log(jnp.sum(jnp.exp(scores - top_score), axis=-1, keepdims=True))
    soft_low = jnp.exp(scores - log_total).astype(jnp.bfloat16)
    context = jnp.einsum("hqk,khd->qhd", soft_low, values_all, preferred_element_type=single)
    context = context.reshape(seq_len, dim_local).astype(jnp.bfloat16)
    branch_part = jnp.dot(context, full_out, preferred_element_type=single)
    branch = (
        lax.psum_scatter(
            branch_part.astype(jnp.bfloat16), "tensor", scatter_dimension=0, tiled=True
        ).astype(jnp.float32)
        + bias_out
    )
    middle = rows_in + branch
    normed_two, pull_two = jax.vjp(layer_norm, middle, gain_two, shift_two)
    second_all = lax.all_gather(normed_two.astype(jnp.bfloat16), "tensor", axis=0, tiled=True)
    hidden = jnp.dot(second_all, full_expand, preferred_element_type=single) + bias_expand
    active, gelu_pull = jax.vjp(gelu_local, hidden)
    active_low = active.astype(jnp.bfloat16)
    shrink_part = jnp.dot(active_low, full_shrink, preferred_element_type=single)
    result = (
        middle
        + lax.psum_scatter(
            shrink_part.astype(jnp.bfloat16), "tensor", scatter_dimension=0, tiled=True
        ).astype(jnp.float32)
        + bias_shrink
    )
    upstream = output_cotangent.astype(single)
    upstream_all = lax.all_gather(upstream.astype(jnp.bfloat16), "tensor", axis=0, tiled=True)
    back_in, back_out, back_expand, back_shrink = (
        lax.all_gather(project_in, "dp", axis=0, tiled=True),
        lax.all_gather(project_out, "dp", axis=1, tiled=True),
        lax.all_gather(expand_weight, "dp", axis=0, tiled=True),
        lax.all_gather(shrink_weight, "dp", axis=1, tiled=True),
    )
    shrink_grad = jnp.einsum("sf,sd->fd", active_low, upstream_all, preferred_element_type=single)
    active_grad = jnp.einsum("sd,fd->sf", upstream_all, back_shrink, preferred_element_type=single)
    (hidden_grad,) = gelu_pull(active_grad)
    hidden_low = hidden_grad.astype(jnp.bfloat16)
    expand_bias_part = jnp.sum(hidden_low.astype(single), axis=0)
    expand_grad = jnp.einsum("sd,sf->df", second_all, hidden_low, preferred_element_type=single)
    second_part = jnp.einsum("sf,df->sd", hidden_low, back_expand, preferred_element_type=single)
    second_grad = lax.psum_scatter(
        second_part.astype(jnp.bfloat16), "tensor", scatter_dimension=0, tiled=True
    ).astype(jnp.float32)
    middle_back, gain_two_grad, shift_two_grad = pull_two(second_grad)
    middle_grad = upstream + middle_back
    middle_all = lax.all_gather(middle_grad.astype(jnp.bfloat16), "tensor", axis=0, tiled=True)
    out_grad = jnp.einsum("sf,sd->fd", context, middle_all, preferred_element_type=single)
    context_grad = jnp.einsum("sd,fd->sf", middle_all, back_out, preferred_element_type=single)
    context_grad = context_grad.astype(jnp.bfloat16).reshape(seq_len, heads_local, HEAD)
    again_scores = score_block(queries, keys_all, first_head)
    soft_again = jnp.exp(again_scores - log_total)
    soft_again_low = soft_again.astype(jnp.bfloat16)
    value_grad = jnp.einsum(
        "hqk,qhd->khd", soft_again_low, context_grad, preferred_element_type=single
    )
    soft_grad = jnp.einsum("qhd,khd->hqk", context_grad, values_all, preferred_element_type=single)
    score_grad = soft_again * (soft_grad - jnp.sum(soft_again * soft_grad, axis=-1, keepdims=True))
    score_low = score_grad.astype(jnp.bfloat16)
    query_grad = jnp.einsum(
        "hqk,khd->qhd", score_low, keys_all, preferred_element_type=single
    ) * HEAD ** (-0.5)
    key_grad = jnp.einsum(
        "hqk,qhd->khd", score_low, queries, preferred_element_type=single
    ) * HEAD ** (-0.5)
    mixed_grad = jnp.stack([query_grad, key_grad, value_grad], axis=1).reshape(
        seq_len, 3, dim_local
    )
    mixed_grad = mixed_grad.astype(jnp.bfloat16)
    mixed_sums = jnp.sum(mixed_grad.astype(single), axis=0)
    bias_qv_part = jnp.stack([mixed_sums[0], mixed_sums[2]])
    in_grad = jnp.einsum("sd,scf->dcf", normed_all, mixed_grad, preferred_element_type=single)
    first_part = jnp.einsum("scf,dcf->sd", mixed_grad, back_in, preferred_element_type=single)
    first_grad = lax.psum_scatter(
        first_part.astype(jnp.bfloat16), "tensor", scatter_dimension=0, tiled=True
    ).astype(jnp.float32)
    rows_back, gain_one_grad, shift_one_grad = pull_one(first_grad)
    input_grad = (middle_grad + rows_back).astype(jnp.bfloat16)
    out_bias_part = jnp.sum(middle_grad, axis=0)
    shrink_bias_part = jnp.sum(upstream, axis=0)
    in_sum, out_sum, expand_sum, shrink_sum = (
        lax.psum_scatter(in_grad, "dp", scatter_dimension=0, tiled=True),
        lax.psum_scatter(out_grad, "dp", scatter_dimension=1, tiled=True),
        lax.psum_scatter(expand_grad, "dp", scatter_dimension=0, tiled=True),
        lax.psum_scatter(shrink_grad, "dp", scatter_dimension=1, tiled=True),
    )
    bias_qv_sum, expand_bias_sum = lax.psum((bias_qv_part, expand_bias_part), "dp")
    gain_one_sum, shift_one_sum, out_bias_sum, gain_two_sum, shift_two_sum, shrink_bias_sum = (
        lax.psum(
            (
                gain_one_grad,
                shift_one_grad,
                out_bias_part,
                gain_two_grad,
                shift_two_grad,
                shrink_bias_part,
            ),
            ("dp", "tensor"),
        )
    )
    return (
        result.astype(jnp.bfloat16),
        input_grad,
        gain_one_sum,
        shift_one_sum,
        in_sum,
        bias_qv_sum,
        out_sum,
        out_bias_sum,
        gain_two_sum,
        shift_two_sum,
        expand_sum,
        expand_bias_sum,
        shrink_sum,
        shrink_bias_sum,
    )


def solution(mesh):
    placed = (
        P(("dp", "tensor"), None),
        P(("dp", "tensor"), None),
        P(),
        P(),
        P("dp", None, "tensor"),
        P(None, "tensor"),
        P("tensor", "dp"),
        P(),
        P(),
        P(),
        P("dp", "tensor"),
        P("tensor"),
        P("tensor", "dp"),
        P(),
    )
    return jax.shard_map(
        body,
        mesh=mesh,
        in_specs=placed,
        out_specs=(
            P(("dp", "tensor"), None),
            P(("dp", "tensor"), None),
            P(),
            P(),
            P("dp", None, "tensor"),
            P(None, "tensor"),
            P("tensor", "dp"),
            P(),
            P(),
            P(),
            P("dp", "tensor"),
            P("tensor"),
            P("tensor", "dp"),
            P(),
        ),
        check_vma=False,
    )
```

profile of v0, /device:TPU:0, one launch (start us, length us, event | category | flops | bytes accessed | tf_op | source)
XLA Modules:
  0.0 564.0 jit_solution(2721932516512304324)
XLA Ops:
  10.9 1.9 fusion.24
  12.8 1.7 copy.28
  14.7 11.7 %all_gather.30 = bf16[256,1024]{1,0:T(8,128)(2,1)S(1)} all-gather(bf16[256,128]{1,0:T(8,128)(2,1)} %param.20), channel_id=1, replica_groups=mesh['dp'=8,'tensor'=4] {'dp'}, dimensions={1}, use_global_device_ids=true | all-gather | bytes 589824 | tf_op jit(solution)/shard_map/all_gather | solution.py:61
  27.9 15.7 %all-gather.8.cloned.1.call-done = bf16[512,1024]{1,0:T(8,128)(2,1)} async-done(((bf16[128,1024]{1,0:T(8,128)(2,1)}), bf16[512,1024]{1,0:T(8,128)(2,1)}) %all-gather.8.cloned.1.call-update) | async-done | bytes 1048592 | tf_op jit(solution)/shard_map/all_gather | solution.py:66
  43.6 27.9 %all-gather.10.cloned.1.call-done = bf16[1024,3,256]{0,2,1:T(8,128)(2,1)} async-done(((bf16[128,3,256]{0,2,1:T(8,128)(2,1)}), bf16[1024,3,256]{0,2,1:T(8,128)(2,1)}) %all-gather.10.cloned.1.call-update) | async-done | bytes 1572880 | tf_op jit(solution)/shard_map/all_gather | solution.py:60
  71.4 2.7 add_convert_fusion
  74.2 2.6 fusion.42
  81.8 26.6 %reduce-scatter.9.cloned.1.call-done = bf16[128,1024]{1,0:T(8,128)(2,1)} async-done(((bf16[512,1024]{1,0:T(8,128)(2,1)}), bf16[128,1024]{1,0:T(8,128)(2,1)}) %reduce-scatter.9.cloned.1.call-update) | async-done | bytes 262160 | tf_op jit(solution)/shard_map/reduce_scatter | solution.py:86
  110.7 1.8 add_convert_fusion.3
  113.9 22.9 %all-gather.14.cloned.1.call-done = bf16[1024,1024]{1,0:T(8,128)(2,1)} async-done(((bf16[128,1024]{1,0:T(8,128)(2,1)}), bf16[1024,1024]{1,0:T(8,128)(2,1)}) %all-gather.14.cloned.1.call-update) | async-done | bytes 2097168 | tf_op jit(solution)/shard_map/all_gather | solution.py:62
  136.8 30.0 %all-gather.12.cloned.1.call-done = bf16[512,1024]{1,0:T(8,128)(2,1)} async-done(((bf16[128,1024]{1,0:T(8,128)(2,1)}), bf16[512,1024]{1,0:T(8,128)(2,1)}) %all-gather.12.cloned.1.call-update) | async-done | bytes 1048592 | tf_op jit(solution)/shard_map/all_gather | solution.py:93
  166.9 4.5 fusion.43
  171.4 24.5 %all-gather.18.cloned.1.call-done = bf16[512,1024]{1,0:T(8,128)(2,1)} async-done(((bf16[128,1024]{1,0:T(8,128)(2,1)}), bf16[512,1024]{1,0:T(8,128)(2,1)}) %all-gather.18.cloned.1.call-update) | async-done | bytes 1048592 | tf_op jit(solution)/shard_map/all_gather | solution.py:106
  195.8 29.8 %all-gather.16.cloned.1.call-done = bf16[1024,1024]{1,0:T(8,128)(2,1)} async-done(((bf16[1024,128]{1,0:T(8,128)(2,1)}), bf16[1024,1024]{1,0:T(8,128)(2,1)}) %all-gather.16.cloned.1.call-update) | async-done | bytes 2097168 | tf_op jit(solution)/shard_map/all_gather | solution.py:63
  225.6 5.2 convert_reduce_fusion
  231.7 2.3 convolution_convert_fusion
  234.2 4.8 convolution_convert_fusion.1
  239.2 22.2 %reduce-scatter.13.cloned.1.call-done = bf16[128,1024]{1,0:T(8,128)(2,1)} async-done(((bf16[512,1024]{1,0:T(8,128)(2,1)}), bf16[128,1024]{1,0:T(8,128)(2,1)}) %reduce-scatter.13.cloned.1.call-update) | async-done | bytes 262160 | tf_op jit(solution)/shard_map/reduce_scatter | solution.py:120
  264.0 25.5 %reduce-scatter.11.cloned.1.call-done = bf16[128,1024]{1,0:T(8,128)(2,1)} async-done(((bf16[512,1024]{1,0:T(8,128)(2,1)}), bf16[128,1024]{1,0:T(8,128)(2,1)}) %reduce-scatter.11.cloned.1.call-update) | async-done | bytes 262160 | tf_op jit(solution)/shard_map/reduce_scatter | solution.py:100
  289.5 2.1 fusion.39
  292.4 26.7 %all-gather.20.cloned.1.call-done = bf16[512,1024]{1,0:T(8,128)(2,1)} async-done(((bf16[128,1024]{1,0:T(8,128)(2,1)}), bf16[512,1024]{1,0:T(8,128)(2,1)}) %all-gather.20.cloned.1.call-update) | async-done | bytes 1048592 | tf_op jit(solution)/shard_map/all_gather | solution.py:125
  320.8 3.1 convolution_convert_fusion.3
  328.1 3.5 bitcast_convert_fusion
  333.1 5.4 fusion.37
  339.8 4.6 fusion.45
  345.6 2.7 fusion.10
  348.5 14.3 %all-reduce.1 = (f32[2,256]{1,0:T(2,128)}, f32[1024]{0:T(1024)}) all-reduce(f32[2,256]{1,0:T(2,128)S(1)} %pad_maximum_fusion.2, f32[1024]{0:T(1024)S(1)} %get-tuple-element.30), channel_id=1, replica_groups=mesh['dp'=8,'tensor'=4] {'dp'}, use_global_device_ids=true, to_apply=%region_21.22 | all-reduce | flops 1536 | bytes 12288 | tf_op jit(solution)/shard_map/psum | solution.py:165
  365.3 39.7 %all-reduce = (f32[1024]{0:T(1024)}, f32[1024]{0:T(1024)}, f32[1024]{0:T(1024)}, f32[1024]{0:T(1024)}, f32[1024]{0:T(1024)}, /*index=5*/f32[1024]{0:T(1024)}) all-reduce(f32[1024]{0:T(1024)S(1)} %get-tuple-element.16, f32[1024]{0:T(1024)S(1)} %get-tuple-element.20, ...), channel_id=1, replica_groups=mesh['dp'=8,'tensor'=4] {'dp','tensor'}, use_global_device_ids=true, to_apply=%region_16.17 | all-reduce | flops 6144 | bytes 49152 | tf_op jit(solution)/shard_map/psum | solution.py:167
  405.0 2.0 add_convert_fusion.1
  407.0 44.9 %reduce-scatter.23.cloned.1.call-done = f32[1024,128]{1,0:T(8,128)} async-done(((f32[1024,1024]{1,0:T(8,128)}), f32[1024,128]{1,0:T(8,128)}) %reduce-scatter.23.cloned.1.call-update) | async-done | bytes 524304 | tf_op jit(solution)/shard_map/reduce_scatter | solution.py:163
  451.9 55.6 %reduce-scatter.21.cloned.1.call-done = f32[128,1024]{1,0:T(8,128)} async-done(((f32[1024,1024]{1,0:T(8,128)}), f32[128,1024]{1,0:T(8,128)}) %reduce-scatter.21.cloned.1.call-update) | async-done | bytes 524304 | tf_op jit(solution)/shard_map/reduce_scatter | solution.py:162
  507.4 50.1 %reduce-scatter.17.cloned.1.call-done = f32[128,3,256]{2,0,1:T(8,128)} async-done(((f32[1024,3,256]{2,0,1:T(8,128)}), f32[128,3,256]{2,0,1:T(8,128)}) %reduce-scatter.17.cloned.1.call-update) | async-done | bytes 393232 | tf_op jit(solution)/shard_map/reduce_scatter | solution.py:160
  (110 shorter events, 31.0 us)
Async XLA Ops:
  7.2 20.6 %copy-start.8 = (bf16[2,256]{1,0:T(2,128)(2,1)S(1)}, bf16[2,256]{1,0:T(2,128)(2,1)}, u32[]{:S(2)}) copy-start(bf16[2,256]{1,0:T(2,128)(2,1)} %param.19) | copy-start | bytes 3076
  7.2 36.4 %all-gather.8.cloned.1.call-start = ((), (), s32[]{:S(2)}) async-start(), calls=%async_computation.8 | async-start | bytes 1310720 | tf_op jit(solution)/shard_map/all_gather | solution.py:66
  12.8 58.6 %all-gather.10.cloned.1.call-start = ((), (), s32[]{:S(2)}) async-start(), calls=%async_computation.9 | async-start | bytes 1769472 | tf_op jit(solution)/shard_map/all_gather | solution.py:60
  14.6 93.8 %reduce-scatter.9.cloned.1.call-start = ((), (), s32[]{:S(2)}) async-start(), calls=%async_computation.10 | async-start | bytes 1310720 | tf_op jit(solution)/shard_map/reduce_scatter | solution.py:86
  76.7 2.0 copy-start
  79.5 2.2 copy-start.9
  79.5 2.2 copy-start.10
  79.5 2.2 copy-start.11
  79.6 28.8 %copy-start.2 = (bf16[128,1024]{1,0:T(8,128)(2,1)S(1)}, bf16[128,1024]{1,0:T(8,128)(2,1)}, u32[]{:S(2)}) copy-start(bf16[128,1024]{1,0:T(8,128)(2,1)} %param.14) | copy-start | bytes 786436
  81.0 32.8 %copy-start.12 = (bf16[1024]{0:T(1024)(128)(2,1)S(1)}, bf16[1024]{0:T(1024)(128)(2,1)}, u32[]{:S(2)}) copy-start(bf16[1024]{0:T(1024)(128)(2,1)} %param.25) | copy-start | bytes 6148
  81.1 55.8 %all-gather.14.cloned.1.call-start = ((), (), s32[]{:S(2)}) async-start(), calls=%async_computation.12 | async-start | bytes 2359296 | tf_op jit(solution)/shard_map/all_gather | solution.py:62
  81.6 85.2 %all-gather.12.cloned.1.call-start = ((), (), s32[]{:S(2)}) async-start(), calls=%async_computation.11 | async-start | bytes 1310720 | tf_op jit(solution)/shard_map/all_gather | solution.py:93
  112.5 83.3 %all-gather.18.cloned.1.call-start = ((), (), s32[]{:S(2)}) async-start(), calls=%async_computation.15 | async-start | bytes 1310720 | tf_op jit(solution)/shard_map/all_gather | solution.py:106
  113.1 112.5 %all-gather.16.cloned.1.call-start = ((), (), s32[]{:S(2)}) async-start(), calls=%async_computation.13 | async-start | bytes 2359296 | tf_op jit(solution)/shard_map/all_gather | solution.py:63
  113.8 147.6 %reduce-scatter.13.cloned.1.call-start = ((), (), s32[]{:S(2)}) async-start(), calls=%async_computation.16 | async-start | bytes 1310720 | tf_op jit(solution)/shard_map/reduce_scatter | solution.py:120
  225.6 6.1 %copy-start.14 = (bf16[1024,1024]{1,0:T(8,128)(2,1)S(1)}, bf16[1024,1024]{1,0:T(8,128)(2,1)}, u32[]{:S(2)}) copy-start(bf16[1024,1024]{1,0:T(8,128)(2,1)} %all-gather.14.cloned.1.call-done) | copy-start | bytes 6291460
  230.8 1.0 copy-start.7
  234.1 5.1 copy-start.13
  234.1 27.3 %copy-start.3 = (bf16[128,1024]{1,0:T(8,128)(2,1)S(1)}, bf16[128,1024]{1,0:T(8,128)(2,1)}, u32[]{:S(2)}) copy-start(bf16[128,1024]{1,0:T(8,128)(2,1)} %reduce-scatter.9.cloned.1.call-done) | copy-start | bytes 786436
  234.1 55.4 %reduce-scatter.11.cloned.1.call-start = ((), (), s32[]{:S(2)}) async-start(), calls=%async_computation.14 | async-start | bytes 1310720 | tf_op jit(solution)/shard_map/reduce_scatter | solution.py:100
  238.9 50.6 %copy-start.5 = (bf16[128,1024]{1,0:T(8,128)(2,1)S(1)}, bf16[128,1024]{1,0:T(8,128)(2,1)}, u32[]{:S(2)}) copy-start(bf16[128,1024]{1,0:T(8,128)(2,1)} %param.15) | copy-start | bytes 786436
  239.0 80.1 %all-gather.20.cloned.1.call-start = ((), (), s32[]{:S(2)}) async-start(), calls=%async_computation.17 | async-start | bytes 1310720 | tf_op jit(solution)/shard_map/all_gather | solution.py:125
  292.3 70.4 %reduce-scatter.15.cloned.1.call-start = ((), (), s32[]{:S(2)}) async-start(), calls=%async_computation.18 | async-start | bytes 1310720 | tf_op jit(solution)/shard_map/reduce_scatter | solution.py:152
  320.8 3.5 copy-start.1
  328.0 3.6 copy-start.6
  331.6 75.4 %reduce-scatter.19.cloned.1.call-start = ((), (), s32[]{:S(2)}) async-start(), calls=%async_computation.20 | async-start | bytes 1179648 | tf_op jit(solution)/shard_map/reduce_scatter | solution.py:161
  333.1 118.8 %reduce-scatter.23.cloned.1.call-start = ((), (), s32[]{:S(2)}) async-start(), calls=%async_computation.22 | async-start | bytes 4718592 | tf_op jit(solution)/shard_map/reduce_scatter | solution.py:163
  338.5 1.2 copy-start.4
  338.6 168.9 %reduce-scatter.21.cloned.1.call-start = ((), (), s32[]{:S(2)}) async-start(), calls=%async_computation.21 | async-start | bytes 4718592 | tf_op jit(solution)/shard_map/reduce_scatter | solution.py:162
  344.3 1.2 copy-start.15
  344.4 213.1 %reduce-scatter.17.cloned.1.call-start = ((), (), s32[]{:S(2)}) async-start(), calls=%async_computation.19 | async-start | bytes 3538944 | tf_op jit(solution)/shard_map/reduce_scatter | solution.py:160
Sparse Core Ops, SparseCore 0:
  12.9 30.6 all-gather.7
  46.0 25.3 all-gather.9
  81.2 27.1 reduce-scatter.8
  110.3 26.5 all-gather.13
  138.9 27.9 all-gather.11
  168.4 27.4 all-gather.17
  197.9 27.6 all-gather.15
  234.2 27.1 reduce-scatter.12
  263.7 25.7 reduce-scatter.10
  292.4 26.5 all-gather.19
  331.7 26.6 reduce-scatter.14
  361.9 34.6 reduce-scatter.18
  400.6 51.2 reduce-scatter.22
  456.1 51.3 reduce-scatter.20
  511.2 46.2 reduce-scatter.16
where the time goes:
time: 565 us; the launch traced here: 564 us
  waiting for transfers between devices  404 us (72%)
  blocking collectives  65.8 us (12%)
  matrix products  48.9 us (9%)
  other arithmetic  22.9 us (4%)
  between operations  14.2 us (3%)
  local copies, waits for them, and re-layouts  7.28 us (1%)
    reduce_scatter x1, waiting for transfers between devices, body(): lax.psum_scatter(expand_grad, 'dp', scatter_dimension=0, tiled=True)  55.6 us
    reduce_scatter x1, waiting for transfers between devices, body(): lax.psum_scatter(in_grad, 'dp', scatter_dimension=0, tiled=True)  50.1 us
    reduce_scatter x1, waiting for transfers between devices, body(): lax.psum_scatter(shrink_grad, 'dp', scatter_dimension=1, tiled=True)  44.9 us
    psum x1, blocking collectives, body(): lax.psum((gain_one_grad, shift_one_grad, out_bias_part, gain_two_grad, sh...  39.7 us
    all_gather x1, waiting for transfers between devices, body(): lax.all_gather(normed_two.astype(jnp.bfloat16), 'tensor', axis=0, tiled=T...  30 us
    all_gather x1, waiting for transfers between devices, body(): lax.all_gather(shrink_weight, 'dp', axis=1, tiled=True)  29.8 us
    all_gather x1, waiting for transfers between devices, body(): lax.all_gather(project_in, 'dp', axis=0, tiled=True)  27.9 us
    all_gather x1, waiting for transfers between devices, body(): lax.all_gather(middle_grad.astype(jnp.bfloat16), 'tensor', axis=0, tiled=...  26.7 us
  transfers between devices with their start and end apart: 15, of which 13 were waited for; matrix products, arithmetic and copies ran while one was open for 7% of the time, Pallas kernels for 0%

commit v1 on v0

v1 whole, which is shorter than its diff:
```python
import jax
import jax.numpy as jnp
from jax import lax
from jax.sharding import PartitionSpec as P

HEADS = 16
HEAD = 64
AXES = ("dp", "tensor")
LOW = jnp.bfloat16
WIDE = jnp.float32


def together(*values):
    return lax.optimization_barrier(values)


def stats(rows):
    average = jnp.mean(rows, axis=-1, keepdims=True)
    centered = rows - average
    variance = jnp.mean(centered * centered, axis=-1, keepdims=True)
    scale = lax.rsqrt(variance + 1e-05)
    return centered * scale, scale


def norm_back(grad, gain, unit, scale):
    inner = grad * gain
    first = jnp.mean(inner, axis=-1, keepdims=True)
    second = jnp.mean(inner * unit, axis=-1, keepdims=True)
    return scale * (inner - first - unit * second)


def gelu_local(hidden):
    return jax.nn.gelu(hidden, approximate=True)


def make_body(n_dp, n_t):
    bits = [1 << k for k in range(1, n_dp.bit_length() - 1)]

    def send(value, target):
        pairs = []
        for d in range(n_dp):
            for t in range(n_t):
                goal = target(d, t)
                if goal is not None:
                    pairs.append((d * n_t + t, goal[0] * n_t + goal[1]))
        return lax.ppermute(value, AXES, pairs)

    def swap_z(value, mask):
        return send(value, lambda d, t: (d, t ^ mask))

    def swap_dp(value, mask):
        return send(value, lambda d, t: (d ^ mask, t))

    def bit_of(mask):
        return (lax.axis_index("dp") & mask) != 0

    def spread(value, order):
        out = value.reshape((1,) * len(bits) + value.shape)

        def step(out, mask):
            axis = len(bits) - 1 - bits.index(mask)
            other = swap_dp(out, mask)
            flag = bit_of(mask)
            return jnp.concatenate(
                [jnp.where(flag, other, out), jnp.where(flag, out, other)], axis=axis
            )

        return out, step

    def spread_two(first, second):
        forth, back = bits[::-1], bits
        a, step = spread(first, forth)
        b, _ = spread(second, back)
        for mask_a, mask_b in zip(forth, back):
            a, b = step(a, mask_a), step(b, mask_b)
            a, b = together(a, b)
        return (
            a.reshape((-1,) + first.shape[1:]),
            b.reshape((-1,) + second.shape[1:]),
        )

    def fold_two(first, second):
        forth, back = bits, bits[::-1]
        lead = (2,) * len(bits)
        a = first.reshape(lead + first.shape[1:])
        b = second.reshape(lead + second.shape[1:])

        def step(value, mask):
            axis = len(bits) - 1 - bits.index(mask)
            place = (lax.axis_index("dp") // mask) % 2
            keep = lax.dynamic_slice_in_dim(value, place, 1, axis)
            give = lax.dynamic_slice_in_dim(value, 1 - place, 1, axis)
            other = swap_dp(give.astype(LOW), mask)
            return keep.astype(WIDE) + other.astype(WIDE)

        for mask_a, mask_b in zip(forth, back):
            a, b = step(a, mask_a).astype(LOW), step(b, mask_b).astype(LOW)
            a, b = together(a, b)
        return a.reshape(first.shape[1:]), b.reshape(second.shape[1:])

    def gather_z(value):
        return jnp.concatenate([value] + [swap_z(value, k) for k in range(1, n_t)], axis=0)

    def fold_z(parts):
        total = parts[0].astype(WIDE)
        for k in range(1, n_t):
            total = total + swap_z(parts[k].astype(LOW), k).astype(WIDE)
        return total

    def gather_four(value):
        near = swap_z(value, 1)
        across = swap_dp(value, 1)
        both = swap_dp(near, 1)
        return jnp.concatenate([value, near, across, both], axis=0)

    def fold_four(parts):
        other = swap_dp(parts[2:].astype(LOW), 1)
        half = parts[:2].astype(WIDE) + other.astype(WIDE)
        return half[0] + swap_z(half[1].astype(LOW), 1).astype(WIDE)

    def body(
        block_input,
        output_cotangent,
        first_gain,
        first_shift,
        project_in,
        query_value_bias,
        project_out,
        project_out_bias,
        second_gain,
        second_shift,
        expand_weight,
        expand_bias,
        shrink_weight,
        shrink_bias,
    ):
        rows, width = block_input.shape
        local = project_out.shape[0]
        wide = expand_weight.shape[1]
        heads = local // HEAD
        core = lax.axis_index("dp") % 2
        place = lax.axis_index("tensor")
        gain_one, shift_one = first_gain.astype(WIDE), first_shift.astype(WIDE)
        gain_two, shift_two = second_gain.astype(WIDE), second_shift.astype(WIDE)
        bias_qv = query_value_bias.astype(WIDE)

        part_in = project_in.reshape(project_in.shape[0], 3 * local)
        part_a = part_in[:, : 2 * local]
        part_b = jnp.concatenate([part_in[:, 2 * local :], project_out.T], axis=1)
        rows_all = gather_z(block_input)
        full_a, full_b = spread_two(part_a[None], part_b[None])
        pair = jnp.concatenate([full_a, full_b], axis=-1)
        mate = swap_dp(pair, 1)
        full = jnp.stack([jnp.where(core == 0, pair, mate), jnp.where(core == 0, mate, pair)], 1)
        full = full.reshape(width, 4 * local)
        full_in, full_out = full[:, : 3 * local], full[:, 3 * local :]

        near = jnp.concatenate([expand_weight, shrink_weight.T], axis=1)
        one = send(near, lambda d, t: (d ^ 1, t) if d % 2 else (d ^ 1, t ^ 2))
        two = send(near, lambda d, t: (d, t ^ 2) if d % 2 else None)
        both = jnp.stack([jnp.where(core == 0, near, one), jnp.where(core == 0, one, two)])
        bias_far = send(expand_bias, lambda d, t: (d, t ^ 2))
        bias_expand = jnp.where(core == 0, expand_bias, bias_far).astype(WIDE)

        wide_rows = rows_all.astype(WIDE)
        unit_all, scale_all = stats(wide_rows)
        normed_all = (unit_all * gain_one + shift_one).astype(LOW)
        tokens = normed_all.shape[0]
        mixed = jnp.dot(normed_all, full_in, preferred_element_type=WIDE)
        bias_full = jnp.concatenate([bias_qv[0], jnp.zeros_like(bias_qv[0]), bias_qv[1]])
        mixed = (mixed + bias_full).astype(LOW)
        shaped = mixed.reshape(tokens, 3, heads, HEAD)
        queries, keys, values = shaped[:, 0], shaped[:, 1], shaped[:, 2]
        chunk = jnp.arange(tokens) // rows
        position = (chunk ^ place) * rows + jnp.arange(tokens) % rows
        distance = (position[:, None] - position[None, :]).astype(WIDE)
        head_ids = (place * heads + jnp.arange(heads) + 1).astype(WIDE)
        slopes = jnp.exp2(-8.0 * head_ids / HEADS)

        def scores_of(queries, keys):
            product = jnp.einsum("qhd,khd->hqk", queries, keys, preferred_element_type=WIDE)
            scores = product * HEAD ** (-0.5) - slopes[:, None, None] * distance[None]
            return jnp.where(distance[None] >= 0, scores, -1e30)

        scores = scores_of(queries, keys)
        top = jnp.max(scores, axis=-1, keepdims=True)
        log_total = top + jnp.log(jnp.sum(jnp.exp(scores - top), axis=-1, keepdims=True))
        soft_low = jnp.exp(scores - log_total).astype(LOW)
        context = jnp.einsum("hqk,khd->qhd", soft_low, values, preferred_element_type=WIDE)
        context = context.reshape(tokens, local).astype(LOW)
        branch = jnp.einsum("sf,df->sd", context, full_out, preferred_element_type=WIDE)
        branch = branch.reshape(n_t, rows, width)
        top_low = output_cotangent
        tops = gather_four(top_low)
        expand_pair, shrink_pair = both[:, :, :wide], both[:, :, wide:]
        full_expand, full_shrink = spread_two(
            expand_pair.reshape(-1, wide)[None], shrink_pair.reshape(-1, wide)[None]
        )
        full_expand = full_expand.reshape(width, wide)
        full_shrink = full_shrink.reshape(width, wide)
        middle = block_input.astype(WIDE) + fold_z(branch) + project_out_bias.astype(WIDE)

        unit_two, scale_two = stats(middle)
        second_all = gather_four((unit_two * gain_two + shift_two).astype(LOW))
        hidden = jnp.dot(second_all, full_expand, preferred_element_type=WIDE) + bias_expand
        active, gelu_pull = jax.vjp(gelu_local, hidden)
        active = active.astype(LOW)
        active_grad = jnp.dot(tops, full_shrink, preferred_element_type=WIDE)
        (hidden_grad,) = gelu_pull(active_grad)
        hidden_grad = hidden_grad.astype(LOW)
        second_part = jnp.einsum("sf,df->sd", hidden_grad, full_expand, preferred_element_type=WIDE)
        second_grad = fold_four(second_part.reshape(4, rows, width))
        shrunk = jnp.einsum("sf,df->sd", active, full_shrink, preferred_element_type=WIDE)
        shrunk = fold_four(shrunk.reshape(4, rows, width))
        result = middle + shrunk + shrink_bias.astype(WIDE)
        expand_bias_part = jnp.sum(hidden_grad.astype(WIDE), axis=0)
        expand_grad = jnp.einsum("sd,sf->df", second_all, hidden_grad, preferred_element_type=WIDE)
        shrink_grad = jnp.einsum("sd,sf->df", tops, active, preferred_element_type=WIDE)
        blocks = n_dp // 2
        expand_sum, shrink_sum = fold_two(
            expand_grad.astype(LOW).reshape(blocks, -1, wide),
            shrink_grad.astype(LOW).reshape(blocks, -1, wide),
        )
        share = jnp.concatenate([expand_sum, shrink_sum], axis=1).reshape(2, -1, 2 * wide)
        away = send(
            jnp.where(core == 0, share[1], share[0]),
            lambda d, t: (d ^ 1, t ^ 2) if d % 2 else (d ^ 1, t),
        )
        far = send(share[1], lambda d, t: (d, t ^ 2) if d % 2 else None)
        feed_sum = away.astype(WIDE) + jnp.where(core == 0, share[0], far).astype(WIDE)

        upstream = output_cotangent.astype(WIDE)
        middle_grad = upstream + norm_back(second_grad, gain_two, unit_two, scale_two)
        middle_all = gather_z(middle_grad.astype(LOW))

        out_grad = jnp.einsum("sd,sf->df", middle_all, context, preferred_element_type=WIDE)
        context_grad = jnp.dot(middle_all, full_out, preferred_element_type=WIDE)
        context_grad = context_grad.astype(LOW).reshape(tokens, heads, HEAD)
        soft = jnp.exp(scores_of(queries, keys) - log_total)
        value_grad = jnp.einsum(
            "hqk,qhd->khd", soft.astype(LOW), context_grad, preferred_element_type=WIDE
        )
        soft_grad = jnp.einsum("qhd,khd->hqk", context_grad, values, preferred_element_type=WIDE)
        score_grad = soft * (soft_grad - jnp.sum(soft * soft_grad, axis=-1, keepdims=True))
        score_grad = score_grad.astype(LOW)
        query_grad = jnp.einsum("hqk,khd->qhd", score_grad, keys, preferred_element_type=WIDE)
        key_grad = jnp.einsum("hqk,qhd->khd", score_grad, queries, preferred_element_type=WIDE)
        mixed_grad = jnp.stack(
            [query_grad * HEAD ** (-0.5), key_grad * HEAD ** (-0.5), value_grad], axis=1
        )
        mixed_grad = mixed_grad.reshape(tokens, 3 * local).astype(LOW)
        mixed_sums = jnp.sum(mixed_grad.astype(WIDE), axis=0)
        first_part = jnp.einsum("sf,df->sd", mixed_grad, full_in, preferred_element_type=WIDE)
        first_grad = fold_z(first_part.reshape(n_t, rows, width))
        gain_one_part = jnp.sum(first_part * unit_all, axis=0)
        shift_one_part = jnp.sum(first_part, axis=0)
        in_grad = jnp.einsum("sd,sf->df", normed_all, mixed_grad, preferred_element_type=WIDE)

        grads = jnp.concatenate([in_grad, out_grad], axis=1).astype(LOW)
        grads = grads.reshape(blocks, 2, -1, 4 * local)
        mine = lax.dynamic_slice_in_dim(grads, core, 1, 1)
        other = lax.dynamic_slice_in_dim(grads, 1 - core, 1, 1)
        grads = (mine.astype(WIDE) + swap_dp(other, 1).astype(WIDE)).astype(LOW)
        grads = grads.reshape(blocks, -1, 4 * local)
        sum_a, sum_b = fold_two(grads[:, :, : 2 * local], grads[:, :, 2 * local :])
        in_sum = jnp.concatenate([sum_a, sum_b[:, :local]], axis=1).astype(WIDE)
        out_sum = sum_b[:, local:].astype(WIDE).T

        unit = unit_all[:rows]
        scale = scale_all[:rows]
        input_grad = middle_grad + norm_back(first_grad, gain_one, unit, scale)
        slot = jnp.arange(n_t)[:, None]
        bias_slots = jnp.where(slot == (place ^ (2 * core)), expand_bias_part[None], 0.0)
        qv_parts = jnp.stack([mixed_sums[:local], mixed_sums[2 * local :]])
        qv_slots = jnp.where(slot[None] == place, qv_parts[:, None], 0.0)
        vectors = jnp.concatenate(
            [
                jnp.stack(
                    [
                        gain_one_part,
                        shift_one_part,
                        jnp.sum(middle_grad, axis=0),
                        jnp.sum(second_grad * unit_two, axis=0),
                        jnp.sum(second_grad, axis=0),
                        jnp.sum(upstream, axis=0),
                    ]
                ),
                bias_slots.reshape(-1, width),
                qv_slots.reshape(2, -1),
            ],
            axis=0,
        )
        for mask in [1] + bits:
            vectors = vectors + swap_dp(vectors, mask)
        for mask in (1, 2):
            vectors = vectors + swap_z(vectors, mask)
        bias_slots = vectors[6:-2].reshape(n_t, wide)
        expand_bias_sum = lax.dynamic_index_in_dim(bias_slots, place, 0, keepdims=False)
        qv_slots = vectors[-2:].reshape(2, n_t, local)
        qv_sum = lax.dynamic_index_in_dim(qv_slots, place, 1, keepdims=False)
        return (
            result.astype(LOW),
            input_grad.astype(LOW),
            vectors[0],
            vectors[1],
            in_sum.reshape(project_in.shape),
            qv_sum,
            out_sum,
            vectors[2],
            vectors[3],
            vectors[4],
            feed_sum[:, :wide],
            expand_bias_sum,
            feed_sum[:, wide:].T,
            vectors[5],
        )

    return body


def solution(mesh):
    placed = (
        P(("dp", "tensor"), None),
        P(("dp", "tensor"), None),
        P(),
        P(),
        P("dp", None, "tensor"),
        P(None, "tensor"),
        P("tensor", "dp"),
        P(),
        P(),
        P(),
        P("dp", "tensor"),
        P("tensor"),
        P("tensor", "dp"),
        P(),
    )
    return jax.shard_map(
        make_body(mesh.shape["dp"], mesh.shape["tensor"]),
        mesh=mesh,
        in_specs=placed,
        out_specs=(
            P(("dp", "tensor"), None),
            P(("dp", "tensor"), None),
            P(),
            P(),
            P("dp", None, "tensor"),
            P(None, "tensor"),
            P("tensor", "dp"),
            P(),
            P(),
            P(),
            P("dp", "tensor"),
            P("tensor"),
            P("tensor", "dp"),
            P(),
        ),
        check_vma=False,
    )
```

time: 565 us -> 275 us (0.49)
  waiting for transfers between devices: 404 us -> 127 us
  blocking collectives: 65.8 us -> 0 us
  starting transfers between devices: 0.79 us -> 61.9 us
  matrix products: 48.9 us -> 26.8 us
  local copies, waits for them, and re-layouts: 7.28 us -> 22.1 us
  between operations: 14.2 us -> 2.11 us
  other arithmetic: 22.9 us -> 30.9 us
    reduce_scatter x8 -> x0, waiting for transfers between devices: 225 us -> none  [the longest x1 55.6 us: body(): lax.psum_scatter(expand_grad, 'dp', scatter_dimension=0, tiled=True)]
    all_gather x7 -> x0, waiting for transfers between devices: 177 us -> none  [the longest x1 30 us: body(): lax.all_gather(normed_two.astype(jnp.bfloat16), 'tensor', axis=0, tiled=T...]
    ppermute x0 -> x50, waiting for transfers between devices: none -> 127 us  [send(): return lax.ppermute(value, AXES, pairs)]
    ppermute x0 -> x50, starting transfers between devices: none -> 61.9 us  [send(): return lax.ppermute(value, AXES, pairs)]
    psum x2 -> x0, blocking collectives: 54 us -> none  [the longest x1 39.7 us: body(): lax.psum((gain_one_grad, shift_one_grad, out_bias_part, gain_two_grad, sh...]
    dot_general x18, matrix products: 48.9 us -> 26.8 us  [the longest x1 4.05 us: body(): jnp.einsum('sf,df->sd', mixed_grad, full_in, preferred_element_type=WIDE)]
    all_gather x1 -> x0, blocking collectives: 11.7 us -> none  [body(): lax.all_gather(project_out, 'dp', axis=1, tiled=True)]
    reduce_sum x11 -> x10, other arithmetic: 12.4 us -> 10.4 us  [the longest x1 4.65 us: body(): shift_one_part = jnp.sum(first_part, axis=0)]
  transfers between devices with their start and end apart: 15 -> 50, of which waited for: 13 -> 23; matrix products, arithmetic and copies ran while one was open for 7% -> 25% of each run, Pallas kernels for 0% -> 0%
where the time goes in v1:
time: 275 us; the launch traced here: 270 us
  waiting for transfers between devices  127 us (46%)
  starting transfers between devices  61.9 us (23%)
  other arithmetic  30.9 us (11%)
  matrix products  26.8 us (10%)
  local copies, waits for them, and re-layouts  22.1 us (8%)
    ppermute x50, waiting for transfers between devices, send(): return lax.ppermute(value, AXES, pairs)  127 us
    ppermute x50, starting transfers between devices, send(): return lax.ppermute(value, AXES, pairs)  61.9 us
    unnamed x107, local copies, waits for them, and re-layouts  9.92 us
  transfers between devices with their start and end apart: 50, of which 23 were waited for; matrix products, arithmetic and copies ran while one was open for 25% of the time, Pallas kernels for 0%

profile of v1, /device:TPU:0, one launch (start us, length us, event | category | flops | bytes accessed | tf_op | source)
XLA Modules:
  0.0 270.4 jit_solution(17240143332668523309)
XLA Ops:
  0.8 4.1 %collective-permute-start.1 = (bf16[128,1024]{1,0:T(8,128)(2,1)}, bf16[128,1024]{1,0:T(8,128)(2,1)S(1)}, u32[]{:S(2)}, u32[]{:S(2)}) collective-permute-start(bf16[128,1024]{1,0:T(8,128)(2,1)} %param.14), channel_id=1, source_target_pairs={{0,2},{1,3},{2,0},{3,1},{4,6},{5,7},{6,4},{7,5},{8,10},{9,11},{10,... | collective-permute-start | bytes 786440 | tf_op jit(solution)/shard_map/ppermute | solution.py:46
  16.8 3.4 %collective-permute-done.4 = bf16[1,1,1,128,512]{3,4,2,1,0:T(8,128)(2,1)S(1)} collective-permute-done((bf16[1,1,1,128,512]{3,4,2,1,0:T(8,128)(2,1)S(1)}, bf16[1,1,1,128,512]{3,4,2,1,0:T(8,128)(2,1)S(1)}, u32[]{:S(2)}, u32[]{:S(2)}) %collective-permute-start.4) | collective-permute-done | bytes 131104 | tf_op jit(solution)/shard_map/ppermute | solution.py:46
  20.2 3.5 %collective-permute-start.20 = (bf16[1024]{0:T(1024)(128)(2,1)S(1)}, bf16[1024]{0:T(1024)(128)(2,1)S(1)}, u32[]{:S(2)}, u32[]{:S(2)}) collective-permute-start(bf16[1024]{0:T(1024)(128)(2,1)S(1)} %copy-done.46), channel_id=1, source_target_pairs={{0,2},{1,3},{2,0},{3,1},{4,6},{5,7},{6,4},{7,5},{8,10},{9,11},{10,... | collective-permute-start | bytes 6152 | tf_op jit(solution)/shard_map/ppermute | solution.py:46
  23.8 4.7 %collective-permute-done.20 = bf16[1024]{0:T(1024)(128)(2,1)S(1)} collective-permute-done((bf16[1024]{0:T(1024)(128)(2,1)S(1)}, bf16[1024]{0:T(1024)(128)(2,1)S(1)}, u32[]{:S(2)}, u32[]{:S(2)}) %collective-permute-start.20) | collective-permute-done | bytes 2080 | tf_op jit(solution)/shard_map/ppermute | solution.py:46
  33.3 2.2 collective-permute-done.5
  39.1 2.2 collective-permute-start.7
  41.4 5.3 %collective-permute-done.14 = bf16[128,2048]{1,0:T(8,128)(2,1)} collective-permute-done((bf16[128,2048]{1,0:T(8,128)(2,1)}, bf16[128,2048]{1,0:T(8,128)(2,1)}, u32[]{:S(2)}, u32[]{:S(2)}) %collective-permute-start.14) | collective-permute-done | bytes 524320 | tf_op jit(solution)/shard_map/ppermute | solution.py:46
  49.7 11.8 %collective-permute-start.25 = (bf16[128,1024]{1,0:T(8,128)(2,1)}, bf16[128,1024]{1,0:T(8,128)(2,1)}, u32[]{:S(2)}, u32[]{:S(2)}) collective-permute-start(bf16[128,1024]{1,0:T(8,128)(2,1)} %collective-permute-done.23), channel_id=1, source_target_pairs={{0,4},{1,5},{2,6},{3,7},{4,0},{5,1},{6,2},{7,3},{8,12},{9,13},{10,... | collective-permute-start | bytes 786440 | tf_op jit(solution)/shard_map/ppermute | solution.py:46
  63.5 11.9 %collective-permute-done.17 = bf16[1,1,1,256,1024]{4,3,2,1,0:T(8,128)(2,1)S(1)} collective-permute-done((bf16[1,1,1,256,1024]{4,3,2,1,0:T(8,128)(2,1)S(1)}, bf16[1,1,1,256,1024]{4,3,2,1,0:T(8,128)(2,1)S(1)}, u32[]{:S(2)}, u32[]{:S(2)}) %collective-permute-start.17) | collective-permute-done | bytes 524320 | tf_op jit(solution)/shard_map/ppermute | solution.py:46
  78.1 2.1 add_convert_fusion.4
  81.6 2.5 fusion.75
  87.6 2.1 collective-permute-start.10
  90.4 3.9 %collective-permute-done.8 = bf16[128,1024]{1,0:T(8,128)(2,1)S(1)} collective-permute-done((bf16[128,1024]{1,0:T(8,128)(2,1)S(1)}, bf16[128,1024]{1,0:T(8,128)(2,1)S(1)}, u32[]{:S(2)}, u32[]{:S(2)}) %collective-permute-start.8) | collective-permute-done | bytes 262176 | tf_op jit(solution)/shard_map/ppermute | solution.py:46
  94.8 7.7 %collective-permute-done.10 = bf16[128,1024]{1,0:T(8,128)(2,1)S(1)} collective-permute-done((bf16[128,1024]{1,0:T(8,128)(2,1)S(1)}, bf16[128,1024]{1,0:T(8,128)(2,1)S(1)}, u32[]{:S(2)}, u32[]{:S(2)}) %collective-permute-start.10) | collective-permute-done | bytes 262176 | tf_op jit(solution)/shard_map/ppermute | solution.py:46
  103.1 9.4 %collective-permute-done.9 = bf16[128,1024]{1,0:T(8,128)(2,1)S(1)} collective-permute-done((bf16[128,1024]{1,0:T(8,128)(2,1)S(1)}, bf16[128,1024]{1,0:T(8,128)(2,1)S(1)}, u32[]{:S(2)}, u32[]{:S(2)}) %collective-permute-start.9) | collective-permute-done | bytes 262176 | tf_op jit(solution)/shard_map/ppermute | solution.py:46
  116.3 3.5 %collective-permute-done.11 = bf16[128,1024]{1,0:T(8,128)(2,1)S(1)} collective-permute-done((bf16[128,1024]{1,0:T(8,128)(2,1)S(1)}, bf16[128,1024]{1,0:T(8,128)(2,1)S(1)}, u32[]{:S(2)}, u32[]{:S(2)}) %collective-permute-start.11) | collective-permute-done | bytes 262176 | tf_op jit(solution)/shard_map/ppermute | solution.py:46
  120.0 4.6 %collective-permute-done.19 = bf16[1,2,1,256,1024]{4,3,2,1,0:T(8,128)(2,1)S(1)} collective-permute-done((bf16[1,2,1,256,1024]{4,3,2,1,0:T(8,128)(2,1)S(1)}, bf16[1,2,1,256,1024]{4,3,2,1,0:T(8,128)(2,1)S(1)}, u32[]{:S(2)}, u32[]{:S(2)}) %collective-permute-start.19) | collective-permute-done | bytes 1048608 | tf_op jit(solution)/shard_map/ppermute | solution.py:46
  128.2 2.7 convert_reduce_fusion.1
  139.1 6.9 %collective-permute-done.27 = bf16[128,1024]{1,0:T(8,128)(2,1)S(1)} collective-permute-done((bf16[128,1024]{1,0:T(8,128)(2,1)S(1)}, bf16[128,1024]{1,0:T(8,128)(2,1)S(1)}, u32[]{:S(2)}, u32[]{:S(2)}) %collective-permute-start.27) | collective-permute-done | bytes 262176 | tf_op jit(solution)/shard_map/ppermute | solution.py:46
  146.3 4.0 %collective-permute-done.22 = bf16[128,1024]{1,0:T(8,128)(2,1)S(1)} collective-permute-done((bf16[128,1024]{1,0:T(8,128)(2,1)S(1)}, bf16[128,1024]{1,0:T(8,128)(2,1)S(1)}, u32[]{:S(2)}, u32[]{:S(2)}) %collective-permute-start.22) | collective-permute-done | bytes 262176 | tf_op jit(solution)/shard_map/ppermute | solution.py:46
  150.3 2.0 fusion.65
  154.3 2.5 collective-permute-start.28
  157.6 6.0 %collective-permute-done.30 = bf16[128,1024]{1,0:T(8,128)(2,1)S(1)} collective-permute-done((bf16[128,1024]{1,0:T(8,128)(2,1)S(1)}, bf16[128,1024]{1,0:T(8,128)(2,1)S(1)}, u32[]{:S(2)}, u32[]{:S(2)}) %collective-permute-start.30) | collective-permute-done | bytes 262176 | tf_op jit(solution)/shard_map/ppermute | solution.py:46
  163.6 12.8 %collective-permute-done.29 = bf16[128,1024]{1,0:T(8,128)(2,1)S(1)} collective-permute-done((bf16[128,1024]{1,0:T(8,128)(2,1)S(1)}, bf16[128,1024]{1,0:T(8,128)(2,1)S(1)}, u32[]{:S(2)}, u32[]{:S(2)}) %collective-permute-start.29) | collective-permute-done | bytes 262176 | tf_op jit(solution)/shard_map/ppermute | solution.py:46
  187.3 4.1 %fusion.11 = f32[512,1024]{1,0:T(8,128)} fusion(bf16[512,768]{0,1:T(8,128)(2,1)S(1)} %bitcast.210, bf16[1024,1024]{1,0:T(8,128)(2,1)} %bitcast.185), kind=kOutput, calls=%fused_computation.40 | convolution fusion | flops 805306368 | bytes 4456448 | tf_op jit(solution)/shard_map/sf,df->sd/dot_general | solution.py:253
  191.5 4.6 %fusion.61 = (f32[1024]{0:T(1024)S(1)}, f32[1024]{0:T(1024)S(1)}, bf16[512,1024]{1,0:T(8,128)(2,1)S(1)}, bf16[1024,512]{0,1:T(8,128)(2,1)S(1)}, f32[512,1024]{1,0:T(8,128)}) fusion(f32[512,1024]{1,0:T(8,128)} %fusion.11, f32[512]{0:T(512)S(1)} %add_rsqrt_fusion, f32[512]{0:T(512)S(1)} %broadcast_multiply_fusion, bf16[128,1024]{1,0:T(8,128)(2,1)} %copy-done.15, ...), kind=kLoop, calls=%fused_computation.206 | loop fusion | flops 8910848 | bytes 7360512 | tf_op jit(solution)/shard_map/reduce_sum | solution.py:256
  201.3 2.2 convolution_convert_fusion.2
  210.1 3.3 %collective-permute-done.37 = f32[12,1024]{1,0:T(8,128)S(1)} collective-permute-done((f32[12,1024]{1,0:T(8,128)S(1)}, f32[12,1024]{1,0:T(8,128)S(1)}, u32[]{:S(2)}, u32[]{:S(2)}) %collective-permute-start.37) | collective-permute-done | bytes 49184 | tf_op jit(solution)/shard_map/ppermute | solution.py:46
  214.7 4.6 %collective-permute-done.38 = f32[12,1024]{1,0:T(8,128)S(1)} collective-permute-done((f32[12,1024]{1,0:T(8,128)S(1)}, f32[12,1024]{1,0:T(8,128)S(1)}, u32[]{:S(2)}, u32[]{:S(2)}) %collective-permute-start.38) | collective-permute-done | bytes 49184 | tf_op jit(solution)/shard_map/ppermute | solution.py:46
  221.7 10.0 %collective-permute-done.32 = bf16[128,1024]{1,0:T(8,128)(2,1)S(1)} collective-permute-done((bf16[128,1024]{1,0:T(8,128)(2,1)S(1)}, bf16[128,1024]{1,0:T(8,128)(2,1)S(1)}, u32[]{:S(2)}, u32[]{:S(2)}) %collective-permute-start.32) | collective-permute-done | bytes 262176 | tf_op jit(solution)/shard_map/ppermute | solution.py:46
  243.3 14.2 %collective-permute-done.48 = bf16[128,2048]{1,0:T(8,128)(2,1)} collective-permute-done((bf16[128,2048]{1,0:T(8,128)(2,1)}, bf16[128,2048]{1,0:T(8,128)(2,1)}, u32[]{:S(2)}, u32[]{:S(2)}) %collective-permute-start.48) | collective-permute-done | bytes 524320 | tf_op jit(solution)/shard_map/ppermute | solution.py:46
  265.3 3.4 %collective-permute-done.42 = bf16[1,1,128,512]{2,3,1,0:T(8,128)(2,1)S(1)} collective-permute-done((bf16[1,1,128,512]{2,3,1,0:T(8,128)(2,1)S(1)}, bf16[1,1,128,512]{2,3,1,0:T(8,128)(2,1)S(1)}, u32[]{:S(2)}, u32[]{:S(2)}) %collective-permute-start.42) | collective-permute-done | bytes 131104 | tf_op jit(solution)/shard_map/ppermute | solution.py:46
  (319 shorter events, 100.0 us)
Async XLA Ops:
  0.8 29.2 %collective-permute-start.1 = (bf16[128,1024]{1,0:T(8,128)(2,1)}, bf16[128,1024]{1,0:T(8,128)(2,1)S(1)}, u32[]{:S(2)}, u32[]{:S(2)}) collective-permute-start(bf16[128,1024]{1,0:T(8,128)(2,1)} %param.14), channel_id=1, source_target_pairs={{0,2},{1,3},{2,0},{3,1},{4,6},{5,7},{6,4},{7,5},{8,10},{9,11},{10,... | collective-permute-start | bytes 786440 | tf_op jit(solution)/shard_map/ppermute | solution.py:46
  4.9 25.2 %collective-permute-start = (bf16[128,1024]{1,0:T(8,128)(2,1)}, bf16[128,1024]{1,0:T(8,128)(2,1)S(1)}, u32[]{:S(2)}, u32[]{:S(2)}) collective-permute-start(bf16[128,1024]{1,0:T(8,128)(2,1)} %param.14), channel_id=1, source_target_pairs={{0,1},{1,0},{2,3},{3,2},{4,5},{5,4},{6,7},{7,6},{8,9},{9,8},{10,11... | collective-permute-start | bytes 786440 | tf_op jit(solution)/shard_map/ppermute | solution.py:46
  6.4 25.1 %collective-permute-start.2 = (bf16[128,1024]{1,0:T(8,128)(2,1)}, bf16[128,1024]{1,0:T(8,128)(2,1)S(1)}, u32[]{:S(2)}, u32[]{:S(2)}) collective-permute-start(bf16[128,1024]{1,0:T(8,128)(2,1)} %param.14), channel_id=1, source_target_pairs={{0,3},{1,2},{2,1},{3,0},{4,7},{5,6},{6,5},{7,4},{8,11},{9,10},{10,... | collective-permute-start | bytes 786440 | tf_op jit(solution)/shard_map/ppermute | solution.py:46
  9.3 40.4 %collective-permute-start.23 = (bf16[128,1024]{1,0:T(8,128)(2,1)}, bf16[128,1024]{1,0:T(8,128)(2,1)}, u32[]{:S(2)}, u32[]{:S(2)}) collective-permute-start(bf16[128,1024]{1,0:T(8,128)(2,1)} %param.15), channel_id=1, source_target_pairs={{0,1},{1,0},{2,3},{3,2},{4,5},{5,4},{6,7},{7,6},{8,9},{9,8},{10,11... | collective-permute-start | bytes 786440 | tf_op jit(solution)/shard_map/ppermute | solution.py:46
  30.0 84.2 %collective-permute-start.24 = (bf16[128,1024]{1,0:T(8,128)(2,1)}, bf16[128,1024]{1,0:T(8,128)(2,1)}, u32[]{:S(2)}, u32[]{:S(2)}) collective-permute-start(bf16[128,1024]{1,0:T(8,128)(2,1)} %param.15), channel_id=1, source_target_pairs={{0,4},{1,5},{2,6},{3,7},{4,0},{5,1},{6,2},{7,3},{8,12},{9,13},{10,... | collective-permute-start | bytes 786440 | tf_op jit(solution)/shard_map/ppermute | solution.py:46
  30.1 11.3 %collective-permute-start.15 = (bf16[128,2048]{1,0:T(8,128)(2,1)}, bf16[128,2048]{1,0:T(8,128)(2,1)}, u32[]{:S(2)}, u32[]{:S(2)}) collective-permute-start(bf16[128,2048]{1,0:T(8,128)(2,1)} %pad_maximum_fusion.13), channel_id=1, source_target_pairs={{4,6},{5,7},{6,4},{7,5},{12,14},{13,15},{14,12},{15,13},{20,22},{2... | collective-permute-start | bytes 1572872 | tf_op jit(solution)/shard_map/ppermute | solution.py:46
  35.5 11.2 %collective-permute-start.14 = (bf16[128,2048]{1,0:T(8,128)(2,1)}, bf16[128,2048]{1,0:T(8,128)(2,1)}, u32[]{:S(2)}, u32[]{:S(2)}) collective-permute-start(bf16[128,2048]{1,0:T(8,128)(2,1)} %pad_maximum_fusion.13), channel_id=1, source_target_pairs={{0,6},{1,7},{2,4},{3,5},{4,0},{5,1},{6,2},{7,3},{8,14},{9,15},{10,... | collective-permute-start | bytes 1572872 | tf_op jit(solution)/shard_map/ppermute | solution.py:46
  39.1 37.3 %collective-permute-start.7 = (bf16[4,128,1024]{2,1,0:T(8,128)(2,1)S(1)}, bf16[4,128,1024]{2,1,0:T(8,128)(2,1)S(1)}, u32[]{:S(2)}, u32[]{:S(2)}) collective-permute-start(bf16[4,128,1024]{2,1,0:T(8,128)(2,1)S(1)} %pad_maximum_fusion.4), channel_id=1, source_target_pairs={{0,4},{1,5},{2,6},{3,7},{4,0},{5,1},{6,2},{7,3},{8,12},{9,13},{10,... | collective-permute-start | bytes 3145736 | tf_op jit(solution)/shard_map/ppermute | solution.py:46
  48.1 14.3 %collective-permute-start.16 = (bf16[1,1,1,256,1024]{4,3,2,1,0:T(8,128)(2,1)S(1)}, bf16[1,1,1,256,1024]{4,3,2,1,0:T(8,128)(2,1)S(1)}, u32[]{:S(2)}, u32[]{:S(2)}) collective-permute-start(bf16[1,1,1,256,1024]{4,3,2,1,0:T(8,128)(2,1)S(1)} %bitcast.196), channel_id=1, source_target_pairs={{0,16},{1,17},{2,18},{3,19},{4,20},{5,21},{6,22},{7,23},{8,24},{9,... | collective-permute-start | bytes 1572872 | tf_op jit(solution)/shard_map/ppermute | solution.py:46
  49.7 65.5 %collective-permute-start.25 = (bf16[128,1024]{1,0:T(8,128)(2,1)}, bf16[128,1024]{1,0:T(8,128)(2,1)}, u32[]{:S(2)}, u32[]{:S(2)}) collective-permute-start(bf16[128,1024]{1,0:T(8,128)(2,1)} %collective-permute-done.23), channel_id=1, source_target_pairs={{0,4},{1,5},{2,6},{3,7},{4,0},{5,1},{6,2},{7,3},{8,12},{9,13},{10,... | collective-permute-start | bytes 786440 | tf_op jit(solution)/shard_map/ppermute | solution.py:46
  61.5 13.9 %collective-permute-start.17 = (bf16[1,1,1,256,1024]{4,3,2,1,0:T(8,128)(2,1)S(1)}, bf16[1,1,1,256,1024]{4,3,2,1,0:T(8,128)(2,1)S(1)}, u32[]{:S(2)}, u32[]{:S(2)}) collective-permute-start(bf16[1,1,1,256,1024]{4,3,2,1,0:T(8,128)(2,1)S(1)} %bitcast.194), channel_id=1, source_target_pairs={{0,8},{1,9},{2,10},{3,11},{4,12},{5,13},{6,14},{7,15},{8,0},{9,1},... | collective-permute-start | bytes 1572872 | tf_op jit(solution)/shard_map/ppermute | solution.py:46
  87.6 15.0 %collective-permute-start.10 = (bf16[128,1024]{1,0:T(8,128)(2,1)S(1)}, bf16[128,1024]{1,0:T(8,128)(2,1)S(1)}, u32[]{:S(2)}, u32[]{:S(2)}) collective-permute-start(bf16[128,1024]{1,0:T(8,128)(2,1)S(1)} %get-tuple-element.116), channel_id=1, source_target_pairs={{0,3},{1,2},{2,1},{3,0},{4,7},{5,6},{6,5},{7,4},{8,11},{9,10},{10,... | collective-permute-start | bytes 786440 | tf_op jit(solution)/shard_map/ppermute | solution.py:46
  89.7 22.8 %collective-permute-start.9 = (bf16[128,1024]{1,0:T(8,128)(2,1)S(1)}, bf16[128,1024]{1,0:T(8,128)(2,1)S(1)}, u32[]{:S(2)}, u32[]{:S(2)}) collective-permute-start(bf16[128,1024]{1,0:T(8,128)(2,1)S(1)} %get-tuple-element.117), channel_id=1, source_target_pairs={{0,2},{1,3},{2,0},{3,1},{4,6},{5,7},{6,4},{7,5},{8,10},{9,11},{10,... | collective-permute-start | bytes 786440 | tf_op jit(solution)/shard_map/ppermute | solution.py:46
  94.3 25.4 %collective-permute-start.18 = (bf16[2,1,1,256,1024]{4,3,2,1,0:T(8,128)(2,1)S(1)}, bf16[2,1,1,256,1024]{4,3,2,1,0:T(8,128)(2,1)S(1)}, u32[]{:S(2)}, u32[]{:S(2)}) collective-permute-start(bf16[2,1,1,256,1024]{4,3,2,1,0:T(8,128)(2,1)S(1)} %pad_maximum_fusion.6), channel_id=1, source_target_pairs={{0,8},{1,9},{2,10},{3,11},{4,12},{5,13},{6,14},{7,15},{8,0},{9,1},... | collective-permute-start | bytes 3145736 | tf_op jit(solution)/shard_map/ppermute | solution.py:46
  102.6 22.1 %collective-permute-start.19 = (bf16[1,2,1,256,1024]{4,3,2,1,0:T(8,128)(2,1)S(1)}, bf16[1,2,1,256,1024]{4,3,2,1,0:T(8,128)(2,1)S(1)}, u32[]{:S(2)}, u32[]{:S(2)}) collective-permute-start(bf16[1,2,1,256,1024]{4,3,2,1,0:T(8,128)(2,1)S(1)} %pad_maximum_fusion.7), channel_id=1, source_target_pairs={{0,16},{1,17},{2,18},{3,19},{4,20},{5,21},{6,22},{7,23},{8,24},{9,... | collective-permute-start | bytes 3145736 | tf_op jit(solution)/shard_map/ppermute | solution.py:46
  134.5 47.0 %collective-permute-start.45 = (bf16[1,2,256,1024]{3,2,1,0:T(8,128)(2,1)S(1)}, bf16[1,2,256,1024]{3,2,1,0:T(8,128)(2,1)S(1)}, u32[]{:S(2)}, u32[]{:S(2)}) collective-permute-start(bf16[1,2,256,1024]{3,2,1,0:T(8,128)(2,1)S(1)} %constant_dynamic-slice_fusion.3), channel_id=1, source_target_pairs={{0,16},{1,17},{2,18},{3,19},{4,20},{5,21},{6,22},{7,23},{8,24},{9,... | collective-permute-start | bytes 3145736 | tf_op jit(solution)/shard_map/ppermute | solution.py:46
  136.7 9.3 %collective-permute-start.27 = (bf16[128,1024]{1,0:T(8,128)(2,1)S(1)}, bf16[128,1024]{1,0:T(8,128)(2,1)S(1)}, u32[]{:S(2)}, u32[]{:S(2)}) collective-permute-start(bf16[128,1024]{1,0:T(8,128)(2,1)S(1)} %fusion.40), channel_id=1, source_target_pairs={{0,1},{1,0},{2,3},{3,2},{4,5},{5,4},{6,7},{7,6},{8,9},{9,8},{10,11... | collective-permute-start | bytes 786440 | tf_op jit(solution)/shard_map/ppermute | solution.py:46
  137.9 12.4 %collective-permute-start.22 = (bf16[128,1024]{1,0:T(8,128)(2,1)S(1)}, bf16[128,1024]{1,0:T(8,128)(2,1)S(1)}, u32[]{:S(2)}, u32[]{:S(2)}) collective-permute-start(bf16[128,1024]{1,0:T(8,128)(2,1)S(1)} %fusion.39), channel_id=1, source_target_pairs={{0,1},{1,0},{2,3},{3,2},{4,5},{5,4},{6,7},{7,6},{8,9},{9,8},{10,11... | collective-permute-start | bytes 786440 | tf_op jit(solution)/shard_map/ppermute | solution.py:46
  152.4 11.2 %collective-permute-start.30 = (bf16[128,1024]{1,0:T(8,128)(2,1)S(1)}, bf16[128,1024]{1,0:T(8,128)(2,1)S(1)}, u32[]{:S(2)}, u32[]{:S(2)}) collective-permute-start(bf16[128,1024]{1,0:T(8,128)(2,1)S(1)} %convert_element_type.303), channel_id=1, source_target_pairs={{0,3},{1,2},{2,1},{3,0},{4,7},{5,6},{6,5},{7,4},{8,11},{9,10},{10,... | collective-permute-start | bytes 786440 | tf_op jit(solution)/shard_map/ppermute | solution.py:46
  154.3 22.1 %collective-permute-start.29 = (bf16[128,1024]{1,0:T(8,128)(2,1)S(1)}, bf16[128,1024]{1,0:T(8,128)(2,1)S(1)}, u32[]{:S(2)}, u32[]{:S(2)}) collective-permute-start(bf16[128,1024]{1,0:T(8,128)(2,1)S(1)} %convert_element_type.303), channel_id=1, source_target_pairs={{0,2},{1,3},{2,0},{3,1},{4,6},{5,7},{6,4},{7,5},{8,10},{9,11},{10,... | collective-permute-start | bytes 786440 | tf_op jit(solution)/shard_map/ppermute | solution.py:46
  154.3 22.1 %collective-permute-start.28 = (bf16[128,1024]{1,0:T(8,128)(2,1)S(1)}, bf16[128,1024]{1,0:T(8,128)(2,1)S(1)}, u32[]{:S(2)}, u32[]{:S(2)}) collective-permute-start(bf16[128,1024]{1,0:T(8,128)(2,1)S(1)} %convert_element_type.303), channel_id=1, source_target_pairs={{0,1},{1,0},{2,3},{3,2},{4,5},{5,4},{6,7},{7,6},{8,9},{9,8},{10,11... | collective-permute-start | bytes 786440 | tf_op jit(solution)/shard_map/ppermute | solution.py:46
  156.9 25.9 %collective-permute-start.44 = (bf16[2,1,256,1024]{3,2,1,0:T(8,128)(2,1)S(1)}, bf16[2,1,256,1024]{3,2,1,0:T(8,128)(2,1)S(1)}, u32[]{:S(2)}, u32[]{:S(2)}) collective-permute-start(bf16[2,1,256,1024]{3,2,1,0:T(8,128)(2,1)S(1)} %constant_dynamic-slice_fusion.4), channel_id=1, source_target_pairs={{0,8},{1,9},{2,10},{3,11},{4,12},{5,13},{6,14},{7,15},{8,0},{9,1},... | collective-permute-start | bytes 3145736 | tf_op jit(solution)/shard_map/ppermute | solution.py:46
  184.9 49.2 %collective-permute-start.47 = (bf16[1,1,256,1024]{3,2,1,0:T(8,128)(2,1)}, bf16[1,1,256,1024]{3,2,1,0:T(8,128)(2,1)}, u32[]{:S(2)}, u32[]{:S(2)}) collective-permute-start(bf16[1,1,256,1024]{3,2,1,0:T(8,128)(2,1)} %constant_dynamic-slice_fusion.1), channel_id=1, source_target_pairs={{0,8},{1,9},{2,10},{3,11},{4,12},{5,13},{6,14},{7,15},{8,0},{9,1},... | collective-permute-start | bytes 1572872 | tf_op jit(solution)/shard_map/ppermute | solution.py:46
  185.5 49.9 %collective-permute-start.46 = (bf16[1,1,256,1024]{3,2,1,0:T(8,128)(2,1)}, bf16[1,1,256,1024]{3,2,1,0:T(8,128)(2,1)}, u32[]{:S(2)}, u32[]{:S(2)}) collective-permute-start(bf16[1,1,256,1024]{3,2,1,0:T(8,128)(2,1)} %constant_dynamic-slice_fusion.2), channel_id=1, source_target_pairs={{0,16},{1,17},{2,18},{3,19},{4,20},{5,21},{6,22},{7,23},{8,24},{9,... | collective-permute-start | bytes 1572872 | tf_op jit(solution)/shard_map/ppermute | solution.py:46
  197.3 24.2 %collective-permute-start.31 = (bf16[128,1024]{1,0:T(8,128)(2,1)}, bf16[128,1024]{1,0:T(8,128)(2,1)}, u32[]{:S(2)}, u32[]{:S(2)}) collective-permute-start(bf16[128,1024]{1,0:T(8,128)(2,1)} %get-tuple-element.106), channel_id=1, source_target_pairs={{0,1},{1,0},{2,3},{3,2},{4,5},{5,4},{6,7},{7,6},{8,9},{9,8},{10,11... | collective-permute-start | bytes 786440 | tf_op jit(solution)/shard_map/ppermute | solution.py:46
  197.3 24.3 %collective-permute-start.33 = (bf16[128,1024]{1,0:T(8,128)(2,1)}, bf16[128,1024]{1,0:T(8,128)(2,1)}, u32[]{:S(2)}, u32[]{:S(2)}) collective-permute-start(bf16[128,1024]{1,0:T(8,128)(2,1)} %get-tuple-element.107), channel_id=1, source_target_pairs={{0,3},{1,2},{2,1},{3,0},{4,7},{5,6},{6,5},{7,4},{8,11},{9,10},{10,... | collective-permute-start | bytes 786440 | tf_op jit(solution)/shard_map/ppermute | solution.py:46
  219.2 12.4 %collective-permute-start.32 = (bf16[128,1024]{1,0:T(8,128)(2,1)S(1)}, bf16[128,1024]{1,0:T(8,128)(2,1)S(1)}, u32[]{:S(2)}, u32[]{:S(2)}) collective-permute-start(bf16[128,1024]{1,0:T(8,128)(2,1)S(1)} %copy-done.30), channel_id=1, source_target_pairs={{0,2},{1,3},{2,0},{3,1},{4,6},{5,7},{6,4},{7,5},{8,10},{9,11},{10,... | collective-permute-start | bytes 786440 | tf_op jit(solution)/shard_map/ppermute | solution.py:46
  221.6 17.5 %collective-permute-start.39 = (bf16[4,1,128,1024]{3,2,1,0:T(8,128)(2,1)S(1)}, bf16[4,1,128,1024]{3,2,1,0:T(8,128)(2,1)S(1)}, u32[]{:S(2)}, u32[]{:S(2)}) collective-permute-start(bf16[4,1,128,1024]{3,2,1,0:T(8,128)(2,1)S(1)} %fusion.17), channel_id=1, source_target_pairs={{0,4},{1,5},{2,6},{3,7},{4,0},{5,1},{6,2},{7,3},{8,12},{9,13},{10,... | collective-permute-start | bytes 3145736 | tf_op jit(solution)/shard_map/ppermute | solution.py:46
  237.6 19.9 %collective-permute-start.48 = (bf16[128,2048]{1,0:T(8,128)(2,1)}, bf16[128,2048]{1,0:T(8,128)(2,1)}, u32[]{:S(2)}, u32[]{:S(2)}) collective-permute-start(bf16[128,2048]{1,0:T(8,128)(2,1)} %get-tuple-element.82), channel_id=1, source_target_pairs={{0,4},{1,5},{2,6},{3,7},{4,2},{5,3},{6,0},{7,1},{8,12},{9,13},{10,... | collective-permute-start | bytes 1572872 | tf_op jit(solution)/shard_map/ppermute | solution.py:46
  237.6 19.9 %collective-permute-start.49 = (bf16[128,2048]{1,0:T(8,128)(2,1)S(1)}, bf16[128,2048]{1,0:T(8,128)(2,1)}, u32[]{:S(2)}, u32[]{:S(2)}) collective-permute-start(bf16[128,2048]{1,0:T(8,128)(2,1)S(1)} %get-tuple-element.83), channel_id=1, source_target_pairs={{4,6},{5,7},{6,4},{7,5},{12,14},{13,15},{14,12},{15,13},{20,22},{2... | collective-permute-start | bytes 1572872 | tf_op jit(solution)/shard_map/ppermute | solution.py:46
  241.3 17.8 %collective-permute-start.40 = (bf16[2,1,128,512]{2,3,1,0:T(8,128)(2,1)}, bf16[2,1,128,512]{2,3,1,0:T(8,128)(2,1)}, u32[]{:S(2)}, u32[]{:S(2)}) collective-permute-start(bf16[2,1,128,512]{2,3,1,0:T(8,128)(2,1)} %copy.80), channel_id=1, source_target_pairs={{0,8},{1,9},{2,10},{3,11},{4,12},{5,13},{6,14},{7,15},{8,0},{9,1},... | collective-permute-start | bytes 786440 | tf_op jit(solution)/shard_map/ppermute | solution.py:46
  242.8 17.4 %collective-permute-start.41 = (bf16[1,2,128,512]{2,3,1,0:T(8,128)(2,1)}, bf16[1,2,128,512]{2,3,1,0:T(8,128)(2,1)S(1)}, u32[]{:S(2)}, u32[]{:S(2)}) collective-permute-start(bf16[1,2,128,512]{2,3,1,0:T(8,128)(2,1)} %copy.82), channel_id=1, source_target_pairs={{0,16},{1,17},{2,18},{3,19},{4,20},{5,21},{6,22},{7,23},{8,24},{9,... | collective-permute-start | bytes 786440 | tf_op jit(solution)/shard_map/ppermute | solution.py:46
  (68 other events, 680.0 us)

commit v2 on v1

v2 whole, which is shorter than its diff:
```python
import functools
import math

import jax
import jax.numpy as jnp
from jax import lax
from jax.experimental import pallas as pl
from jax.experimental.pallas import tpu as pltpu
from jax.sharding import PartitionSpec as P

HEADS = 16
HEAD = 64
AXES = ("dp", "tensor")
LOW = jnp.bfloat16
WIDE = jnp.float32


def together(*values):
    return lax.optimization_barrier(values)


def stats(rows):
    average = jnp.mean(rows, axis=-1, keepdims=True)
    centered = rows - average
    variance = jnp.mean(centered * centered, axis=-1, keepdims=True)
    scale = lax.rsqrt(variance + 1e-05)
    return centered * scale, scale


def norm_back(grad, gain, unit, scale):
    inner = grad * gain
    first = jnp.mean(inner, axis=-1, keepdims=True)
    second = jnp.mean(inner * unit, axis=-1, keepdims=True)
    return scale * (inner - first - unit * second)


def gelu_local(hidden):
    return jax.nn.gelu(hidden, approximate=True)


def clean_dot(x, y, contract):
    return lax.dot_general(x, y, (contract, ((), ())), preferred_element_type=WIDE)


def row_norm(rows):
    centered = rows - jnp.mean(rows, axis=-1, keepdims=True)
    variance = jnp.mean(centered * centered, axis=-1, keepdims=True)
    return centered * lax.rsqrt(variance + 1e-05)


def distances(starts, rows):
    count = starts.shape[0]
    down = lax.broadcasted_iota(jnp.int32, (rows, 1), 0)
    across = lax.broadcasted_iota(jnp.int32, (1, rows), 1)
    down = jnp.concatenate([down + starts[k] for k in range(count)], axis=0)
    across = jnp.concatenate([across + starts[k] for k in range(count)], axis=1)
    return (across - down).astype(WIDE)


def attend_kernel(
    heads, slopes, starts, row_a, gain, shift, weights, bias, row_b, row_c, row_d,
    normed, mixed, context, totals, branch_a, branch_b, branch_c, branch_d, turned,
):
    rows = row_a.shape[0]
    local = heads * HEAD
    for k, block in enumerate((row_a, row_b, row_c, row_d)):
        unit = row_norm(block[...].astype(WIDE))
        low = (unit * gain[...] + shift[...]).astype(LOW)
        here = pl.ds(k * rows, rows)
        normed[here, :] = low
        out = jnp.dot(low, weights[:, : 3 * local], preferred_element_type=WIDE)
        mixed[here, :] = (out + bias[...]).astype(LOW)
    distance = distances(starts, rows)
    allowed = distance >= 0
    for h in range(heads):
        query = mixed[:, pl.ds(h * HEAD, HEAD)]
        key = mixed[:, pl.ds(local + h * HEAD, HEAD)]
        value = mixed[:, pl.ds(2 * local + h * HEAD, HEAD)]
        scores = clean_dot(key, query, ((1,), (1,))) * HEAD ** (-0.5) - slopes[h] * distance
        scores = jnp.where(allowed, scores, -1e30)
        top = jnp.max(scores, axis=0, keepdims=True)
        grown = jnp.exp(scores - top)
        total = jnp.sum(grown, axis=0, keepdims=True)
        totals[h : h + 1, :] = top + jnp.log(total)
        soft = (grown * (1.0 / total)).astype(LOW)
        turned[h * HEAD : (h + 1) * HEAD, :] = jnp.dot(
            value.T, soft, preferred_element_type=WIDE
        ).astype(LOW)
    context[...] = turned[...].T
    for k, block in enumerate((branch_a, branch_b, branch_c, branch_d)):
        out = clean_dot(context[pl.ds(k * rows, rows), :], weights[:, 3 * local :], ((1,), (1,)))
        block[...] = out.astype(block.dtype)


def attend_back_kernel(
    heads, slopes, starts, grad_a, weights, grad_b, grad_c, grad_d, mixed, totals,
    row_a, row_b, row_c, row_d,
    mixed_grad, first_a, first_b, first_c, first_d, sums, vectors, back, turned,
):
    rows = row_a.shape[0]
    local = heads * HEAD
    for k, block in enumerate((grad_a, grad_b, grad_c, grad_d)):
        out = jnp.dot(block[...], weights[:, 3 * local :], preferred_element_type=WIDE)
        back[pl.ds(k * rows, rows), :] = out.astype(LOW)
    distance = distances(starts, rows)
    allowed = distance >= 0
    for h in range(heads):
        query = mixed[:, pl.ds(h * HEAD, HEAD)]
        key = mixed[:, pl.ds(local + h * HEAD, HEAD)]
        value = mixed[:, pl.ds(2 * local + h * HEAD, HEAD)]
        given = back[:, pl.ds(h * HEAD, HEAD)]
        scores = clean_dot(key, query, ((1,), (1,))) * HEAD ** (-0.5) - slopes[h] * distance
        scores = jnp.where(allowed, scores, -1e30)
        soft = jnp.exp(scores - totals[h : h + 1, :])
        value_grad = jnp.dot(soft.astype(LOW), given, preferred_element_type=WIDE)
        soft_grad = clean_dot(value, given, ((1,), (1,)))
        middle = jnp.sum(soft * soft_grad, axis=0, keepdims=True)
        score_grad = (soft * (soft_grad - middle)).astype(LOW)
        key_grad = jnp.dot(score_grad, query, preferred_element_type=WIDE) * HEAD ** (-0.5)
        query_grad = jnp.dot(key.T, score_grad, preferred_element_type=WIDE) * HEAD ** (-0.5)
        turned[h * HEAD : (h + 1) * HEAD, :] = query_grad.astype(LOW)
        mixed_grad[:, pl.ds(local + h * HEAD, HEAD)] = key_grad.astype(LOW)
        mixed_grad[:, pl.ds(2 * local + h * HEAD, HEAD)] = value_grad.astype(LOW)
    mixed_grad[:, :local] = turned[...].T
    sums[...] = jnp.sum(mixed_grad[...].astype(WIDE), axis=0, keepdims=True)
    gain_sum = jnp.zeros(vectors.shape[1:], WIDE)[None]
    shift_sum = gain_sum
    for k, (block, unit) in enumerate(
        ((first_a, row_a), (first_b, row_b), (first_c, row_c), (first_d, row_d))
    ):
        here = mixed_grad[pl.ds(k * rows, rows), :]
        out = clean_dot(here, weights[:, : 3 * local], ((1,), (1,)))
        block[...] = out.astype(block.dtype)
        unit = row_norm(unit[...].astype(WIDE))
        gain_sum = gain_sum + jnp.sum(out * unit, axis=0, keepdims=True)
        shift_sum = shift_sum + jnp.sum(out, axis=0, keepdims=True)
    vectors[0:1, :] = gain_sum
    vectors[1:2, :] = shift_sum


def feed_kernel(
    row_a, expand, bias, top_a, shrink, row_b, top_b, row_c, top_c, row_d, top_d,
    active, back, part_a, part_b, part_c, part_d, sums,
):
    rows = row_a.shape[0]
    wide = active.shape[1]
    total = jnp.zeros((1, wide), WIDE)
    ins = ((row_a, top_a, part_a), (row_b, top_b, part_b), (row_c, top_c, part_c), (row_d, top_d, part_d))
    for k, (row, top, part) in enumerate(ins):
        here = pl.ds(k * rows, rows)
        hidden = jnp.dot(row[...], expand[...], preferred_element_type=WIDE) + bias[...]
        square = hidden * hidden
        curve = jnp.tanh(0.7978845608028654 * hidden * (1.0 + 0.044715 * square))
        half = 0.5 * (1.0 + curve)
        active[here, :] = (hidden * half).astype(LOW)
        slope = 0.7978845608028654 * (1.0 + 3 * 0.044715 * square)
        slope = half + 0.5 * hidden * (1.0 - curve * curve) * slope
        grad = jnp.dot(top[...], shrink[...], preferred_element_type=WIDE)
        grad = (grad * slope).astype(LOW)
        back[here, :] = grad
        total = total + jnp.sum(grad.astype(WIDE), axis=0, keepdims=True)
        out = clean_dot(grad, expand[...], ((1,), (1,)))
        part[...] = out.astype(part.dtype)
    sums[...] = total


class Late:
    def __init__(self, copy, ref):
        self.copy, self.ref, self.shape = copy, ref, ref.shape

    def here(self):
        if self.copy is not None:
            self.copy.wait()
            self.copy = None
        return self.ref

    def __getitem__(self, index):
        return self.here()[index]


def call_kernel(body, scalars, arrays, outs, scratch, flops, mega=32):
    count, first = len(arrays), len(scalars)

    def kernel(*refs):
        sources = refs[first : first + count]
        results = refs[first + count : first + count + len(outs)]
        rest = refs[first + count + len(outs) :]
        held, arrived, own = rest[:count], rest[count], rest[count + 1 :]
        inputs = []
        for k in range(count):
            copy = pltpu.make_async_copy(sources[k], held[k], arrived.at[k])
            copy.start()
            inputs.append(Late(copy, held[k]))
        body(*refs[:first], *inputs, *results, *own)
        for late in inputs:
            late.here()

    def space(array):
        return pl.BlockSpec(array.shape, lambda _: (0,) * len(array.shape))

    sizes = sum(math.prod(a.shape) * a.dtype.itemsize for a in list(arrays) + list(outs))
    return pl.pallas_call(
        kernel,
        grid=(1,),
        in_specs=[pl.BlockSpec(memory_space=pltpu.SMEM)] * first
        + [pl.BlockSpec(memory_space=pltpu.HBM)] * count,
        out_specs=[space(array) for array in outs],
        out_shape=outs,
        scratch_shapes=[pltpu.VMEM(array.shape, array.dtype) for array in arrays]
        + [pltpu.SemaphoreType.DMA((count,))]
        + scratch,
        compiler_params=pltpu.CompilerParams(vmem_limit_bytes=mega << 20),
        cost_estimate=pl.CostEstimate(flops=flops, bytes_accessed=sizes, transcendentals=0),
    )(*scalars, *arrays)


def grads_kernel(steps, x_ref, y_ref, u_ref, v_ref, out_ref, turned):
    step = pl.program_id(0)

    @pl.when(step == 0)
    def _():
        turned[...] = x_ref[...].T

    @pl.when(step == steps)
    def _():
        turned[...] = u_ref[...].T

    @pl.when(step < steps)
    def _():
        out = jnp.dot(turned[...], y_ref[...], preferred_element_type=WIDE)
        out_ref[...] = out.astype(LOW)

    @pl.when(step >= steps)
    def _():
        out = jnp.dot(turned[...], v_ref[...], preferred_element_type=WIDE)
        out_ref[...] = out.astype(LOW)


def weight_grads(x, y, u, v):
    tokens, width = x.shape
    columns = 256
    steps, more = y.shape[1] // columns, v.shape[1] // columns
    whole = pl.BlockSpec((tokens, width), lambda j: (0, 0))
    return pl.pallas_call(
        functools.partial(grads_kernel, steps),
        grid=(steps + more,),
        in_specs=[
            whole,
            pl.BlockSpec((tokens, columns), lambda j: (0, jnp.minimum(j, steps - 1))),
            whole,
            pl.BlockSpec((tokens, columns), lambda j: (0, jnp.maximum(j - steps, 0))),
        ],
        out_specs=pl.BlockSpec((width, columns), lambda j: (0, j)),
        out_shape=jax.ShapeDtypeStruct((width, columns * (steps + more)), LOW),
        scratch_shapes=[pltpu.VMEM((width, tokens), LOW)],
        compiler_params=pltpu.CompilerParams(vmem_limit_bytes=24 << 20),
        cost_estimate=pl.CostEstimate(
            flops=2 * tokens * width * columns * (steps + more),
            bytes_accessed=2 * width * (2 * tokens + columns * (steps + more)),
            transcendentals=0,
        ),
    )(x, y, u, v)


def make_body(n_dp, n_t):
    bits = [1 << k for k in range(1, n_dp.bit_length() - 1)]

    def send(value, target, name):
        pairs = []
        for d in range(n_dp):
            for t in range(n_t):
                goal = target(d, t)
                if goal is not None:
                    pairs.append((d * n_t + t, goal[0] * n_t + goal[1]))
        with jax.named_scope(name):
            return lax.ppermute(value, AXES, pairs)

    def swap_z(value, mask, name):
        return send(value, lambda d, t: (d, t ^ mask), f"{name}_z{mask}")

    def swap_dp(value, mask, name):
        return send(value, lambda d, t: (d ^ mask, t), f"{name}_d{mask}")

    def bit_of(mask):
        return (lax.axis_index("dp") & mask) != 0

    class Spread:
        def __init__(self, first, second, name):
            lead = (1,) * len(bits)
            self.ops = [first.reshape(lead + first.shape), second.reshape(lead + second.shape)]
            self.shapes = (first.shape, second.shape)
            self.name = name
            self.left = list(zip(bits[::-1], bits))

        def go(self):
            self.masks = self.left.pop(0)
            self.others = [
                swap_dp(value, mask, self.name + label)
                for value, mask, label in zip(self.ops, self.masks, ("_a", "_b"))
            ]

        def land(self):
            for k, (mask, other) in enumerate(zip(self.masks, self.others)):
                axis = len(bits) - 1 - bits.index(mask)
                own, flag = self.ops[k], bit_of(mask)
                self.ops[k] = jnp.concatenate(
                    [jnp.where(flag, other, own), jnp.where(flag, own, other)], axis=axis
                )

        def finish(self):
            while self.left:
                self.go()
                self.land()
                self.ops = list(together(*self.ops))
            return [
                value.reshape((-1,) + shape[1:]) for value, shape in zip(self.ops, self.shapes)
            ]

    class Fold:
        def __init__(self, first, second, name):
            lead = (2,) * len(bits)
            self.shapes = (first.shape, second.shape)
            self.values = [
                first.reshape(lead + first.shape[1:]),
                second.reshape(lead + second.shape[1:]),
            ]
            self.name = name
            self.left = list(zip(bits, bits[::-1]))
            self.cut()

        def cut(self):
            self.ops, self.keep = [], []
            for value, mask in zip(self.values, self.left[0]):
                axis = len(bits) - 1 - bits.index(mask)
                place = (lax.axis_index("dp") // mask) % 2
                self.keep.append(lax.dynamic_slice_in_dim(value, place, 1, axis))
                self.ops.append(lax.dynamic_slice_in_dim(value, 1 - place, 1, axis).astype(LOW))

        def go(self):
            masks = self.left.pop(0)
            self.others = [
                swap_dp(value, mask, self.name + label)
                for value, mask, label in zip(self.ops, masks, ("_a", "_b"))
            ]

        def land(self):
            self.values = [
                (keep.astype(WIDE) + other.astype(WIDE)).astype(LOW)
                for keep, other in zip(self.keep, self.others)
            ]
            self.ops = list(self.values)
            if self.left:
                self.cut()

        def finish(self):
            while self.left:
                self.go()
                self.land()
                self.ops = list(together(*self.ops))
            return [value.reshape(shape[1:]) for value, shape in zip(self.ops, self.shapes)]

    def gate(chain, *values):
        count = len(chain.ops)
        *ops, = together(*chain.ops, *values)
        chain.ops = ops[:count]
        return ops[count:]

    def gather_z(value, name):
        one = swap_z(value, 1, name)
        two = swap_z(value, 2, name)
        return [value, one, two, swap_z(two, 1, name + "_far")]

    def fold_far(parts, name):
        far = swap_z(parts[3].astype(LOW), 1, name + "_far")
        return (parts[2].astype(WIDE) + far.astype(WIDE)).astype(LOW)

    def fold_near(parts, both, name):
        two = swap_z(both, 2, name)
        one = swap_z(parts[1].astype(LOW), 1, name)
        return one, two

    def fold_end(parts, one, two):
        return parts[0].astype(WIDE) + one.astype(WIDE) + two.astype(WIDE)

    def body(
        block_input,
        output_cotangent,
        first_gain,
        first_shift,
        project_in,
        query_value_bias,
        project_out,
        project_out_bias,
        second_gain,
        second_shift,
        expand_weight,
        expand_bias,
        shrink_weight,
        shrink_bias,
    ):
        rows, width = block_input.shape
        local = project_out.shape[0]
        wide = expand_weight.shape[1]
        heads = local // HEAD
        core = lax.axis_index("dp") % 2
        place = lax.axis_index("tensor")
        gain_one, shift_one = first_gain.astype(WIDE), first_shift.astype(WIDE)
        gain_two, shift_two = second_gain.astype(WIDE), second_shift.astype(WIDE)
        bias_qv = query_value_bias.astype(WIDE)
        tokens = n_t * rows

        def shape(*dims, kind=WIDE):
            return jax.ShapeDtypeStruct(dims, kind)

        def parts():
            return [shape(rows, width)] + [shape(rows, width, kind=LOW)] * (n_t - 1)


        part_in = project_in.reshape(project_in.shape[0], 3 * local)
        part_a = part_in[:, : 2 * local]
        part_b = jnp.concatenate([part_in[:, 2 * local :], project_out.T], axis=1)
        rows_one = swap_z(block_input, 1, "rows")
        rows_two = swap_z(block_input, 2, "rows")
        attend = Spread(part_a[None], part_b[None], "att")
        attend.go()
        attend.land()
        (rows_one,) = gate(attend, rows_one)
        while len(attend.left) > 1:
            attend.go()
            attend.land()
        attend.go()
        attend.land()
        near = jnp.concatenate([expand_weight, shrink_weight.T], axis=1)
        rows_two, near = gate(attend, rows_two, near)
        rows_three = swap_z(rows_two, 1, "rows_far")
        full_a, full_b = attend.finish()
        pair = jnp.concatenate([full_a, full_b], axis=-1)
        mate = swap_dp(pair, 1, "att")
        full = jnp.stack([jnp.where(core == 0, pair, mate), jnp.where(core == 0, mate, pair)], 1)
        full = full.reshape(width, 4 * local)
        full, near, top_low, rows_three = together(full, near, output_cotangent, rows_three)
        rows_list = [block_input, rows_one, rows_two, rows_three]

        feed = lax.all_gather(near, "dp", axis=0, tiled=True)
        bias_wide = expand_bias.astype(WIDE)
        full_expand, full_shrink = feed[:, :wide], feed[:, wide:]

        bias_full = jnp.concatenate([bias_qv[0], jnp.zeros_like(bias_qv[0]), bias_qv[1]])
        starts = ((jnp.arange(n_t) ^ place) * rows).astype(jnp.int32)
        head_ids = (place * heads + jnp.arange(heads) + 1).astype(WIDE)
        slopes = jnp.exp2(-8.0 * head_ids / HEADS)
        normed_all, mixed, context, totals, *branch_low = call_kernel(
            functools.partial(attend_kernel, heads),
            [slopes, starts],
            [rows_list[0], gain_one[None], shift_one[None], full, bias_full[None]]
            + rows_list[1:],
            [
                shape(tokens, width, kind=LOW),
                shape(tokens, 3 * local, kind=LOW),
                shape(tokens, local, kind=LOW),
                shape(heads, tokens),
            ]
            + parts(),
            [pltpu.VMEM((local, tokens), LOW)],
            2 * tokens * width * 4 * local + 4 * tokens * tokens * local,
        )
        tops_one, tops_two = swap_z(top_low, 1, "tops"), swap_z(top_low, 2, "tops")
        both = fold_far(branch_low, "branch")
        both, tops_one, tops_two, branch_low[1] = together(both, tops_one, tops_two, branch_low[1])
        tops_far = swap_z(tops_two, 1, "tops_far")
        one, two = fold_near(branch_low, both, "branch")
        one, two, tops_far = together(one, two, tops_far)
        tops_list = [top_low, tops_one, tops_two, tops_far]
        branch = fold_end(branch_low, one, two)
        middle = block_input.astype(WIDE) + branch + project_out_bias.astype(WIDE)

        unit_two, scale_two = stats(middle)
        second_low = (unit_two * gain_two + shift_two).astype(LOW)
        second_list = gather_z(second_low, "second")
        active, hidden_grad, *second_parts, expand_bias_part = call_kernel(
            feed_kernel,
            [],
            [second_list[0], full_expand, bias_wide[None], tops_list[0], full_shrink]
            + [block for two in zip(second_list[1:], tops_list[1:]) for block in two],
            [shape(tokens, wide, kind=LOW), shape(tokens, wide, kind=LOW)]
            + parts()
            + [shape(1, wide)],
            [],
            6 * tokens * width * wide,
        )
        second_low_parts = second_parts
        both = fold_far(second_low_parts, "second_grad")
        second_all = jnp.concatenate(second_list, axis=0)
        tops = jnp.concatenate(tops_list, axis=0)
        feed_grad = weight_grads(second_all, hidden_grad, tops, active)
        both, feed_grad = together(both, feed_grad)
        shrunk = jnp.einsum("sf,df->sd", active, full_shrink, preferred_element_type=WIDE)
        shrunk = shrunk.reshape(n_t, rows, width)
        shrunk = [shrunk[0]] + [shrunk[k].astype(LOW) for k in range(1, n_t)]
        second_grad = fold_end(second_low_parts, *fold_near(second_low_parts, both, "second_grad"))
        feed_sum = lax.psum_scatter(feed_grad, "dp", scatter_dimension=0, tiled=True)
        feed_sum = feed_sum.astype(WIDE)
        upstream = output_cotangent.astype(WIDE)
        middle_grad = upstream + norm_back(second_grad, gain_two, unit_two, scale_two)
        middle_list = gather_z(middle_grad.astype(LOW), "middle")
        *middle_list, shrunk[1], shrunk[2], shrunk[3] = together(*middle_list, *shrunk[1:])
        shrunk_both = fold_far(shrunk, "shrunk")

        middle_all = jnp.concatenate(middle_list, axis=0)
        mixed_grad, *first_low, mixed_sums, gain_parts = call_kernel(
            functools.partial(attend_back_kernel, heads),
            [slopes, starts],
            [middle_list[0], full] + middle_list[1:] + [mixed, totals] + rows_list,
            [shape(tokens, 3 * local, kind=LOW)]
            + parts()
            + [shape(1, 3 * local), shape(2, width)],
            [pltpu.VMEM((tokens, local), LOW), pltpu.VMEM((local, tokens), LOW)],
            2 * tokens * width * 4 * local + 10 * tokens * tokens * local,
        )
        mixed_sums = mixed_sums[0]
        shrunk_one, shrunk_two = fold_near(shrunk, shrunk_both, "shrunk")
        both = fold_far(first_low, "first_grad")
        grads = weight_grads(normed_all, mixed_grad, middle_all, context)
        both, grads, shrunk_one, shrunk_two, feed_sum = together(
            both, grads, shrunk_one, shrunk_two, feed_sum
        )
        grads = lax.psum_scatter(grads, "dp", scatter_dimension=0, tiled=True).astype(WIDE)
        in_sum, out_sum = grads[:, : 3 * local], grads[:, 3 * local :].T
        result = middle + fold_end(shrunk, shrunk_one, shrunk_two) + shrink_bias.astype(WIDE)
        result = result.astype(LOW)
        first_one, first_two = fold_near(first_low, both, "first_grad")
        first_one, first_two, gain_parts = together(first_one, first_two, gain_parts)
        first_grad = fold_end(first_low, first_one, first_two)

        unit, scale = stats(block_input.astype(WIDE))
        input_grad = middle_grad + norm_back(first_grad, gain_one, unit, scale)
        slot = jnp.arange(n_t)[:, None]
        bias_slots = jnp.where(slot == place, expand_bias_part, 0.0)
        qv_parts = jnp.stack([mixed_sums[:local], mixed_sums[2 * local :]])
        qv_slots = jnp.where(slot[None] == place, qv_parts[:, None], 0.0)
        vectors = jnp.concatenate(
            [
                jnp.stack(
                    [
                        gain_parts[0],
                        gain_parts[1],
                        jnp.sum(middle_grad, axis=0),
                        jnp.sum(second_grad * unit_two, axis=0),
                        jnp.sum(second_grad, axis=0),
                        jnp.sum(upstream, axis=0),
                    ]
                ),
                bias_slots.reshape(-1, width),
                qv_slots.reshape(2, -1),
            ],
            axis=0,
        )
        for mask in [1] + bits:
            vectors = vectors + swap_dp(vectors, mask, "vectors")
        for mask in (1, 2):
            vectors = vectors + swap_z(vectors, mask, "vectors")
        bias_slots = vectors[6:-2].reshape(n_t, wide)
        expand_bias_sum = lax.dynamic_index_in_dim(bias_slots, place, 0, keepdims=False)
        qv_slots = vectors[-2:].reshape(2, n_t, local)
        qv_sum = lax.dynamic_index_in_dim(qv_slots, place, 1, keepdims=False)
        return (
            result,
            input_grad.astype(LOW),
            vectors[0],
            vectors[1],
            in_sum.reshape(project_in.shape),
            qv_sum,
            out_sum,
            vectors[2],
            vectors[3],
            vectors[4],
            feed_sum[:, :wide],
            expand_bias_sum,
            feed_sum[:, wide:].T,
            vectors[5],
        )

    return body


def solution(mesh):
    placed = (
        P(("dp", "tensor"), None),
        P(("dp", "tensor"), None),
        P(),
        P(),
        P("dp", None, "tensor"),
        P(None, "tensor"),
        P("tensor", "dp"),
        P(),
        P(),
        P(),
        P("dp", "tensor"),
        P("tensor"),
        P("tensor", "dp"),
        P(),
    )
    return jax.shard_map(
        make_body(mesh.shape["dp"], mesh.shape["tensor"]),
        mesh=mesh,
        in_specs=placed,
        out_specs=(
            P(("dp", "tensor"), None),
            P(("dp", "tensor"), None),
            P(),
            P(),
            P("dp", None, "tensor"),
            P(None, "tensor"),
            P("tensor", "dp"),
            P(),
            P(),
            P(),
            P("dp", "tensor"),
            P("tensor"),
            P("tensor", "dp"),
            P(),
        ),
        check_vma=False,
    )
```

time: 275 us -> 253 us (0.920); the launches traced: 270 us -> 252 us
  Pallas kernels: 0 us -> 34.3 us
  matrix products: 26.8 us -> 4.51 us
  waiting for transfers between devices: 127 us -> 111 us
  other arithmetic: 30.9 us -> 18.4 us
  between operations: 2.11 us -> 14.6 us
  starting transfers between devices: 61.9 us -> 50.9 us
  local copies, waits for them, and re-layouts: 22.1 us -> 18.5 us
    pallas_call x0 -> x5, Pallas kernels: none -> 34.3 us  [the longest x3 25.2 us: call_kernel(): pl.pallas_call(kernel, grid=(1,), in_specs=[pl.BlockSpec(memory_space=plt...]
    dot_general x17 -> x0, matrix products: 25.3 us -> none  [the longest x1 4.05 us: body(): jnp.einsum('sf,df->sd', mixed_grad, full_in, preferred_element_type=WIDE)]
    ppermute x50 -> x34, waiting for transfers between devices: 127 us -> 110 us  [send(): return lax.ppermute(value, AXES, pairs)]
    ppermute x50 -> x34, starting transfers between devices: 61.9 us -> 50.8 us  [send(): return lax.ppermute(value, AXES, pairs)]
    reduce_sum x3 -> x0, other arithmetic: 5.41 us -> none  [the longest x1 4.65 us: body(): shift_one_part = jnp.sum(first_part, axis=0)]
    dot_general x1, matrix products: 1.51 us -> 4.51 us  [body(): jnp.einsum('sf,df->sd', active, full_shrink, preferred_element_type=WIDE)]
    unnamed x107 -> x113, local copies, waits for them, and re-layouts: 9.92 us -> 10.4 us
    convert_element_type x15 -> x11, other arithmetic: 7.01 us -> 7.45 us  [the longest x4 3.41 us: fold_far(): return (parts[2].astype(WIDE) + far.astype(WIDE)).astype(LOW)]
  transfers between devices with their start and end apart: 50 -> 37, of which waited for: 23 -> 26; matrix products, arithmetic and copies ran while one was open for 25% -> 11% of each run, Pallas kernels for 0% -> 10%
where the time goes in v2:
time: 253 us; the launch traced here: 252 us
  waiting for transfers between devices  111 us (44%)
  starting transfers between devices  50.9 us (20%)
  Pallas kernels  34.3 us (14%)
  local copies, waits for them, and re-layouts  18.5 us (7%)
  other arithmetic  18.4 us (7%)
  between operations  14.6 us (6%)
  matrix products  4.51 us (2%)
    ppermute x34, waiting for transfers between devices, send(): return lax.ppermute(value, AXES, pairs)  110 us
    ppermute x34, starting transfers between devices, send(): return lax.ppermute(value, AXES, pairs)  50.8 us
    pallas_call x3, Pallas kernels, call_kernel(): pl.pallas_call(kernel, grid=(1,), in_specs=[pl.BlockSpec(memory_space=plt...  25.2 us
    unnamed x113, local copies, waits for them, and re-layouts  10.4 us
    pallas_call x2, Pallas kernels, weight_grads(): pl.pallas_call(functools.partial(grads_kernel, steps), grid=(steps + more...  9.03 us
  transfers between devices with their start and end apart: 37, of which 26 were waited for; matrix products, arithmetic and copies ran while one was open for 11% of the time, Pallas kernels for 10%

profile of v2, /device:TPU:0, one launch (start us, length us, event | category | flops | bytes accessed | tf_op | source)
XLA Modules:
  0.0 252.4 jit_solution(14966186391543329485)
XLA Ops:
  8.4 3.0 %collective-permute-start = (bf16[1,1,1,128,512]{3,4,2,1,0:T(8,128)(2,1)S(1)}, bf16[1,1,1,128,512]{3,4,2,1,0:T(8,128)(2,1)S(1)}, u32[]{:S(2)}, u32[]{:S(2)}) collective-permute-start(bf16[1,1,1,128,512]{3,4,2,1,0:T(8,128)(2,1)S(1)} %slice_bitcast_fusion.2), channel_id=1, source_target_pairs={{0,16},{1,17},{2,18},{3,19},{4,20},{5,21},{6,22},{7,23},{8,24},{9,... | collective-permute-start | bytes 393224 | tf_op jit(solution)/shard_map/att_a_d4/ppermute | solution.py:276
  18.3 3.2 %collective-permute-done.2.refs_7_.refs_10_ = bf16[128,1024]{1,0:T(8,128)(2,1)S(1)} collective-permute-done((bf16[128,1024]{1,0:T(8,128)(2,1)}, bf16[128,1024]{1,0:T(8,128)(2,1)S(1)}, u32[]{:S(2)}, u32[]{:S(2)}) %collective-permute-start.2) | collective-permute-done | bytes 262176 | tf_op jit(solution)/shard_map/rows_z1/ppermute | solution.py:276
  22.1 2.6 %collective-permute-start.5 = (bf16[128,1024]{1,0:T(8,128)(2,1)S(1)}, bf16[128,1024]{1,0:T(8,128)(2,1)S(1)}, u32[]{:S(2)}, u32[]{:S(2)}) collective-permute-start(bf16[128,1024]{1,0:T(8,128)(2,1)S(1)} %copy-done.1), channel_id=1, source_target_pairs={{0,2},{1,3},{2,0},{3,1},{4,6},{5,7},{6,4},{7,5},{8,10},{9,11},{10,... | collective-permute-start | bytes 786440 | tf_op jit(solution)/shard_map/rows_z2/ppermute | solution.py:276
  28.2 3.1 %collective-permute-done.4 = bf16[1,2,1,128,512]{3,4,2,1,0:T(8,128)(2,1)S(1)} collective-permute-done((bf16[1,2,1,128,512]{3,4,2,1,0:T(8,128)(2,1)S(1)}, bf16[1,2,1,128,512]{3,4,2,1,0:T(8,128)(2,1)S(1)}, u32[]{:S(2)}, u32[]{:S(2)}) %collective-permute-start.4) | collective-permute-done | bytes 262176 | tf_op jit(solution)/shard_map/att_b_d4/ppermute | solution.py:276
  31.4 3.5 %collective-permute-done.5.refs_8_.refs_11_ = bf16[128,1024]{1,0:T(8,128)(2,1)S(1)} collective-permute-done((bf16[128,1024]{1,0:T(8,128)(2,1)S(1)}, bf16[128,1024]{1,0:T(8,128)(2,1)S(1)}, u32[]{:S(2)}, u32[]{:S(2)}) %collective-permute-start.5) | collective-permute-done | bytes 262176 | tf_op jit(solution)/shard_map/rows_z2/ppermute | solution.py:276
  40.2 5.1 %collective-permute-done.7.refs_9_.refs_12_ = bf16[128,1024]{1,0:T(8,128)(2,1)S(1)} collective-permute-done((bf16[128,1024]{1,0:T(8,128)(2,1)S(1)}, bf16[128,1024]{1,0:T(8,128)(2,1)S(1)}, u32[]{:S(2)}, u32[]{:S(2)}) %collective-permute-start.7) | collective-permute-done | bytes 262176 | tf_op jit(solution)/shard_map/rows_far_z1/ppermute | solution.py:276
  45.6 6.6 %shard_map.245 = (bf16[512,1024]{1,0:T(8,128)(2,1)S(1)}, bf16[512,768]{1,0:T(8,128)(2,1)S(1)}, bf16[512,256]{1,0:T(8,128)(2,1)S(1)}, f32[4,512]{1,0:T(4,128)S(1)...) custom-call(f32[4]{0:T(128)S(1)} %multiply_exponential_fusion.refs_0, ...), custom_call_target="tpu_custom_call" | custom-call | flops 1342177280 | bytes 6573056 | tf_op jit(solution)/shard_map/pallas_call | solution.py:202
  57.4 10.5 %collective-permute-done.8 = bf16[128,1024]{1,0:T(8,128)(2,1)S(1)} collective-permute-done((bf16[128,1024]{1,0:T(8,128)(2,1)S(1)}, bf16[128,1024]{1,0:T(8,128)(2,1)S(1)}, u32[]{:S(2)}, u32[]{:S(2)}) %collective-permute-start.8) | collective-permute-done | bytes 262176 | tf_op jit(solution)/shard_map/branch_far_z1/ppermute | solution.py:276
  68.0 4.3 %collective-permute-done.9.refs_6_ = bf16[128,1024]{1,0:T(8,128)(2,1)S(1)} collective-permute-done((bf16[128,1024]{1,0:T(8,128)(2,1)S(1)}, bf16[128,1024]{1,0:T(8,128)(2,1)S(1)}, u32[]{:S(2)}, u32[]{:S(2)}) %collective-permute-start.9) | collective-permute-done | bytes 262176 | tf_op jit(solution)/shard_map/tops_z1/ppermute | solution.py:276
  72.3 2.5 collective-permute-start.11
  76.7 10.6 %collective-permute-done.11 = bf16[128,1024]{1,0:T(8,128)(2,1)S(1)} collective-permute-done((bf16[128,1024]{1,0:T(8,128)(2,1)S(1)}, bf16[128,1024]{1,0:T(8,128)(2,1)S(1)}, u32[]{:S(2)}, u32[]{:S(2)}) %collective-permute-start.11) | collective-permute-done | bytes 262176 | tf_op jit(solution)/shard_map/branch_z1/ppermute | solution.py:276
  88.0 3.6 %collective-permute-done.13.refs_10_ = bf16[128,1024]{1,0:T(8,128)(2,1)S(1)} collective-permute-done((bf16[128,1024]{1,0:T(8,128)(2,1)S(1)}, bf16[128,1024]{1,0:T(8,128)(2,1)S(1)}, u32[]{:S(2)}, u32[]{:S(2)}) %collective-permute-start.13) | collective-permute-done | bytes 262176 | tf_op jit(solution)/shard_map/tops_far_z1/ppermute | solution.py:276
  96.3 10.1 %collective-permute-done.15.refs_7_ = bf16[128,1024]{1,0:T(8,128)(2,1)} collective-permute-done((bf16[128,1024]{1,0:T(8,128)(2,1)}, bf16[128,1024]{1,0:T(8,128)(2,1)}, u32[]{:S(2)}, u32[]{:S(2)}) %collective-permute-start.15) | collective-permute-done | bytes 262176 | tf_op jit(solution)/shard_map/second_z2/ppermute | solution.py:276
  106.5 2.7 %fusion.21 = (bf16[1024,1024]{1,0:T(8,128)(2,1)S(1)}, bf16[1024,1024]{1,0:T(8,128)(2,1)S(1)}) fusion(bf16[1024,2048]{1,0:T(8,128)(2,1)} %all-gather.2.cloned.1.call-done), kind=kLoop, calls=%fused_computation.80 | loop fusion | bytes 8388608 | tf_op jit(solution)/shard_map/slice | solution.py:446
  109.2 4.7 %collective-permute-done.16.refs_9_ = bf16[128,1024]{1,0:T(8,128)(2,1)} collective-permute-done((bf16[128,1024]{1,0:T(8,128)(2,1)}, bf16[128,1024]{1,0:T(8,128)(2,1)}, u32[]{:S(2)}, u32[]{:S(2)}) %collective-permute-start.16) | collective-permute-done | bytes 262176 | tf_op jit(solution)/shard_map/second_far_z1/ppermute | solution.py:276
  114.0 9.3 %shard_map.246 = (bf16[512,1024]{1,0:T(8,128)(2,1)S(1)}, bf16[512,1024]{1,0:T(8,128)(2,1)S(1)}, f32[128,1024]{1,0:T(8,128)S(1)}, bf16[128,1024]{1,0:T(8,128)(2,1...) custom-call(bf16[128,1024]{1,0:T(8,128)(2,1)} %add_convert_fusion.3.refs_0_, ...), custom_call_target="tpu_custom_call" | custom-call | flops 3221225472 | bytes 9707520 | tf_op jit(solution)/shard_map/pallas_call | solution.py:202
  125.3 5.2 %shard_map.247 = bf16[1024,2048]{1,0:T(8,128)(2,1)S(1)} custom-call(bf16[512,1024]{1,0:T(8,128)(2,1)S(1)} %pad_maximum_fusion.2.x_ref, bf16[512,1024]{1,0:T(8,128)(2,1)S(1)} %get-tuple-element.98.y_ref, bf16[512,1024]{1,0:T(8,128)(2,1)S(1)} %pad_maximum_fusion.3.u_ref, bf16[512,1024]{1,0:T(8,128)(2,1)S(1)} %get-tuple-element.93.v_ref), custom_call_target="tpu_custom_call" | custom-call | flops 2147483648 | bytes 6291456 | tf_op jit(solution)/shard_map/pallas_call | solution.py:244
  136.7 2.5 collective-permute-start.19
  139.2 8.1 %collective-permute-done.17 = bf16[128,1024]{1,0:T(8,128)(2,1)S(1)} collective-permute-done((bf16[128,1024]{1,0:T(8,128)(2,1)S(1)}, bf16[128,1024]{1,0:T(8,128)(2,1)S(1)}, u32[]{:S(2)}, u32[]{:S(2)}) %collective-permute-start.17) | collective-permute-done | bytes 262176 | tf_op jit(solution)/shard_map/second_grad_z1/ppermute | solution.py:276
  152.5 4.5 %collective-permute-start.20 = (bf16[128,1024]{1,0:T(8,128)(2,1)S(1)}, bf16[128,1024]{1,0:T(8,128)(2,1)S(1)}, u32[]{:S(2)}, u32[]{:S(2)}) collective-permute-start(bf16[128,1024]{1,0:T(8,128)(2,1)S(1)} %convert_element_type.130.refs_2_), channel_id=1, source_target_pairs={{0,1},{1,0},{2,3},{3,2},{4,5},{5,4},{6,7},{7,6},{8,9},{9,8},{10,11... | collective-permute-start | bytes 786440 | tf_op jit(solution)/shard_map/middle_z1/ppermute | solution.py:276
  157.0 5.4 %collective-permute-done.21.refs_5_ = bf16[128,1024]{1,0:T(8,128)(2,1)S(1)} collective-permute-done((bf16[128,1024]{1,0:T(8,128)(2,1)S(1)}, bf16[128,1024]{1,0:T(8,128)(2,1)S(1)}, u32[]{:S(2)}, u32[]{:S(2)}) %collective-permute-start.21) | collective-permute-done | bytes 262176 | tf_op jit(solution)/shard_map/middle_z2/ppermute | solution.py:276
  164.1 4.5 %fusion.26 = (bf16[512,1024]{1,0:T(8,128)(2,1)S(1)}, f32[512,1024]{1,0:T(8,128)}) fusion(bf16[512,1024]{1,0:T(8,128)(2,1)} %copy-done.7, bf16[1024,2048]{1,0:T(8,128)(2,1)} %all-gather.2.cloned.1.call-done), kind=kOutput, calls=%fused_computation.85 | convolution fusion | flops 1074266112 | bytes 6291456 | tf_op jit(solution)/shard_map/sf,df->sd/dot_general | solution.py:497
  172.2 9.3 %shard_map.248 = (bf16[512,768]{1,0:T(8,128)(2,1)S(1)}, f32[128,1024]{1,0:T(8,128)S(1)}, bf16[128,1024]{1,0:T(8,128)(2,1)S(1)}, bf16[128,1024]{1,0:T(8,128)(2,1)...) custom-call(f32[4]{0:T(128)S(1)} %multiply_exponential_fusion.refs_0_, ...), custom_call_target="tpu_custom_call" | custom-call | flops 1744830464 | bytes 7097344 | tf_op jit(solution)/shard_map/pallas_call | solution.py:202
  184.5 3.9 %collective-permute-start.26 = (bf16[128,1024]{1,0:T(8,128)(2,1)}, bf16[128,1024]{1,0:T(8,128)(2,1)S(1)}, u32[]{:S(2)}, u32[]{:S(2)}) collective-permute-start(bf16[128,1024]{1,0:T(8,128)(2,1)} %add_convert_fusion), channel_id=1, source_target_pairs={{0,2},{1,3},{2,0},{3,1},{4,6},{5,7},{6,4},{7,5},{8,10},{9,11},{10,... | collective-permute-start | bytes 786440 | tf_op jit(solution)/shard_map/shrunk_z2/ppermute | solution.py:276
  188.4 3.8 %shard_map.249 = bf16[1024,1024]{1,0:T(8,128)(2,1)} custom-call(bf16[512,1024]{1,0:T(8,128)(2,1)S(1)} %copy-done.3, bf16[512,768]{1,0:T(8,128)(2,1)S(1)} %get-tuple-element.109.y_ref, bf16[512,1024]{1,0:T(8,128)(2,1)S(1)} %pad_maximum_fusion.4.u_ref, bf16[512,256]{1,0:T(8,128)(2,1)S(1)} %copy-done.11), custom_call_target="tpu_custom_call" | custom-call | flops 1073741824 | bytes 4194304 | tf_op jit(solution)/shard_map/pallas_call | solution.py:244
  192.2 4.1 %collective-permute-done.23 = bf16[128,1024]{1,0:T(8,128)(2,1)S(1)} collective-permute-done((bf16[128,1024]{1,0:T(8,128)(2,1)}, bf16[128,1024]{1,0:T(8,128)(2,1)S(1)}, u32[]{:S(2)}, u32[]{:S(2)}) %collective-permute-start.23) | collective-permute-done | bytes 262176 | tf_op jit(solution)/shard_map/first_grad_far_z1/ppermute | solution.py:276
  199.2 5.4 %collective-permute-start.27 = (bf16[128,1024]{1,0:T(8,128)(2,1)S(1)}, bf16[128,1024]{1,0:T(8,128)(2,1)S(1)}, u32[]{:S(2)}, u32[]{:S(2)}) collective-permute-start(bf16[128,1024]{1,0:T(8,128)(2,1)S(1)} %copy-done.28), channel_id=1, source_target_pairs={{0,1},{1,0},{2,3},{3,2},{4,5},{5,4},{6,7},{7,6},{8,9},{9,8},{10,11... | collective-permute-start | bytes 786440 | tf_op jit(solution)/shard_map/first_grad_z1/ppermute | solution.py:276
  206.7 5.7 %collective-permute-done.27 = bf16[128,1024]{1,0:T(8,128)(2,1)S(1)} collective-permute-done((bf16[128,1024]{1,0:T(8,128)(2,1)S(1)}, bf16[128,1024]{1,0:T(8,128)(2,1)S(1)}, u32[]{:S(2)}, u32[]{:S(2)}) %collective-permute-start.27) | collective-permute-done | bytes 262176 | tf_op jit(solution)/shard_map/first_grad_z1/ppermute | solution.py:276
  212.4 4.6 %collective-permute-done.28 = bf16[128,1024]{1,0:T(8,128)(2,1)S(1)} collective-permute-done((bf16[128,1024]{1,0:T(8,128)(2,1)S(1)}, bf16[128,1024]{1,0:T(8,128)(2,1)S(1)}, u32[]{:S(2)}, u32[]{:S(2)}) %collective-permute-start.28) | collective-permute-done | bytes 262176 | tf_op jit(solution)/shard_map/first_grad_z2/ppermute | solution.py:276
  225.2 5.4 %collective-permute-done.31 = f32[12,1024]{1,0:T(8,128)S(1)} collective-permute-done((f32[12,1024]{1,0:T(8,128)S(1)}, f32[12,1024]{1,0:T(8,128)S(1)}, u32[]{:S(2)}, u32[]{:S(2)}) %collective-permute-start.31) | collective-permute-done | bytes 49184 | tf_op jit(solution)/shard_map/vectors_d4/ppermute | solution.py:276
  230.7 4.2 %collective-permute-done.32 = f32[12,1024]{1,0:T(8,128)S(1)} collective-permute-done((f32[12,1024]{1,0:T(8,128)S(1)}, f32[12,1024]{1,0:T(8,128)S(1)}, u32[]{:S(2)}, u32[]{:S(2)}) %collective-permute-start.32) | collective-permute-done | bytes 49184 | tf_op jit(solution)/shard_map/vectors_z1/ppermute | solution.py:276
  236.0 4.3 %collective-permute-done.33 = f32[12,1024]{1,0:T(8,128)S(1)} collective-permute-done((f32[12,1024]{1,0:T(8,128)S(1)}, f32[12,1024]{1,0:T(8,128)S(1)}, u32[]{:S(2)}, u32[]{:S(2)}) %collective-permute-start.33) | collective-permute-done | bytes 49184 | tf_op jit(solution)/shard_map/vectors_z2/ppermute | solution.py:276
  (244 shorter events, 71.3 us)
Async XLA Ops:
  7.2 99.2 %all-gather.2.cloned.1.call-start = ((), (), s32[]{:S(2)}) async-start(), calls=%async_computation.2 | async-start | bytes 4718592 | tf_op jit(solution)/shard_map/all_gather | solution.py:444
  8.4 7.0 %collective-permute-start = (bf16[1,1,1,128,512]{3,4,2,1,0:T(8,128)(2,1)S(1)}, bf16[1,1,1,128,512]{3,4,2,1,0:T(8,128)(2,1)S(1)}, u32[]{:S(2)}, u32[]{:S(2)}) collective-permute-start(bf16[1,1,1,128,512]{3,4,2,1,0:T(8,128)(2,1)S(1)} %slice_bitcast_fusion.2), channel_id=1, source_target_pairs={{0,16},{1,17},{2,18},{3,19},{4,20},{5,21},{6,22},{7,23},{8,24},{9,... | collective-permute-start | bytes 393224 | tf_op jit(solution)/shard_map/att_a_d4/ppermute | solution.py:276
  13.9 7.7 %collective-permute-start.2 = (bf16[128,1024]{1,0:T(8,128)(2,1)}, bf16[128,1024]{1,0:T(8,128)(2,1)S(1)}, u32[]{:S(2)}, u32[]{:S(2)}) collective-permute-start(bf16[128,1024]{1,0:T(8,128)(2,1)} %refs_9_.1), channel_id=1, source_target_pairs={{0,1},{1,0},{2,3},{3,2},{4,5},{5,4},{6,7},{7,6},{8,9},{9,8},{10,11... | collective-permute-start | bytes 786440 | tf_op jit(solution)/shard_map/rows_z1/ppermute | solution.py:276
  21.6 6.6 %collective-permute-start.3 = (bf16[2,1,1,128,512]{3,4,2,1,0:T(8,128)(2,1)S(1)}, bf16[2,1,1,128,512]{3,4,2,1,0:T(8,128)(2,1)S(1)}, u32[]{:S(2)}, u32[]{:S(2)}) collective-permute-start(bf16[2,1,1,128,512]{3,4,2,1,0:T(8,128)(2,1)S(1)} %pad_maximum_fusion.8), channel_id=1, source_target_pairs={{0,8},{1,9},{2,10},{3,11},{4,12},{5,13},{6,14},{7,15},{8,0},{9,1},... | collective-permute-start | bytes 786440 | tf_op jit(solution)/shard_map/att_a_d2/ppermute | solution.py:276
  22.1 12.8 %collective-permute-start.5 = (bf16[128,1024]{1,0:T(8,128)(2,1)S(1)}, bf16[128,1024]{1,0:T(8,128)(2,1)S(1)}, u32[]{:S(2)}, u32[]{:S(2)}) collective-permute-start(bf16[128,1024]{1,0:T(8,128)(2,1)S(1)} %copy-done.1), channel_id=1, source_target_pairs={{0,2},{1,3},{2,0},{3,1},{4,6},{5,7},{6,4},{7,5},{8,10},{9,11},{10,... | collective-permute-start | bytes 786440 | tf_op jit(solution)/shard_map/rows_z2/ppermute | solution.py:276
  24.9 6.4 %collective-permute-start.4 = (bf16[1,2,1,128,512]{3,4,2,1,0:T(8,128)(2,1)S(1)}, bf16[1,2,1,128,512]{3,4,2,1,0:T(8,128)(2,1)S(1)}, u32[]{:S(2)}, u32[]{:S(2)}) collective-permute-start(bf16[1,2,1,128,512]{3,4,2,1,0:T(8,128)(2,1)S(1)} %pad_maximum_fusion.9), channel_id=1, source_target_pairs={{0,16},{1,17},{2,18},{3,19},{4,20},{5,21},{6,22},{7,23},{8,24},{9,... | collective-permute-start | bytes 786440 | tf_op jit(solution)/shard_map/att_b_d4/ppermute | solution.py:276
  36.6 8.7 %collective-permute-start.7 = (bf16[128,1024]{1,0:T(8,128)(2,1)S(1)}, bf16[128,1024]{1,0:T(8,128)(2,1)S(1)}, u32[]{:S(2)}, u32[]{:S(2)}) collective-permute-start(bf16[128,1024]{1,0:T(8,128)(2,1)S(1)} %collective-permute-done.5.refs_8_.refs_11_), channel_id=1, source_target_pairs={{0,1},{1,0},{2,3},{3,2},{4,5},{5,4},{6,7},{7,6},{8,9},{9,8},{10,11... | collective-permute-start | bytes 786440 | tf_op jit(solution)/shard_map/rows_far_z1/ppermute | solution.py:276
  45.3 151.8 %reduce-scatter.3.cloned.1.call-start = ((), (), s32[]{:S(2)}) async-start(), calls=%async_computation.3 | async-start | bytes 4718592 | tf_op jit(solution)/shard_map/reduce_scatter | solution.py:501
  53.1 14.8 %collective-permute-start.8 = (bf16[128,1024]{1,0:T(8,128)(2,1)S(1)}, bf16[128,1024]{1,0:T(8,128)(2,1)S(1)}, u32[]{:S(2)}, u32[]{:S(2)}) collective-permute-start(bf16[128,1024]{1,0:T(8,128)(2,1)S(1)} %get-tuple-element.82), channel_id=1, source_target_pairs={{0,1},{1,0},{2,3},{3,2},{4,5},{5,4},{6,7},{7,6},{8,9},{9,8},{10,11... | collective-permute-start | bytes 786440 | tf_op jit(solution)/shard_map/branch_far_z1/ppermute | solution.py:276
  53.8 18.5 %collective-permute-start.9 = (bf16[128,1024]{1,0:T(8,128)(2,1)S(1)}, bf16[128,1024]{1,0:T(8,128)(2,1)S(1)}, u32[]{:S(2)}, u32[]{:S(2)}) collective-permute-start(bf16[128,1024]{1,0:T(8,128)(2,1)S(1)} %copy-done.4), channel_id=1, source_target_pairs={{0,1},{1,0},{2,3},{3,2},{4,5},{5,4},{6,7},{7,6},{8,9},{9,8},{10,11... | collective-permute-start | bytes 786440 | tf_op jit(solution)/shard_map/tops_z1/ppermute | solution.py:276
  55.1 17.1 %collective-permute-start.10 = (bf16[128,1024]{1,0:T(8,128)(2,1)S(1)}, bf16[128,1024]{1,0:T(8,128)(2,1)S(1)}, u32[]{:S(2)}, u32[]{:S(2)}) collective-permute-start(bf16[128,1024]{1,0:T(8,128)(2,1)S(1)} %copy-done.4), channel_id=1, source_target_pairs={{0,2},{1,3},{2,0},{3,1},{4,6},{5,7},{6,4},{7,5},{8,10},{9,11},{10,... | collective-permute-start | bytes 786440 | tf_op jit(solution)/shard_map/tops_z2/ppermute | solution.py:276
  72.3 15.0 %collective-permute-start.11 = (bf16[128,1024]{1,0:T(8,128)(2,1)S(1)}, bf16[128,1024]{1,0:T(8,128)(2,1)S(1)}, u32[]{:S(2)}, u32[]{:S(2)}) collective-permute-start(bf16[128,1024]{1,0:T(8,128)(2,1)S(1)} %get-tuple-element.85), channel_id=1, source_target_pairs={{0,1},{1,0},{2,3},{3,2},{4,5},{5,4},{6,7},{7,6},{8,9},{9,8},{10,11... | collective-permute-start | bytes 786440 | tf_op jit(solution)/shard_map/branch_z1/ppermute | solution.py:276
  74.8 13.2 %collective-permute-start.12 = (bf16[128,1024]{1,0:T(8,128)(2,1)S(1)}, bf16[128,1024]{1,0:T(8,128)(2,1)S(1)}, u32[]{:S(2)}, u32[]{:S(2)}) collective-permute-start(bf16[128,1024]{1,0:T(8,128)(2,1)S(1)} %add_convert_fusion.4), channel_id=1, source_target_pairs={{0,2},{1,3},{2,0},{3,1},{4,6},{5,7},{6,4},{7,5},{8,10},{9,11},{10,... | collective-permute-start | bytes 786440 | tf_op jit(solution)/shard_map/branch_z2/ppermute | solution.py:276
  76.4 15.2 %collective-permute-start.13 = (bf16[128,1024]{1,0:T(8,128)(2,1)S(1)}, bf16[128,1024]{1,0:T(8,128)(2,1)S(1)}, u32[]{:S(2)}, u32[]{:S(2)}) collective-permute-start(bf16[128,1024]{1,0:T(8,128)(2,1)S(1)} %collective-permute-done.10.refs_8_), channel_id=1, source_target_pairs={{0,1},{1,0},{2,3},{3,2},{4,5},{5,4},{6,7},{7,6},{8,9},{9,8},{10,11... | collective-permute-start | bytes 786440 | tf_op jit(solution)/shard_map/tops_far_z1/ppermute | solution.py:276
  93.0 13.5 %collective-permute-start.15 = (bf16[128,1024]{1,0:T(8,128)(2,1)}, bf16[128,1024]{1,0:T(8,128)(2,1)}, u32[]{:S(2)}, u32[]{:S(2)}) collective-permute-start(bf16[128,1024]{1,0:T(8,128)(2,1)} %add_convert_fusion.3.refs_0_), channel_id=1, source_target_pairs={{0,2},{1,3},{2,0},{3,1},{4,6},{5,7},{6,4},{7,5},{8,10},{9,11},{10,... | collective-permute-start | bytes 786440 | tf_op jit(solution)/shard_map/second_z2/ppermute | solution.py:276
  94.5 14.7 %collective-permute-start.14 = (bf16[128,1024]{1,0:T(8,128)(2,1)}, bf16[128,1024]{1,0:T(8,128)(2,1)}, u32[]{:S(2)}, u32[]{:S(2)}) collective-permute-start(bf16[128,1024]{1,0:T(8,128)(2,1)} %add_convert_fusion.3.refs_0_), channel_id=1, source_target_pairs={{0,1},{1,0},{2,3},{3,2},{4,5},{5,4},{6,7},{7,6},{8,9},{9,8},{10,11... | collective-permute-start | bytes 786440 | tf_op jit(solution)/shard_map/second_z1/ppermute | solution.py:276
  106.4 7.5 %collective-permute-start.16 = (bf16[128,1024]{1,0:T(8,128)(2,1)}, bf16[128,1024]{1,0:T(8,128)(2,1)}, u32[]{:S(2)}, u32[]{:S(2)}) collective-permute-start(bf16[128,1024]{1,0:T(8,128)(2,1)} %collective-permute-done.15.refs_7_), channel_id=1, source_target_pairs={{0,1},{1,0},{2,3},{3,2},{4,5},{5,4},{6,7},{7,6},{8,9},{9,8},{10,11... | collective-permute-start | bytes 786440 | tf_op jit(solution)/shard_map/second_far_z1/ppermute | solution.py:276
  123.3 9.3 %collective-permute-start.18 = (bf16[128,1024]{1,0:T(8,128)(2,1)}, bf16[128,1024]{1,0:T(8,128)(2,1)}, u32[]{:S(2)}, u32[]{:S(2)}) collective-permute-start(bf16[128,1024]{1,0:T(8,128)(2,1)} %get-tuple-element.97), channel_id=1, source_target_pairs={{0,1},{1,0},{2,3},{3,2},{4,5},{5,4},{6,7},{7,6},{8,9},{9,8},{10,11... | collective-permute-start | bytes 786440 | tf_op jit(solution)/shard_map/second_grad_far_z1/ppermute | solution.py:276
  134.4 108.6 %reduce-scatter.5.cloned.1.call-start = ((), (), s32[]{:S(2)}) async-start(), calls=%async_computation.4 | async-start | bytes 2359296 | tf_op jit(solution)/shard_map/reduce_scatter | solution.py:527
  135.3 12.1 %collective-permute-start.17 = (bf16[128,1024]{1,0:T(8,128)(2,1)S(1)}, bf16[128,1024]{1,0:T(8,128)(2,1)S(1)}, u32[]{:S(2)}, u32[]{:S(2)}) collective-permute-start(bf16[128,1024]{1,0:T(8,128)(2,1)S(1)} %copy-done.30), channel_id=1, source_target_pairs={{0,1},{1,0},{2,3},{3,2},{4,5},{5,4},{6,7},{7,6},{8,9},{9,8},{10,11... | collective-permute-start | bytes 786440 | tf_op jit(solution)/shard_map/second_grad_z1/ppermute | solution.py:276
  136.7 10.7 %collective-permute-start.19 = (bf16[128,1024]{1,0:T(8,128)(2,1)}, bf16[128,1024]{1,0:T(8,128)(2,1)S(1)}, u32[]{:S(2)}, u32[]{:S(2)}) collective-permute-start(bf16[128,1024]{1,0:T(8,128)(2,1)} %add_convert_fusion.2), channel_id=1, source_target_pairs={{0,2},{1,3},{2,0},{3,1},{4,6},{5,7},{6,4},{7,5},{8,10},{9,11},{10,... | collective-permute-start | bytes 786440 | tf_op jit(solution)/shard_map/second_grad_z2/ppermute | solution.py:276
  150.0 12.4 %collective-permute-start.21 = (bf16[128,1024]{1,0:T(8,128)(2,1)S(1)}, bf16[128,1024]{1,0:T(8,128)(2,1)S(1)}, u32[]{:S(2)}, u32[]{:S(2)}) collective-permute-start(bf16[128,1024]{1,0:T(8,128)(2,1)S(1)} %convert_element_type.130.refs_2_), channel_id=1, source_target_pairs={{0,2},{1,3},{2,0},{3,1},{4,6},{5,7},{6,4},{7,5},{8,10},{9,11},{10,... | collective-permute-start | bytes 786440 | tf_op jit(solution)/shard_map/middle_z2/ppermute | solution.py:276
  152.5 16.9 %collective-permute-start.20 = (bf16[128,1024]{1,0:T(8,128)(2,1)S(1)}, bf16[128,1024]{1,0:T(8,128)(2,1)S(1)}, u32[]{:S(2)}, u32[]{:S(2)}) collective-permute-start(bf16[128,1024]{1,0:T(8,128)(2,1)S(1)} %convert_element_type.130.refs_2_), channel_id=1, source_target_pairs={{0,1},{1,0},{2,3},{3,2},{4,5},{5,4},{6,7},{7,6},{8,9},{9,8},{10,11... | collective-permute-start | bytes 786440 | tf_op jit(solution)/shard_map/middle_z1/ppermute | solution.py:276
  162.4 7.1 %collective-permute-start.22 = (bf16[128,1024]{1,0:T(8,128)(2,1)S(1)}, bf16[128,1024]{1,0:T(8,128)(2,1)S(1)}, u32[]{:S(2)}, u32[]{:S(2)}) collective-permute-start(bf16[128,1024]{1,0:T(8,128)(2,1)S(1)} %collective-permute-done.21.refs_5_), channel_id=1, source_target_pairs={{0,1},{1,0},{2,3},{3,2},{4,5},{5,4},{6,7},{7,6},{8,9},{9,8},{10,11... | collective-permute-start | bytes 786440 | tf_op jit(solution)/shard_map/middle_far_z1/ppermute | solution.py:276
  169.5 14.3 %collective-permute-start.25 = (bf16[128,1024]{1,0:T(8,128)(2,1)S(1)}, bf16[128,1024]{1,0:T(8,128)(2,1)S(1)}, u32[]{:S(2)}, u32[]{:S(2)}) collective-permute-start(bf16[128,1024]{1,0:T(8,128)(2,1)S(1)} %get-tuple-element.113), channel_id=1, source_target_pairs={{0,1},{1,0},{2,3},{3,2},{4,5},{5,4},{6,7},{7,6},{8,9},{9,8},{10,11... | collective-permute-start | bytes 786440 | tf_op jit(solution)/shard_map/shrunk_far_z1/ppermute | solution.py:276
  181.5 14.7 %collective-permute-start.23 = (bf16[128,1024]{1,0:T(8,128)(2,1)}, bf16[128,1024]{1,0:T(8,128)(2,1)S(1)}, u32[]{:S(2)}, u32[]{:S(2)}) collective-permute-start(bf16[128,1024]{1,0:T(8,128)(2,1)} %get-tuple-element.107), channel_id=1, source_target_pairs={{0,1},{1,0},{2,3},{3,2},{4,5},{5,4},{6,7},{7,6},{8,9},{9,8},{10,11... | collective-permute-start | bytes 786440 | tf_op jit(solution)/shard_map/first_grad_far_z1/ppermute | solution.py:276
  181.9 17.2 %collective-permute-start.24 = (bf16[128,1024]{1,0:T(8,128)(2,1)}, bf16[128,1024]{1,0:T(8,128)(2,1)S(1)}, u32[]{:S(2)}, u32[]{:S(2)}) collective-permute-start(bf16[128,1024]{1,0:T(8,128)(2,1)} %get-tuple-element.111), channel_id=1, source_target_pairs={{0,1},{1,0},{2,3},{3,2},{4,5},{5,4},{6,7},{7,6},{8,9},{9,8},{10,11... | collective-permute-start | bytes 786440 | tf_op jit(solution)/shard_map/shrunk_z1/ppermute | solution.py:276
  184.5 14.6 %collective-permute-start.26 = (bf16[128,1024]{1,0:T(8,128)(2,1)}, bf16[128,1024]{1,0:T(8,128)(2,1)S(1)}, u32[]{:S(2)}, u32[]{:S(2)}) collective-permute-start(bf16[128,1024]{1,0:T(8,128)(2,1)} %add_convert_fusion), channel_id=1, source_target_pairs={{0,2},{1,3},{2,0},{3,1},{4,6},{5,7},{6,4},{7,5},{8,10},{9,11},{10,... | collective-permute-start | bytes 786440 | tf_op jit(solution)/shard_map/shrunk_z2/ppermute | solution.py:276
  199.2 13.2 %collective-permute-start.27 = (bf16[128,1024]{1,0:T(8,128)(2,1)S(1)}, bf16[128,1024]{1,0:T(8,128)(2,1)S(1)}, u32[]{:S(2)}, u32[]{:S(2)}) collective-permute-start(bf16[128,1024]{1,0:T(8,128)(2,1)S(1)} %copy-done.28), channel_id=1, source_target_pairs={{0,1},{1,0},{2,3},{3,2},{4,5},{5,4},{6,7},{7,6},{8,9},{9,8},{10,11... | collective-permute-start | bytes 786440 | tf_op jit(solution)/shard_map/first_grad_z1/ppermute | solution.py:276
  204.7 12.3 %collective-permute-start.28 = (bf16[128,1024]{1,0:T(8,128)(2,1)S(1)}, bf16[128,1024]{1,0:T(8,128)(2,1)S(1)}, u32[]{:S(2)}, u32[]{:S(2)}) collective-permute-start(bf16[128,1024]{1,0:T(8,128)(2,1)S(1)} %copy-done.39), channel_id=1, source_target_pairs={{0,2},{1,3},{2,0},{3,1},{4,6},{5,7},{6,4},{7,5},{8,10},{9,11},{10,... | collective-permute-start | bytes 786440 | tf_op jit(solution)/shard_map/first_grad_z2/ppermute | solution.py:276
  224.8 5.9 %collective-permute-start.31 = (f32[12,1024]{1,0:T(8,128)S(1)}, f32[12,1024]{1,0:T(8,128)S(1)}, u32[]{:S(2)}, u32[]{:S(2)}) collective-permute-start(f32[12,1024]{1,0:T(8,128)S(1)} %add.155), channel_id=1, source_target_pairs={{0,16},{1,17},{2,18},{3,19},{4,20},{5,21},{6,22},{7,23},{8,24},{9,... | collective-permute-start | bytes 147464 | tf_op jit(solution)/shard_map/vectors_d4/ppermute | solution.py:276
  235.0 5.4 %collective-permute-start.33 = (f32[12,1024]{1,0:T(8,128)S(1)}, f32[12,1024]{1,0:T(8,128)S(1)}, u32[]{:S(2)}, u32[]{:S(2)}) collective-permute-start(f32[12,1024]{1,0:T(8,128)S(1)} %add.157), channel_id=1, source_target_pairs={{0,2},{1,3},{2,0},{3,1},{4,6},{5,7},{6,4},{7,5},{8,10},{9,11},{10,... | collective-permute-start | bytes 147464 | tf_op jit(solution)/shard_map/vectors_z2/ppermute | solution.py:276
  (58 other events, 624.8 us)
Sparse Core Ops, SparseCore 0:
  45.4 36.8 all-gather.1
  134.5 51.3 reduce-scatter.2
  199.2 43.6 reduce-scatter.4

commit v3 on v2

--- a/solution.py
+++ b/solution.py
@@ -139,7 +139,7 @@
 
 
 def feed_kernel(
-    row_a, expand, bias, top_a, shrink, row_b, top_b, row_c, top_c, row_d, top_d,
+    row_a, weights, bias, top_a, row_b, top_b, row_c, top_c, row_d, top_d,
     active, back, part_a, part_b, part_c, part_d, sums,
 ):
     rows = row_a.shape[0]
@@ -148,18 +148,18 @@
     ins = ((row_a, top_a, part_a), (row_b, top_b, part_b), (row_c, top_c, part_c), (row_d, top_d, part_d))
     for k, (row, top, part) in enumerate(ins):
         here = pl.ds(k * rows, rows)
-        hidden = jnp.dot(row[...], expand[...], preferred_element_type=WIDE) + bias[...]
+        hidden = jnp.dot(row[...], weights[:, :wide], preferred_element_type=WIDE) + bias[...]
         square = hidden * hidden
         curve = jnp.tanh(0.7978845608028654 * hidden * (1.0 + 0.044715 * square))
         half = 0.5 * (1.0 + curve)
         active[here, :] = (hidden * half).astype(LOW)
         slope = 0.7978845608028654 * (1.0 + 3 * 0.044715 * square)
         slope = half + 0.5 * hidden * (1.0 - curve * curve) * slope
-        grad = jnp.dot(top[...], shrink[...], preferred_element_type=WIDE)
+        grad = jnp.dot(top[...], weights[:, wide:], preferred_element_type=WIDE)
         grad = (grad * slope).astype(LOW)
         back[here, :] = grad
         total = total + jnp.sum(grad.astype(WIDE), axis=0, keepdims=True)
-        out = clean_dot(grad, expand[...], ((1,), (1,)))
+        out = clean_dot(grad, weights[:, :wide], ((1,), (1,)))
         part[...] = out.astype(part.dtype)
     sums[...] = total
 
@@ -214,16 +214,25 @@
     )(*scalars, *arrays)
 
 
-def grads_kernel(steps, x_ref, y_ref, u_ref, v_ref, out_ref, turned):
+def grads_kernel(steps, count, *refs):
+    blocks, others = refs[:count], refs[count + 1 : -4]
+    y_ref, v_ref, out_ref, more_ref, turned = refs[count], *refs[-4:]
     step = pl.program_id(0)
+
+    def turn(pieces):
+        first = 0
+        for piece in pieces:
+            size = piece.shape[0]
+            turned[:, first : first + size] = piece[...].T
+            first += size
 
     @pl.when(step == 0)
     def _():
-        turned[...] = x_ref[...].T
+        turn(blocks)
 
     @pl.when(step == steps)
     def _():
-        turned[...] = u_ref[...].T
+        turn(others)
 
     @pl.when(step < steps)
     def _():
@@ -233,25 +242,29 @@
     @pl.when(step >= steps)
     def _():
         out = jnp.dot(turned[...], v_ref[...], preferred_element_type=WIDE)
-        out_ref[...] = out.astype(LOW)
-
-
-def weight_grads(x, y, u, v):
-    tokens, width = x.shape
+        more_ref[...] = out.astype(LOW)
+
+
+def weight_grads(blocks, y, others, v):
+    tokens, width = y.shape[0], blocks[0].shape[1]
     columns = 256
     steps, more = y.shape[1] // columns, v.shape[1] // columns
-    whole = pl.BlockSpec((tokens, width), lambda j: (0, 0))
+
+    def whole(block):
+        return pl.BlockSpec(block.shape, lambda j: (0, 0))
+
     return pl.pallas_call(
-        functools.partial(grads_kernel, steps),
+        functools.partial(grads_kernel, steps, len(blocks)),
         grid=(steps + more,),
-        in_specs=[
-            whole,
-            pl.BlockSpec((tokens, columns), lambda j: (0, jnp.minimum(j, steps - 1))),
-            whole,
-            pl.BlockSpec((tokens, columns), lambda j: (0, jnp.maximum(j - steps, 0))),
+        in_specs=[whole(block) for block in blocks]
+        + [pl.BlockSpec((tokens, columns), lambda j: (0, jnp.minimum(j, steps - 1)))]
+        + [whole(block) for block in others]
+        + [pl.BlockSpec((tokens, columns), lambda j: (0, jnp.maximum(j - steps, 0)))],
+        out_specs=[
+            pl.BlockSpec((width, columns), lambda j: (0, jnp.minimum(j, steps - 1))),
+            pl.BlockSpec((width, columns), lambda j: (0, jnp.maximum(j - steps, 0))),
         ],
-        out_specs=pl.BlockSpec((width, columns), lambda j: (0, j)),
-        out_shape=jax.ShapeDtypeStruct((width, columns * (steps + more)), LOW),
+        out_shape=[jax.ShapeDtypeStruct((width, z.shape[1]), LOW) for z in (y, v)],
         scratch_shapes=[pltpu.VMEM((width, tokens), LOW)],
         compiler_params=pltpu.CompilerParams(vmem_limit_bytes=24 << 20),
         cost_estimate=pl.CostEstimate(
@@ -259,7 +272,7 @@
             bytes_accessed=2 * width * (2 * tokens + columns * (steps + more)),
             transcendentals=0,
         ),
-    )(x, y, u, v)
+    )(*blocks, y, *others, v)
 
 
 def make_body(n_dp, n_t):
@@ -419,31 +432,26 @@
         part_in = project_in.reshape(project_in.shape[0], 3 * local)
         part_a = part_in[:, : 2 * local]
         part_b = jnp.concatenate([part_in[:, 2 * local :], project_out.T], axis=1)
+        near = jnp.concatenate([expand_weight, shrink_weight.T], axis=1)
         rows_one = swap_z(block_input, 1, "rows")
         rows_two = swap_z(block_input, 2, "rows")
         attend = Spread(part_a[None], part_b[None], "att")
         attend.go()
         attend.land()
-        (rows_one,) = gate(attend, rows_one)
-        while len(attend.left) > 1:
-            attend.go()
-            attend.land()
-        attend.go()
-        attend.land()
-        near = jnp.concatenate([expand_weight, shrink_weight.T], axis=1)
-        rows_two, near = gate(attend, rows_two, near)
+        rows_one, rows_two, near = gate(attend, rows_one, rows_two, near)
         rows_three = swap_z(rows_two, 1, "rows_far")
         full_a, full_b = attend.finish()
+        full_a, full_b, near, rows_three, top_low = together(
+            full_a, full_b, near, rows_three, output_cotangent
+        )
         pair = jnp.concatenate([full_a, full_b], axis=-1)
         mate = swap_dp(pair, 1, "att")
         full = jnp.stack([jnp.where(core == 0, pair, mate), jnp.where(core == 0, mate, pair)], 1)
         full = full.reshape(width, 4 * local)
-        full, near, top_low, rows_three = together(full, near, output_cotangent, rows_three)
         rows_list = [block_input, rows_one, rows_two, rows_three]
 
         feed = lax.all_gather(near, "dp", axis=0, tiled=True)
         bias_wide = expand_bias.astype(WIDE)
-        full_expand, full_shrink = feed[:, :wide], feed[:, wide:]
 
         bias_full = jnp.concatenate([bias_qv[0], jnp.zeros_like(bias_qv[0]), bias_qv[1]])
         starts = ((jnp.arange(n_t) ^ place) * rows).astype(jnp.int32)
@@ -465,11 +473,11 @@
             2 * tokens * width * 4 * local + 4 * tokens * tokens * local,
         )
         tops_one, tops_two = swap_z(top_low, 1, "tops"), swap_z(top_low, 2, "tops")
+        branch_low[3], tops_one, tops_two = together(branch_low[3], tops_one, tops_two)
         both = fold_far(branch_low, "branch")
-        both, tops_one, tops_two, branch_low[1] = together(both, tops_one, tops_two, branch_low[1])
+        one, two = fold_near(branch_low, both, "branch")
+        one, two, tops_two, feed = together(one, two, tops_two, feed)
         tops_far = swap_z(tops_two, 1, "tops_far")
-        one, two = fold_near(branch_low, both, "branch")
-        one, two, tops_far = together(one, two, tops_far)
         tops_list = [top_low, tops_one, tops_two, tops_far]
         branch = fold_end(branch_low, one, two)
         middle = block_input.astype(WIDE) + branch + project_out_bias.astype(WIDE)
@@ -480,7 +488,7 @@
         active, hidden_grad, *second_parts, expand_bias_part = call_kernel(
             feed_kernel,
             [],
-            [second_list[0], full_expand, bias_wide[None], tops_list[0], full_shrink]
+            [second_list[0], feed, bias_wide[None], tops_list[0]]
             + [block for two in zip(second_list[1:], tops_list[1:]) for block in two],
             [shape(tokens, wide, kind=LOW), shape(tokens, wide, kind=LOW)]
             + parts()
@@ -490,23 +498,26 @@
         )
         second_low_parts = second_parts
         both = fold_far(second_low_parts, "second_grad")
-        second_all = jnp.concatenate(second_list, axis=0)
-        tops = jnp.concatenate(tops_list, axis=0)
-        feed_grad = weight_grads(second_all, hidden_grad, tops, active)
-        both, feed_grad = together(both, feed_grad)
-        shrunk = jnp.einsum("sf,df->sd", active, full_shrink, preferred_element_type=WIDE)
-        shrunk = shrunk.reshape(n_t, rows, width)
-        shrunk = [shrunk[0]] + [shrunk[k].astype(LOW) for k in range(1, n_t)]
-        second_grad = fold_end(second_low_parts, *fold_near(second_low_parts, both, "second_grad"))
+        both, hidden_grad, active = together(both, hidden_grad, active)
+        one, two = fold_near(second_low_parts, both, "second_grad")
+        feed_grad = weight_grads(second_list, hidden_grad, tops_list, active)
+        one, two, *feed_grad = together(one, two, *feed_grad)
+        second_grad = fold_end(second_low_parts, one, two)
+        feed_grad = jnp.concatenate(feed_grad, axis=1)
         feed_sum = lax.psum_scatter(feed_grad, "dp", scatter_dimension=0, tiled=True)
         feed_sum = feed_sum.astype(WIDE)
+
         upstream = output_cotangent.astype(WIDE)
         middle_grad = upstream + norm_back(second_grad, gain_two, unit_two, scale_two)
         middle_list = gather_z(middle_grad.astype(LOW), "middle")
-        *middle_list, shrunk[1], shrunk[2], shrunk[3] = together(*middle_list, *shrunk[1:])
+        middle_list[1], middle_list[2], active = together(middle_list[1], middle_list[2], active)
+        middle_list[3] = swap_z(middle_list[2], 1, "middle_far")
+        shrunk = jnp.einsum("sf,df->sd", active, feed[:, wide:], preferred_element_type=WIDE)
+        shrunk = shrunk.reshape(n_t, rows, width)
+        shrunk = [shrunk[0]] + [shrunk[k].astype(LOW) for k in range(1, n_t)]
+        middle_list[3], *shrunk[1:] = together(middle_list[3], *shrunk[1:])
         shrunk_both = fold_far(shrunk, "shrunk")
 
-        middle_all = jnp.concatenate(middle_list, axis=0)
         mixed_grad, *first_low, mixed_sums, gain_parts = call_kernel(
             functools.partial(attend_back_kernel, heads),
             [slopes, starts],
@@ -516,49 +527,61 @@
             + [shape(1, 3 * local), shape(2, width)],
             [pltpu.VMEM((tokens, local), LOW), pltpu.VMEM((local, tokens), LOW)],
             2 * tokens * width * 4 * local + 10 * tokens * tokens * local,
+            58,
         )
         mixed_sums = mixed_sums[0]
-        shrunk_one, shrunk_two = fold_near(shrunk, shrunk_both, "shrunk")
-        both = fold_far(first_low, "first_grad")
-        grads = weight_grads(normed_all, mixed_grad, middle_all, context)
-        both, grads, shrunk_one, shrunk_two, feed_sum = together(
-            both, grads, shrunk_one, shrunk_two, feed_sum
-        )
-        grads = lax.psum_scatter(grads, "dp", scatter_dimension=0, tiled=True).astype(WIDE)
-        in_sum, out_sum = grads[:, : 3 * local], grads[:, 3 * local :].T
-        result = middle + fold_end(shrunk, shrunk_one, shrunk_two) + shrink_bias.astype(WIDE)
-        result = result.astype(LOW)
-        first_one, first_two = fold_near(first_low, both, "first_grad")
-        first_one, first_two, gain_parts = together(first_one, first_two, gain_parts)
-        first_grad = fold_end(first_low, first_one, first_two)
-
-        unit, scale = stats(block_input.astype(WIDE))
-        input_grad = middle_grad + norm_back(first_grad, gain_one, unit, scale)
         slot = jnp.arange(n_t)[:, None]
         bias_slots = jnp.where(slot == place, expand_bias_part, 0.0)
         qv_parts = jnp.stack([mixed_sums[:local], mixed_sums[2 * local :]])
         qv_slots = jnp.where(slot[None] == place, qv_parts[:, None], 0.0)
+        early = [
+            jnp.sum(middle_grad, axis=0),
+            jnp.sum(second_grad * unit_two, axis=0),
+            jnp.sum(second_grad, axis=0),
+            jnp.sum(upstream, axis=0),
+        ]
         vectors = jnp.concatenate(
-            [
-                jnp.stack(
-                    [
-                        gain_parts[0],
-                        gain_parts[1],
-                        jnp.sum(middle_grad, axis=0),
-                        jnp.sum(second_grad * unit_two, axis=0),
-                        jnp.sum(second_grad, axis=0),
-                        jnp.sum(upstream, axis=0),
-                    ]
-                ),
-                bias_slots.reshape(-1, width),
-                qv_slots.reshape(2, -1),
-            ],
+            [gain_parts, jnp.stack(early), bias_slots.reshape(-1, width), qv_slots.reshape(2, -1)],
             axis=0,
         )
-        for mask in [1] + bits:
+        first_low[3], shrunk_both, shrunk[1], mixed_grad, vectors = together(
+            first_low[3], shrunk_both, shrunk[1], mixed_grad, vectors
+        )
+        both = fold_far(first_low, "first_grad")
+        shrunk_one, shrunk_two = fold_near(shrunk, shrunk_both, "shrunk")
+        vectors = vectors + swap_z(vectors, 1, "vectors")
+        in_grad, out_grad = weight_grads([normed_all], mixed_grad, middle_list, context)
+        blocks = n_dp // 2
+        grads = jnp.concatenate([in_grad, out_grad], axis=1).reshape(blocks, 2, -1, 4 * local)
+        mine = lax.dynamic_slice_in_dim(grads, core, 1, 1)
+        other = lax.dynamic_slice_in_dim(grads, 1 - core, 1, 1)
+        both, other, vectors, shrunk_one, shrunk_two = together(
+            both, other, vectors, shrunk_one, shrunk_two
+        )
+        first_one, first_two = fold_near(first_low, both, "first_grad")
+        swapped = swap_dp(other, 1, "att_grad")
+        vectors = vectors + swap_dp(vectors, 1, "vectors")
+        grads = (mine.astype(WIDE) + swapped.astype(WIDE)).astype(LOW)
+        grads = grads.reshape(blocks, -1, 4 * local)
+        attend = Fold(grads[:, :, : 2 * local], grads[:, :, 2 * local :], "att_grad")
+        (vectors,) = gate(attend, vectors)
+        attend.go()
+        for mask in bits[:1]:
             vectors = vectors + swap_dp(vectors, mask, "vectors")
-        for mask in (1, 2):
-            vectors = vectors + swap_z(vectors, mask, "vectors")
+        attend.land()
+        first_one, first_two, vectors = gate(attend, first_one, first_two, vectors)
+        for mask in bits[1:]:
+            vectors = vectors + swap_dp(vectors, mask, "vectors")
+        vectors = vectors + swap_z(vectors, 2, "vectors")
+        sum_a, sum_b = attend.finish()
+        in_sum = jnp.concatenate([sum_a, sum_b[:, :local]], axis=1).astype(WIDE)
+        out_sum = sum_b[:, local:].astype(WIDE).T
+        result = middle + fold_end(shrunk, shrunk_one, shrunk_two) + shrink_bias.astype(WIDE)
+        result = result.astype(LOW)
+        first_grad = fold_end(first_low, first_one, first_two)
+
+        unit, scale = stats(block_input.astype(WIDE))
+        input_grad = middle_grad + norm_back(first_grad, gain_one, unit, scale)
         bias_slots = vectors[6:-2].reshape(n_t, wide)
         expand_bias_sum = lax.dynamic_index_in_dim(bias_slots, place, 0, keepdims=False)
         qv_slots = vectors[-2:].reshape(2, n_t, local)

time: 253 us -> 226 us (0.89)
  waiting for transfers between devices: 111 us -> 82.3 us
  starting transfers between devices: 50.9 us -> 45.1 us
  local copies, waits for them, and re-layouts: 18.5 us -> 22.4 us
    ppermute x34 -> x39, waiting for transfers between devices: 110 us -> 82.3 us  [send(): return lax.ppermute(value, AXES, pairs)]
    ppermute x34 -> x39, starting transfers between devices: 50.8 us -> 45.1 us  [send(): return lax.ppermute(value, AXES, pairs)]
    unnamed x113 -> x96, local copies, waits for them, and re-layouts: 10.4 us -> 15 us
  transfers between devices with their start and end apart: 37 -> 41, of which waited for: 26 -> 22; matrix products, arithmetic and copies ran while one was open for 11% -> 14% of each run, Pallas kernels for 10% -> 12%
where the time goes in v3:
time: 226 us; the launch traced here: 225 us
  waiting for transfers between devices  82.3 us (36%)
  starting transfers between devices  45.1 us (20%)
  Pallas kernels  34.9 us (15%)
  local copies, waits for them, and re-layouts  22.4 us (10%)
  other arithmetic  20.8 us (9%)
  between operations  15 us (7%)
  matrix products  4.22 us (2%)
    ppermute x39, waiting for transfers between devices, send(): return lax.ppermute(value, AXES, pairs)  82.3 us
    ppermute x39, starting transfers between devices, send(): return lax.ppermute(value, AXES, pairs)  45.1 us
    pallas_call x3, Pallas kernels, call_kernel(): pl.pallas_call(kernel, grid=(1,), in_specs=[pl.BlockSpec(memory_space=plt...  26.5 us
    unnamed x96, local copies, waits for them, and re-layouts  15 us
    pallas_call x2, Pallas kernels, weight_grads(): pl.pallas_call(functools.partial(grads_kernel, steps, len(blocks)), grid=...  8.43 us
  transfers between devices with their start and end apart: 41, of which 22 were waited for; matrix products, arithmetic and copies ran while one was open for 14% of the time, Pallas kernels for 12%

profile of v3, /device:TPU:0, one launch (start us, length us, event | category | flops | bytes accessed | tf_op | source)
XLA Modules:
  0.0 224.8 jit_solution(3942966666465365186)
XLA Ops:
  7.2 3.1 %collective-permute-start.2 = (bf16[128,1024]{1,0:T(8,128)(2,1)}, bf16[128,1024]{1,0:T(8,128)(2,1)S(1)}, u32[]{:S(2)}, u32[]{:S(2)}) collective-permute-start(bf16[128,1024]{1,0:T(8,128)(2,1)} %refs_9_.1), channel_id=1, source_target_pairs={{0,1},{1,0},{2,3},{3,2},{4,5},{5,4},{6,7},{7,6},{8,9},{9,8},{10,11... | collective-permute-start | bytes 786440 | tf_op jit(solution)/shard_map/rows_z1/ppermute | solution.py:289
  10.3 2.6 %collective-permute-start.3 = (bf16[128,1024]{1,0:T(8,128)(2,1)}, bf16[128,1024]{1,0:T(8,128)(2,1)S(1)}, u32[]{:S(2)}, u32[]{:S(2)}) collective-permute-start(bf16[128,1024]{1,0:T(8,128)(2,1)} %refs_9_.1), channel_id=1, source_target_pairs={{0,2},{1,3},{2,0},{3,1},{4,6},{5,7},{6,4},{7,5},{8,10},{9,11},{10,... | collective-permute-start | bytes 786440 | tf_op jit(solution)/shard_map/rows_z2/ppermute | solution.py:289
  22.3 2.5 %collective-permute-done.3.refs_8_.refs_11_ = bf16[128,1024]{1,0:T(8,128)(2,1)S(1)} collective-permute-done((bf16[128,1024]{1,0:T(8,128)(2,1)}, bf16[128,1024]{1,0:T(8,128)(2,1)S(1)}, u32[]{:S(2)}, u32[]{:S(2)}) %collective-permute-start.3) | collective-permute-done | bytes 262176 | tf_op jit(solution)/shard_map/rows_z2/ppermute | solution.py:289
  28.3 2.9 %collective-permute-done.4 = bf16[2,1,1,128,512]{3,4,2,1,0:T(8,128)(2,1)S(1)} collective-permute-done((bf16[2,1,1,128,512]{3,4,2,1,0:T(8,128)(2,1)S(1)}, bf16[2,1,1,128,512]{3,4,2,1,0:T(8,128)(2,1)S(1)}, u32[]{:S(2)}, u32[]{:S(2)}) %collective-permute-start.4) | collective-permute-done | bytes 262176 | tf_op jit(solution)/shard_map/att_a_d2/ppermute | solution.py:289
  36.9 2.4 %collective-permute-start.10 = (bf16[128,1024]{1,0:T(8,128)(2,1)S(1)}, bf16[128,1024]{1,0:T(8,128)(2,1)S(1)}, u32[]{:S(2)}, u32[]{:S(2)}) collective-permute-start(bf16[128,1024]{1,0:T(8,128)(2,1)S(1)} %copy-done.5), channel_id=1, source_target_pairs={{0,2},{1,3},{2,0},{3,1},{4,6},{5,7},{6,4},{7,5},{8,10},{9,11},{10,... | collective-permute-start | bytes 786440 | tf_op jit(solution)/shard_map/tops_z2/ppermute | solution.py:289
  42.1 6.6 %shard_map.245 = (bf16[512,1024]{1,0:T(8,128)(2,1)S(1)}, bf16[512,768]{1,0:T(8,128)(2,1)S(1)}, bf16[512,256]{1,0:T(8,128)(2,1)S(1)}, f32[4,512]{1,0:T(4,128)S(1)...) custom-call(f32[4]{0:T(128)S(1)} %multiply_exponential_fusion.refs_0, ...), custom_call_target="tpu_custom_call" | custom-call | flops 1342177280 | bytes 6573056 | tf_op jit(solution)/shard_map/pallas_call | solution.py:202
  52.0 1.9 collective-permute-start.8
  53.9 7.2 %collective-permute-done.11 = bf16[128,1024]{1,0:T(8,128)(2,1)S(1)} collective-permute-done((bf16[128,1024]{1,0:T(8,128)(2,1)S(1)}, bf16[128,1024]{1,0:T(8,128)(2,1)S(1)}, u32[]{:S(2)}, u32[]{:S(2)}) %collective-permute-start.11) | collective-permute-done | bytes 262176 | tf_op jit(solution)/shard_map/branch_far_z1/ppermute | solution.py:289
  62.1 5.3 %collective-permute-done.8 = bf16[128,1024]{1,0:T(8,128)(2,1)S(1)} collective-permute-done((bf16[128,1024]{1,0:T(8,128)(2,1)S(1)}, bf16[128,1024]{1,0:T(8,128)(2,1)S(1)}, u32[]{:S(2)}, u32[]{:S(2)}) %collective-permute-start.8) | collective-permute-done | bytes 262176 | tf_op jit(solution)/shard_map/branch_z1/ppermute | solution.py:289
  67.4 6.3 %collective-permute-done.12 = bf16[128,1024]{1,0:T(8,128)(2,1)S(1)} collective-permute-done((bf16[128,1024]{1,0:T(8,128)(2,1)S(1)}, bf16[128,1024]{1,0:T(8,128)(2,1)S(1)}, u32[]{:S(2)}, u32[]{:S(2)}) %collective-permute-start.12) | collective-permute-done | bytes 262176 | tf_op jit(solution)/shard_map/branch_z2/ppermute | solution.py:289
  75.6 2.7 %collective-permute-start.13 = (bf16[128,1024]{1,0:T(8,128)(2,1)S(1)}, bf16[128,1024]{1,0:T(8,128)(2,1)S(1)}, u32[]{:S(2)}, u32[]{:S(2)}) collective-permute-start(bf16[128,1024]{1,0:T(8,128)(2,1)S(1)} %add_convert_fusion.6.refs_0_), channel_id=1, source_target_pairs={{0,1},{1,0},{2,3},{3,2},{4,5},{5,4},{6,7},{7,6},{8,9},{9,8},{10,11... | collective-permute-start | bytes 786440 | tf_op jit(solution)/shard_map/second_z1/ppermute | solution.py:289
  78.3 8.0 %collective-permute-done.14.refs_6_.refs_2_ = bf16[128,1024]{1,0:T(8,128)(2,1)S(1)} collective-permute-done((bf16[128,1024]{1,0:T(8,128)(2,1)S(1)}, bf16[128,1024]{1,0:T(8,128)(2,1)S(1)}, u32[]{:S(2)}, u32[]{:S(2)}) %collective-permute-start.14) | collective-permute-done | bytes 262176 | tf_op jit(solution)/shard_map/second_z2/ppermute | solution.py:289
  86.8 2.6 %collective-permute-done.13.refs_4_.refs_1_ = bf16[128,1024]{1,0:T(8,128)(2,1)S(1)} collective-permute-done((bf16[128,1024]{1,0:T(8,128)(2,1)S(1)}, bf16[128,1024]{1,0:T(8,128)(2,1)S(1)}, u32[]{:S(2)}, u32[]{:S(2)}) %collective-permute-start.13) | collective-permute-done | bytes 262176 | tf_op jit(solution)/shard_map/second_z1/ppermute | solution.py:289
  89.4 5.5 %collective-permute-done.16.refs_9_.refs_8_ = bf16[128,1024]{1,0:T(8,128)(2,1)S(1)} collective-permute-done((bf16[128,1024]{1,0:T(8,128)(2,1)S(1)}, bf16[128,1024]{1,0:T(8,128)(2,1)S(1)}, u32[]{:S(2)}, u32[]{:S(2)}) %collective-permute-start.16) | collective-permute-done | bytes 262176 | tf_op jit(solution)/shard_map/tops_far_z1/ppermute | solution.py:289
  94.9 2.8 %collective-permute-done.15.refs_8_.refs_3_ = bf16[128,1024]{1,0:T(8,128)(2,1)S(1)} collective-permute-done((bf16[128,1024]{1,0:T(8,128)(2,1)S(1)}, bf16[128,1024]{1,0:T(8,128)(2,1)S(1)}, u32[]{:S(2)}, u32[]{:S(2)}) %collective-permute-start.15) | collective-permute-done | bytes 262176 | tf_op jit(solution)/shard_map/second_far_z1/ppermute | solution.py:289
  97.7 2.2 copy-done.6
  99.9 8.2 %shard_map.246 = (bf16[512,1024]{1,0:T(8,128)(2,1)S(1)}, bf16[512,1024]{1,0:T(8,128)(2,1)S(1)}, f32[128,1024]{1,0:T(8,128)S(1)}, bf16[128,1024]{1,0:T(8,128)(2,1...) custom-call(bf16[128,1024]{1,0:T(8,128)(2,1)S(1)} %add_convert_fusion.6.refs_0_, ...), custom_call_target="tpu_custom_call" | custom-call | flops 3221225472 | bytes 9707520 | tf_op jit(solution)/shard_map/pallas_call | solution.py:202
  112.1 8.3 %collective-permute-done.18 = bf16[128,1024]{1,0:T(8,128)(2,1)} collective-permute-done((bf16[128,1024]{1,0:T(8,128)(2,1)S(1)}, bf16[128,1024]{1,0:T(8,128)(2,1)}, u32[]{:S(2)}, u32[]{:S(2)}) %collective-permute-start.18) | collective-permute-done | bytes 262176 | tf_op jit(solution)/shard_map/second_grad_far_z1/ppermute | solution.py:289
  124.5 5.5 %shard_map.247 = (bf16[1024,1024]{1,0:T(8,128)(2,1)S(1)}, bf16[1024,1024]{1,0:T(8,128)(2,1)S(1)}) custom-call(bf16[128,1024]{1,0:T(8,128)(2,1)S(1)} %add_convert_fusion.6.refs_0_, bf16[128,1024]{1,0:T(8,128)(2,1)S(1)} %collective-permute-done.13.refs_4_.refs_1_, bf16[128,1024]{1,0:T(8,128)(2,1)S(1)} %collective-permute-done.14.refs_6_.refs_2_, ...), custom_call_target="tpu_custom_call" | custom-call | flops 2147483648 | bytes 6291456 | tf_op jit(solution)/shard_map/pallas_call | solution.py:256
  130.0 6.7 %collective-permute-done.19 = bf16[128,1024]{1,0:T(8,128)(2,1)S(1)} collective-permute-done((bf16[128,1024]{1,0:T(8,128)(2,1)S(1)}, bf16[128,1024]{1,0:T(8,128)(2,1)S(1)}, u32[]{:S(2)}, u32[]{:S(2)}) %collective-permute-start.19) | collective-permute-done | bytes 262176 | tf_op jit(solution)/shard_map/second_grad_z2/ppermute | solution.py:289
  139.3 2.4 %pad_maximum_fusion = bf16[1024,2048]{1,0:T(8,128)(2,1)} fusion(bf16[1024,1024]{1,0:T(8,128)(2,1)S(1)} %get-tuple-element.171, bf16[1024,1024]{1,0:T(8,128)(2,1)S(1)} %get-tuple-element.170), kind=kLoop, calls=%fused_computation | loop fusion | flops 8388608 | bytes 8388608 | tf_op jit(solution)/shard_map/concatenate | solution.py:506
  141.7 6.2 %collective-permute-done.20.refs_4_.refs_3_ = bf16[128,1024]{1,0:T(8,128)(2,1)S(1)} collective-permute-done((bf16[128,1024]{1,0:T(8,128)(2,1)S(1)}, bf16[128,1024]{1,0:T(8,128)(2,1)S(1)}, u32[]{:S(2)}, u32[]{:S(2)}) %collective-permute-start.20) | collective-permute-done | bytes 262176 | tf_op jit(solution)/shard_map/middle_z1/ppermute | solution.py:289
  148.3 4.2 %fusion.28 = (bf16[512,1024]{1,0:T(8,128)(2,1)S(1)}, f32[512,1024]{1,0:T(8,128)}) fusion(bf16[512,1024]{1,0:T(8,128)(2,1)S(1)} %copy-done.26, bf16[1024,2048]{1,0:T(8,128)(2,1)} %all-gather.2.cloned.1.call-done.refs_1_), kind=kOutput, calls=%fused_computation.97 | convolution fusion | flops 1074266112 | bytes 6291456 | tf_op jit(solution)/shard_map/sf,df->sd/dot_general | solution.py:515
  155.2 11.7 %shard_map.248 = (bf16[512,768]{1,0:T(8,128)(2,1)}, f32[128,1024]{1,0:T(8,128)}, bf16[128,1024]{1,0:T(8,128)(2,1)}, bf16[128,1024]{1,0:T(8,128)(2,1)}, bf16[128,...) custom-call(f32[4]{0:T(128)} %copy-done.17, s32[4]{0:T(128)} %copy-done.16, bf16[128,1024]{1,0:T(8,128)(2,1)} %copy-done.3, ...), custom_call_target="tpu_custom_call" | custom-call | flops 1744830464 | bytes 7097344 | tf_op jit(solution)/shard_map/pallas_call | solution.py:202
  175.5 2.9 %shard_map.249 = (bf16[1024,768]{1,0:T(8,128)(2,1)S(1)}, bf16[1024,256]{1,0:T(8,128)(2,1)S(1)}) custom-call(bf16[512,1024]{1,0:T(8,128)(2,1)S(1)} %copy-done.19, bf16[512,768]{1,0:T(8,128)(2,1)S(1)} %copy-done.20, bf16[128,1024]{1,0:T(8,128)(2,1)S(1)} %copy-done.4, bf16[128,1024]{1,0:T(8,128)(2,1)S(1)} %copy-done.11, bf16[128,1024]{1,0:T(8,128)(2,1)S(1)} %copy-done.13, ...), custom_call_target="tpu_custom_call" | custom-call | flops 1073741824 | bytes 4194304 | tf_op jit(solution)/shard_map/pallas_call | solution.py:256
  182.8 2.0 collective-permute-start.32
  187.8 3.3 %collective-permute-start.30 = (bf16[2,1,128,512]{2,3,1,0:T(8,128)(2,1)S(1)}, bf16[2,1,128,512]{2,3,1,0:T(8,128)(2,1)S(1)}, u32[]{:S(2)}, u32[]{:S(2)}) collective-permute-start(bf16[2,1,128,512]{2,3,1,0:T(8,128)(2,1)S(1)} %constant_dynamic-slice_fusion.5), channel_id=1, source_target_pairs={{0,8},{1,9},{2,10},{3,11},{4,12},{5,13},{6,14},{7,15},{8,0},{9,1},... | collective-permute-start | bytes 786440 | tf_op jit(solution)/shard_map/att_grad_a_d2/ppermute | solution.py:289
  192.9 1.9 fusion.17
  194.8 4.8 %collective-permute-done.34 = f32[12,1024]{1,0:T(8,128)S(1)} collective-permute-done((f32[12,1024]{1,0:T(8,128)S(1)}, f32[12,1024]{1,0:T(8,128)S(1)}, u32[]{:S(2)}, u32[]{:S(2)}) %collective-permute-start.34) | collective-permute-done | bytes 49184 | tf_op jit(solution)/shard_map/vectors_d2/ppermute | solution.py:289
  199.9 2.5 %collective-permute-start.35 = (f32[12,1024]{1,0:T(8,128)S(1)}, f32[12,1024]{1,0:T(8,128)S(1)}, u32[]{:S(2)}, u32[]{:S(2)}) collective-permute-start(f32[12,1024]{1,0:T(8,128)S(1)} %add.212), channel_id=1, source_target_pairs={{0,16},{1,17},{2,18},{3,19},{4,20},{5,21},{6,22},{7,23},{8,24},{9,... | collective-permute-start | bytes 147464 | tf_op jit(solution)/shard_map/vectors_d4/ppermute | solution.py:289
  203.8 2.3 %collective-permute-start.38 = (bf16[1,1,128,512]{2,3,1,0:T(8,128)(2,1)S(1)}, bf16[1,1,128,512]{2,3,1,0:T(8,128)(2,1)S(1)}, u32[]{:S(2)}, u32[]{:S(2)}) collective-permute-start(bf16[1,1,128,512]{2,3,1,0:T(8,128)(2,1)S(1)} %constant_dynamic-slice_fusion.2), channel_id=1, source_target_pairs={{0,8},{1,9},{2,10},{3,11},{4,12},{5,13},{6,14},{7,15},{8,0},{9,1},... | collective-permute-start | bytes 393224 | tf_op jit(solution)/shard_map/att_grad_b_d2/ppermute | solution.py:289
  207.7 3.6 %collective-permute-done.36 = f32[12,1024]{1,0:T(8,128)S(1)} collective-permute-done((f32[12,1024]{1,0:T(8,128)S(1)}, f32[12,1024]{1,0:T(8,128)S(1)}, u32[]{:S(2)}, u32[]{:S(2)}) %collective-permute-start.36) | collective-permute-done | bytes 49184 | tf_op jit(solution)/shard_map/vectors_z2/ppermute | solution.py:289
  (244 shorter events, 68.6 us)
Async XLA Ops:
  7.2 66.6 %all-gather.2.cloned.1.call-start = ((), (), s32[]{:S(2)}) async-start(), calls=%async_computation.1 | async-start | bytes 4718592 | tf_op jit(solution)/shard_map/all_gather | solution.py:453
  7.2 15.1 %collective-permute-start.2 = (bf16[128,1024]{1,0:T(8,128)(2,1)}, bf16[128,1024]{1,0:T(8,128)(2,1)S(1)}, u32[]{:S(2)}, u32[]{:S(2)}) collective-permute-start(bf16[128,1024]{1,0:T(8,128)(2,1)} %refs_9_.1), channel_id=1, source_target_pairs={{0,1},{1,0},{2,3},{3,2},{4,5},{5,4},{6,7},{7,6},{8,9},{9,8},{10,11... | collective-permute-start | bytes 786440 | tf_op jit(solution)/shard_map/rows_z1/ppermute | solution.py:289
  10.3 14.6 %collective-permute-start.3 = (bf16[128,1024]{1,0:T(8,128)(2,1)}, bf16[128,1024]{1,0:T(8,128)(2,1)S(1)}, u32[]{:S(2)}, u32[]{:S(2)}) collective-permute-start(bf16[128,1024]{1,0:T(8,128)(2,1)} %refs_9_.1), channel_id=1, source_target_pairs={{0,2},{1,3},{2,0},{3,1},{4,6},{5,7},{6,4},{7,5},{8,10},{9,11},{10,... | collective-permute-start | bytes 786440 | tf_op jit(solution)/shard_map/rows_z2/ppermute | solution.py:289
  14.0 6.9 %collective-permute-start = (bf16[1,1,1,128,512]{3,4,2,1,0:T(8,128)(2,1)S(1)}, bf16[1,1,1,128,512]{3,4,2,1,0:T(8,128)(2,1)S(1)}, u32[]{:S(2)}, u32[]{:S(2)}) collective-permute-start(bf16[1,1,1,128,512]{3,4,2,1,0:T(8,128)(2,1)S(1)} %slice_bitcast_fusion.1), channel_id=1, source_target_pairs={{0,16},{1,17},{2,18},{3,19},{4,20},{5,21},{6,22},{7,23},{8,24},{9,... | collective-permute-start | bytes 393224 | tf_op jit(solution)/shard_map/att_a_d4/ppermute | solution.py:289
  34.3 180.6 %reduce-scatter.2.cloned.1.call-start = ((), (), s32[]{:S(2)}) async-start(), calls=%async_computation.2 | async-start | bytes 4718592 | tf_op jit(solution)/shard_map/reduce_scatter | solution.py:507
  36.2 13.9 %collective-permute-start.9 = (bf16[128,1024]{1,0:T(8,128)(2,1)S(1)}, bf16[128,1024]{1,0:T(8,128)(2,1)S(1)}, u32[]{:S(2)}, u32[]{:S(2)}) collective-permute-start(bf16[128,1024]{1,0:T(8,128)(2,1)S(1)} %copy-done.5), channel_id=1, source_target_pairs={{0,1},{1,0},{2,3},{3,2},{4,5},{5,4},{6,7},{7,6},{8,9},{9,8},{10,11... | collective-permute-start | bytes 786440 | tf_op jit(solution)/shard_map/tops_z1/ppermute | solution.py:289
  36.9 15.0 %collective-permute-start.10 = (bf16[128,1024]{1,0:T(8,128)(2,1)S(1)}, bf16[128,1024]{1,0:T(8,128)(2,1)S(1)}, u32[]{:S(2)}, u32[]{:S(2)}) collective-permute-start(bf16[128,1024]{1,0:T(8,128)(2,1)S(1)} %copy-done.5), channel_id=1, source_target_pairs={{0,2},{1,3},{2,0},{3,1},{4,6},{5,7},{6,4},{7,5},{8,10},{9,11},{10,... | collective-permute-start | bytes 786440 | tf_op jit(solution)/shard_map/tops_z2/ppermute | solution.py:289
  51.9 9.3 %collective-permute-start.11 = (bf16[128,1024]{1,0:T(8,128)(2,1)S(1)}, bf16[128,1024]{1,0:T(8,128)(2,1)S(1)}, u32[]{:S(2)}, u32[]{:S(2)}) collective-permute-start(bf16[128,1024]{1,0:T(8,128)(2,1)S(1)} %get-tuple-element.108), channel_id=1, source_target_pairs={{0,1},{1,0},{2,3},{3,2},{4,5},{5,4},{6,7},{7,6},{8,9},{9,8},{10,11... | collective-permute-start | bytes 786440 | tf_op jit(solution)/shard_map/branch_far_z1/ppermute | solution.py:289
  52.0 15.4 %collective-permute-start.8 = (bf16[128,1024]{1,0:T(8,128)(2,1)S(1)}, bf16[128,1024]{1,0:T(8,128)(2,1)S(1)}, u32[]{:S(2)}, u32[]{:S(2)}) collective-permute-start(bf16[128,1024]{1,0:T(8,128)(2,1)S(1)} %get-tuple-element.104), channel_id=1, source_target_pairs={{0,1},{1,0},{2,3},{3,2},{4,5},{5,4},{6,7},{7,6},{8,9},{9,8},{10,11... | collective-permute-start | bytes 786440 | tf_op jit(solution)/shard_map/branch_z1/ppermute | solution.py:289
  61.2 12.5 %collective-permute-start.12 = (bf16[128,1024]{1,0:T(8,128)(2,1)S(1)}, bf16[128,1024]{1,0:T(8,128)(2,1)S(1)}, u32[]{:S(2)}, u32[]{:S(2)}) collective-permute-start(bf16[128,1024]{1,0:T(8,128)(2,1)S(1)} %add_convert_fusion.7), channel_id=1, source_target_pairs={{0,2},{1,3},{2,0},{3,1},{4,6},{5,7},{6,4},{7,5},{8,10},{9,11},{10,... | collective-permute-start | bytes 786440 | tf_op jit(solution)/shard_map/branch_z2/ppermute | solution.py:289
  75.6 10.8 %collective-permute-start.14 = (bf16[128,1024]{1,0:T(8,128)(2,1)S(1)}, bf16[128,1024]{1,0:T(8,128)(2,1)S(1)}, u32[]{:S(2)}, u32[]{:S(2)}) collective-permute-start(bf16[128,1024]{1,0:T(8,128)(2,1)S(1)} %add_convert_fusion.6.refs_0_), channel_id=1, source_target_pairs={{0,2},{1,3},{2,0},{3,1},{4,6},{5,7},{6,4},{7,5},{8,10},{9,11},{10,... | collective-permute-start | bytes 786440 | tf_op jit(solution)/shard_map/second_z2/ppermute | solution.py:289
  75.6 13.8 %collective-permute-start.13 = (bf16[128,1024]{1,0:T(8,128)(2,1)S(1)}, bf16[128,1024]{1,0:T(8,128)(2,1)S(1)}, u32[]{:S(2)}, u32[]{:S(2)}) collective-permute-start(bf16[128,1024]{1,0:T(8,128)(2,1)S(1)} %add_convert_fusion.6.refs_0_), channel_id=1, source_target_pairs={{0,1},{1,0},{2,3},{3,2},{4,5},{5,4},{6,7},{7,6},{8,9},{9,8},{10,11... | collective-permute-start | bytes 786440 | tf_op jit(solution)/shard_map/second_z1/ppermute | solution.py:289
  78.3 16.6 %collective-permute-start.16 = (bf16[128,1024]{1,0:T(8,128)(2,1)S(1)}, bf16[128,1024]{1,0:T(8,128)(2,1)S(1)}, u32[]{:S(2)}, u32[]{:S(2)}) collective-permute-start(bf16[128,1024]{1,0:T(8,128)(2,1)S(1)} %collective-permute-done.10.refs_7_), channel_id=1, source_target_pairs={{0,1},{1,0},{2,3},{3,2},{4,5},{5,4},{6,7},{7,6},{8,9},{9,8},{10,11... | collective-permute-start | bytes 786440 | tf_op jit(solution)/shard_map/tops_far_z1/ppermute | solution.py:289
  86.3 11.4 %collective-permute-start.15 = (bf16[128,1024]{1,0:T(8,128)(2,1)S(1)}, bf16[128,1024]{1,0:T(8,128)(2,1)S(1)}, u32[]{:S(2)}, u32[]{:S(2)}) collective-permute-start(bf16[128,1024]{1,0:T(8,128)(2,1)S(1)} %collective-permute-done.14.refs_6_.refs_2_), channel_id=1, source_target_pairs={{0,1},{1,0},{2,3},{3,2},{4,5},{5,4},{6,7},{7,6},{8,9},{9,8},{10,11... | collective-permute-start | bytes 786440 | tf_op jit(solution)/shard_map/second_far_z1/ppermute | solution.py:289
  110.0 10.4 %collective-permute-start.18 = (bf16[128,1024]{1,0:T(8,128)(2,1)S(1)}, bf16[128,1024]{1,0:T(8,128)(2,1)}, u32[]{:S(2)}, u32[]{:S(2)}) collective-permute-start(bf16[128,1024]{1,0:T(8,128)(2,1)S(1)} %get-tuple-element.119), channel_id=1, source_target_pairs={{0,1},{1,0},{2,3},{3,2},{4,5},{5,4},{6,7},{7,6},{8,9},{9,8},{10,11... | collective-permute-start | bytes 786440 | tf_op jit(solution)/shard_map/second_grad_far_z1/ppermute | solution.py:289
  111.5 18.6 %collective-permute-start.17 = (bf16[128,1024]{1,0:T(8,128)(2,1)S(1)}, bf16[128,1024]{1,0:T(8,128)(2,1)S(1)}, u32[]{:S(2)}, u32[]{:S(2)}) collective-permute-start(bf16[128,1024]{1,0:T(8,128)(2,1)S(1)} %get-tuple-element.117), channel_id=1, source_target_pairs={{0,1},{1,0},{2,3},{3,2},{4,5},{5,4},{6,7},{7,6},{8,9},{9,8},{10,11... | collective-permute-start | bytes 786440 | tf_op jit(solution)/shard_map/second_grad_z1/ppermute | solution.py:289
  121.4 15.3 %collective-permute-start.19 = (bf16[128,1024]{1,0:T(8,128)(2,1)S(1)}, bf16[128,1024]{1,0:T(8,128)(2,1)S(1)}, u32[]{:S(2)}, u32[]{:S(2)}) collective-permute-start(bf16[128,1024]{1,0:T(8,128)(2,1)S(1)} %add_convert_fusion.5), channel_id=1, source_target_pairs={{0,2},{1,3},{2,0},{3,1},{4,6},{5,7},{6,4},{7,5},{8,10},{9,11},{10,... | collective-permute-start | bytes 786440 | tf_op jit(solution)/shard_map/second_grad_z2/ppermute | solution.py:289
  137.4 10.4 %collective-permute-start.20 = (bf16[128,1024]{1,0:T(8,128)(2,1)S(1)}, bf16[128,1024]{1,0:T(8,128)(2,1)S(1)}, u32[]{:S(2)}, u32[]{:S(2)}) collective-permute-start(bf16[128,1024]{1,0:T(8,128)(2,1)S(1)} %convert_element_type.180.refs_2_), channel_id=1, source_target_pairs={{0,1},{1,0},{2,3},{3,2},{4,5},{5,4},{6,7},{7,6},{8,9},{9,8},{10,11... | collective-permute-start | bytes 786440 | tf_op jit(solution)/shard_map/middle_z1/ppermute | solution.py:289
  137.5 10.4 %collective-permute-start.21 = (bf16[128,1024]{1,0:T(8,128)(2,1)S(1)}, bf16[128,1024]{1,0:T(8,128)(2,1)S(1)}, u32[]{:S(2)}, u32[]{:S(2)}) collective-permute-start(bf16[128,1024]{1,0:T(8,128)(2,1)S(1)} %convert_element_type.180.refs_2_), channel_id=1, source_target_pairs={{0,2},{1,3},{2,0},{3,1},{4,6},{5,7},{6,4},{7,5},{8,10},{9,11},{10,... | collective-permute-start | bytes 786440 | tf_op jit(solution)/shard_map/middle_z2/ppermute | solution.py:289
  147.9 6.6 %collective-permute-start.22 = (bf16[128,1024]{1,0:T(8,128)(2,1)S(1)}, bf16[128,1024]{1,0:T(8,128)(2,1)S(1)}, u32[]{:S(2)}, u32[]{:S(2)}) collective-permute-start(bf16[128,1024]{1,0:T(8,128)(2,1)S(1)} %collective-permute-done.21.refs_5_.refs_4_), channel_id=1, source_target_pairs={{0,1},{1,0},{2,3},{3,2},{4,5},{5,4},{6,7},{7,6},{8,9},{9,8},{10,11... | collective-permute-start | bytes 786440 | tf_op jit(solution)/shard_map/middle_far_z1/ppermute | solution.py:289
  154.5 14.0 %collective-permute-start.23 = (bf16[128,1024]{1,0:T(8,128)(2,1)S(1)}, bf16[128,1024]{1,0:T(8,128)(2,1)S(1)}, u32[]{:S(2)}, u32[]{:S(2)}) collective-permute-start(bf16[128,1024]{1,0:T(8,128)(2,1)S(1)} %get-tuple-element.138), channel_id=1, source_target_pairs={{0,1},{1,0},{2,3},{3,2},{4,5},{5,4},{6,7},{7,6},{8,9},{9,8},{10,11... | collective-permute-start | bytes 786440 | tf_op jit(solution)/shard_map/shrunk_far_z1/ppermute | solution.py:289
  168.6 11.2 %collective-permute-start.24 = (bf16[128,1024]{1,0:T(8,128)(2,1)}, bf16[128,1024]{1,0:T(8,128)(2,1)S(1)}, u32[]{:S(2)}, u32[]{:S(2)}) collective-permute-start(bf16[128,1024]{1,0:T(8,128)(2,1)} %get-tuple-element.144), channel_id=1, source_target_pairs={{0,1},{1,0},{2,3},{3,2},{4,5},{5,4},{6,7},{7,6},{8,9},{9,8},{10,11... | collective-permute-start | bytes 786440 | tf_op jit(solution)/shard_map/first_grad_far_z1/ppermute | solution.py:289
  170.0 9.8 %collective-permute-start.25 = (f32[12,1024]{1,0:T(8,128)S(1)}, f32[12,1024]{1,0:T(8,128)S(1)}, u32[]{:S(2)}, u32[]{:S(2)}) collective-permute-start(f32[12,1024]{1,0:T(8,128)S(1)} %concatenate.44), channel_id=1, source_target_pairs={{0,1},{1,0},{2,3},{3,2},{4,5},{5,4},{6,7},{7,6},{8,9},{9,8},{10,11... | collective-permute-start | bytes 147464 | tf_op jit(solution)/shard_map/vectors_z1/ppermute | solution.py:289
  170.7 10.9 %collective-permute-start.26 = (bf16[128,1024]{1,0:T(8,128)(2,1)}, bf16[128,1024]{1,0:T(8,128)(2,1)S(1)}, u32[]{:S(2)}, u32[]{:S(2)}) collective-permute-start(bf16[128,1024]{1,0:T(8,128)(2,1)} %get-tuple-element.151), channel_id=1, source_target_pairs={{0,1},{1,0},{2,3},{3,2},{4,5},{5,4},{6,7},{7,6},{8,9},{9,8},{10,11... | collective-permute-start | bytes 786440 | tf_op jit(solution)/shard_map/shrunk_z1/ppermute | solution.py:289
  172.1 9.5 %collective-permute-start.27 = (bf16[128,1024]{1,0:T(8,128)(2,1)S(1)}, bf16[128,1024]{1,0:T(8,128)(2,1)S(1)}, u32[]{:S(2)}, u32[]{:S(2)}) collective-permute-start(bf16[128,1024]{1,0:T(8,128)(2,1)S(1)} %add_convert_fusion.4), channel_id=1, source_target_pairs={{0,2},{1,3},{2,0},{3,1},{4,6},{5,7},{6,4},{7,5},{8,10},{9,11},{10,... | collective-permute-start | bytes 786440 | tf_op jit(solution)/shard_map/shrunk_z2/ppermute | solution.py:289
  182.8 17.2 %collective-permute-start.32 = (bf16[128,1024]{1,0:T(8,128)(2,1)}, bf16[128,1024]{1,0:T(8,128)(2,1)}, u32[]{:S(2)}, u32[]{:S(2)}) collective-permute-start(bf16[128,1024]{1,0:T(8,128)(2,1)} %get-tuple-element.160), channel_id=1, source_target_pairs={{0,1},{1,0},{2,3},{3,2},{4,5},{5,4},{6,7},{7,6},{8,9},{9,8},{10,11... | collective-permute-start | bytes 786440 | tf_op jit(solution)/shard_map/first_grad_z1/ppermute | solution.py:289
  184.7 15.2 %collective-permute-start.33 = (bf16[128,1024]{1,0:T(8,128)(2,1)S(1)}, bf16[128,1024]{1,0:T(8,128)(2,1)}, u32[]{:S(2)}, u32[]{:S(2)}) collective-permute-start(bf16[128,1024]{1,0:T(8,128)(2,1)S(1)} %add_convert_fusion.3), channel_id=1, source_target_pairs={{0,2},{1,3},{2,0},{3,1},{4,6},{5,7},{6,4},{7,5},{8,10},{9,11},{10,... | collective-permute-start | bytes 786440 | tf_op jit(solution)/shard_map/first_grad_z2/ppermute | solution.py:289
  187.8 11.8 %collective-permute-start.30 = (bf16[2,1,128,512]{2,3,1,0:T(8,128)(2,1)S(1)}, bf16[2,1,128,512]{2,3,1,0:T(8,128)(2,1)S(1)}, u32[]{:S(2)}, u32[]{:S(2)}) collective-permute-start(bf16[2,1,128,512]{2,3,1,0:T(8,128)(2,1)S(1)} %constant_dynamic-slice_fusion.5), channel_id=1, source_target_pairs={{0,8},{1,9},{2,10},{3,11},{4,12},{5,13},{6,14},{7,15},{8,0},{9,1},... | collective-permute-start | bytes 786440 | tf_op jit(solution)/shard_map/att_grad_a_d2/ppermute | solution.py:289
  191.2 8.6 %collective-permute-start.31 = (bf16[1,2,128,512]{2,3,1,0:T(8,128)(2,1)S(1)}, bf16[1,2,128,512]{2,3,1,0:T(8,128)(2,1)S(1)}, u32[]{:S(2)}, u32[]{:S(2)}) collective-permute-start(bf16[1,2,128,512]{2,3,1,0:T(8,128)(2,1)S(1)} %constant_dynamic-slice_fusion.4), channel_id=1, source_target_pairs={{0,16},{1,17},{2,18},{3,19},{4,20},{5,21},{6,22},{7,23},{8,24},{9,... | collective-permute-start | bytes 786440 | tf_op jit(solution)/shard_map/att_grad_b_d4/ppermute | solution.py:289
  191.2 8.5 %collective-permute-start.34 = (f32[12,1024]{1,0:T(8,128)S(1)}, f32[12,1024]{1,0:T(8,128)S(1)}, u32[]{:S(2)}, u32[]{:S(2)}) collective-permute-start(f32[12,1024]{1,0:T(8,128)S(1)} %add.208), channel_id=1, source_target_pairs={{0,8},{1,9},{2,10},{3,11},{4,12},{5,13},{6,14},{7,15},{8,0},{9,1},... | collective-permute-start | bytes 147464 | tf_op jit(solution)/shard_map/vectors_d2/ppermute | solution.py:289
  203.8 9.4 %collective-permute-start.37 = (bf16[1,1,128,512]{2,3,1,0:T(8,128)(2,1)S(1)}, bf16[1,1,128,512]{2,3,1,0:T(8,128)(2,1)S(1)}, u32[]{:S(2)}, u32[]{:S(2)}) collective-permute-start(bf16[1,1,128,512]{2,3,1,0:T(8,128)(2,1)S(1)} %constant_dynamic-slice_fusion.3), channel_id=1, source_target_pairs={{0,16},{1,17},{2,18},{3,19},{4,20},{5,21},{6,22},{7,23},{8,24},{9,... | collective-permute-start | bytes 393224 | tf_op jit(solution)/shard_map/att_grad_a_d4/ppermute | solution.py:289
  203.8 9.4 %collective-permute-start.38 = (bf16[1,1,128,512]{2,3,1,0:T(8,128)(2,1)S(1)}, bf16[1,1,128,512]{2,3,1,0:T(8,128)(2,1)S(1)}, u32[]{:S(2)}, u32[]{:S(2)}) collective-permute-start(bf16[1,1,128,512]{2,3,1,0:T(8,128)(2,1)S(1)} %constant_dynamic-slice_fusion.2), channel_id=1, source_target_pairs={{0,8},{1,9},{2,10},{3,11},{4,12},{5,13},{6,14},{7,15},{8,0},{9,1},... | collective-permute-start | bytes 393224 | tf_op jit(solution)/shard_map/att_grad_b_d2/ppermute | solution.py:289
  (54 other events, 460.6 us)
Sparse Core Ops, SparseCore 0:
  34.4 34.9 all-gather.1
  141.8 52.9 reduce-scatter.1

commit v4 on v3

--- a/solution.py
+++ b/solution.py
@@ -138,15 +138,13 @@
     vectors[1:2, :] = shift_sum
 
 
-def feed_kernel(
-    row_a, weights, bias, top_a, row_b, top_b, row_c, top_c, row_d, top_d,
-    active, back, part_a, part_b, part_c, part_d, sums,
-):
-    rows = row_a.shape[0]
+def feed_kernel(count, row, weights, bias, top, *refs):
+    blocks = [(row, top)] + [(refs[2 * k], refs[2 * k + 1]) for k in range(count - 1)]
+    active, back, *parts, sums = refs[2 * count - 2 :]
+    rows = row.shape[0]
     wide = active.shape[1]
     total = jnp.zeros((1, wide), WIDE)
-    ins = ((row_a, top_a, part_a), (row_b, top_b, part_b), (row_c, top_c, part_c), (row_d, top_d, part_d))
-    for k, (row, top, part) in enumerate(ins):
+    for k, ((row, top), part) in enumerate(zip(blocks, parts)):
         here = pl.ds(k * rows, rows)
         hidden = jnp.dot(row[...], weights[:, :wide], preferred_element_type=WIDE) + bias[...]
         square = hidden * hidden
@@ -214,9 +212,10 @@
     )(*scalars, *arrays)
 
 
-def grads_kernel(steps, count, *refs):
-    blocks, others = refs[:count], refs[count + 1 : -4]
-    y_ref, v_ref, out_ref, more_ref, turned = refs[count], *refs[-4:]
+def grads_kernel(steps, counts, *refs):
+    refs = list(refs)
+    blocks, ys, others, vs = [[refs.pop(0) for _ in range(count)] for count in counts]
+    out_ref, more_ref, turned = refs
     step = pl.program_id(0)
 
     def turn(pieces):
@@ -226,6 +225,16 @@
             turned[:, first : first + size] = piece[...].T
             first += size
 
+    def product(pieces):
+        total, first = 0.0, 0
+        for piece in pieces:
+            size = piece.shape[0]
+            total = total + jnp.dot(
+                turned[:, first : first + size], piece[...], preferred_element_type=WIDE
+            )
+            first += size
+        return total.astype(LOW)
+
     @pl.when(step == 0)
     def _():
         turn(blocks)
@@ -236,35 +245,37 @@
 
     @pl.when(step < steps)
     def _():
-        out = jnp.dot(turned[...], y_ref[...], preferred_element_type=WIDE)
-        out_ref[...] = out.astype(LOW)
+        out_ref[...] = product(ys)
 
     @pl.when(step >= steps)
     def _():
-        out = jnp.dot(turned[...], v_ref[...], preferred_element_type=WIDE)
-        more_ref[...] = out.astype(LOW)
-
-
-def weight_grads(blocks, y, others, v):
-    tokens, width = y.shape[0], blocks[0].shape[1]
+        more_ref[...] = product(vs)
+
+
+def weight_grads(blocks, ys, others, vs):
+    tokens, width = sum(block.shape[0] for block in blocks), blocks[0].shape[1]
     columns = 256
-    steps, more = y.shape[1] // columns, v.shape[1] // columns
+    steps, more = ys[0].shape[1] // columns, vs[0].shape[1] // columns
 
     def whole(block):
         return pl.BlockSpec(block.shape, lambda j: (0, 0))
 
+    def early(block):
+        return pl.BlockSpec((block.shape[0], columns), lambda j: (0, jnp.minimum(j, steps - 1)))
+
+    def late(block):
+        return pl.BlockSpec((block.shape[0], columns), lambda j: (0, jnp.maximum(j - steps, 0)))
+
+    groups = ((blocks, whole), (ys, early), (others, whole), (vs, late))
     return pl.pallas_call(
-        functools.partial(grads_kernel, steps, len(blocks)),
+        functools.partial(grads_kernel, steps, [len(group) for group, _ in groups]),
         grid=(steps + more,),
-        in_specs=[whole(block) for block in blocks]
-        + [pl.BlockSpec((tokens, columns), lambda j: (0, jnp.minimum(j, steps - 1)))]
-        + [whole(block) for block in others]
-        + [pl.BlockSpec((tokens, columns), lambda j: (0, jnp.maximum(j - steps, 0)))],
+        in_specs=[spec(block) for group, spec in groups for block in group],
         out_specs=[
             pl.BlockSpec((width, columns), lambda j: (0, jnp.minimum(j, steps - 1))),
             pl.BlockSpec((width, columns), lambda j: (0, jnp.maximum(j - steps, 0))),
         ],
-        out_shape=[jax.ShapeDtypeStruct((width, z.shape[1]), LOW) for z in (y, v)],
+        out_shape=[jax.ShapeDtypeStruct((width, z[0].shape[1]), LOW) for z in (ys, vs)],
         scratch_shapes=[pltpu.VMEM((width, tokens), LOW)],
         compiler_params=pltpu.CompilerParams(vmem_limit_bytes=24 << 20),
         cost_estimate=pl.CostEstimate(
@@ -272,7 +283,7 @@
             bytes_accessed=2 * width * (2 * tokens + columns * (steps + more)),
             transcendentals=0,
         ),
-    )(*blocks, y, *others, v)
+    )(*blocks, *ys, *others, *vs)
 
 
 def make_body(n_dp, n_t):
@@ -485,22 +496,36 @@
         unit_two, scale_two = stats(middle)
         second_low = (unit_two * gain_two + shift_two).astype(LOW)
         second_list = gather_z(second_low, "second")
-        active, hidden_grad, *second_parts, expand_bias_part = call_kernel(
-            feed_kernel,
-            [],
-            [second_list[0], feed, bias_wide[None], tops_list[0]]
-            + [block for two in zip(second_list[1:], tops_list[1:]) for block in two],
-            [shape(tokens, wide, kind=LOW), shape(tokens, wide, kind=LOW)]
-            + parts()
-            + [shape(1, wide)],
-            [],
-            6 * tokens * width * wide,
-        )
+        def feed_forward(row_blocks, top_blocks, outs):
+            count = len(row_blocks)
+            pairs = list(zip(row_blocks, top_blocks))
+            return call_kernel(
+                functools.partial(feed_kernel, count),
+                [],
+                [pairs[0][0], feed, bias_wide[None], pairs[0][1]]
+                + [block for pair in pairs[1:] for block in pair],
+                [shape(count * rows, wide, kind=LOW)] * 2 + outs + [shape(1, wide)],
+                [],
+                6 * count * rows * width * wide,
+            )
+
+        active, hidden_grad, *second_parts, sums = feed_forward(
+            second_list[:3], tops_list[:3], parts()[:3]
+        )
+        active_far, hidden_far, part_far, sums_far = feed_forward(
+            second_list[3:], tops_list[3:], parts()[3:]
+        )
+        second_parts.append(part_far)
+        expand_bias_part = sums + sums_far
         second_low_parts = second_parts
         both = fold_far(second_low_parts, "second_grad")
-        both, hidden_grad, active = together(both, hidden_grad, active)
+        both, hidden_grad, active, hidden_far, active_far = together(
+            both, hidden_grad, active, hidden_far, active_far
+        )
         one, two = fold_near(second_low_parts, both, "second_grad")
-        feed_grad = weight_grads(second_list, hidden_grad, tops_list, active)
+        feed_grad = weight_grads(
+            second_list, [hidden_grad, hidden_far], tops_list, [active, active_far]
+        )
         one, two, *feed_grad = together(one, two, *feed_grad)
         second_grad = fold_end(second_low_parts, one, two)
         feed_grad = jnp.concatenate(feed_grad, axis=1)
@@ -510,11 +535,16 @@
         upstream = output_cotangent.astype(WIDE)
         middle_grad = upstream + norm_back(second_grad, gain_two, unit_two, scale_two)
         middle_list = gather_z(middle_grad.astype(LOW), "middle")
-        middle_list[1], middle_list[2], active = together(middle_list[1], middle_list[2], active)
+        middle_list[1], middle_list[2], active, active_far = together(
+            middle_list[1], middle_list[2], active, active_far
+        )
         middle_list[3] = swap_z(middle_list[2], 1, "middle_far")
         shrunk = jnp.einsum("sf,df->sd", active, feed[:, wide:], preferred_element_type=WIDE)
-        shrunk = shrunk.reshape(n_t, rows, width)
-        shrunk = [shrunk[0]] + [shrunk[k].astype(LOW) for k in range(1, n_t)]
+        shrunk = shrunk.reshape(n_t - 1, rows, width)
+        shrunk_last = jnp.einsum(
+            "sf,df->sd", active_far, feed[:, wide:], preferred_element_type=WIDE
+        )
+        shrunk = [shrunk[0], shrunk[1].astype(LOW), shrunk[2].astype(LOW), shrunk_last.astype(LOW)]
         middle_list[3], *shrunk[1:] = together(middle_list[3], *shrunk[1:])
         shrunk_both = fold_far(shrunk, "shrunk")
 
@@ -550,7 +580,7 @@
         both = fold_far(first_low, "first_grad")
         shrunk_one, shrunk_two = fold_near(shrunk, shrunk_both, "shrunk")
         vectors = vectors + swap_z(vectors, 1, "vectors")
-        in_grad, out_grad = weight_grads([normed_all], mixed_grad, middle_list, context)
+        in_grad, out_grad = weight_grads([normed_all], [mixed_grad], middle_list, [context])
         blocks = n_dp // 2
         grads = jnp.concatenate([in_grad, out_grad], axis=1).reshape(blocks, 2, -1, 4 * local)
         mine = lax.dynamic_slice_in_dim(grads, core, 1, 1)
@@ -569,7 +599,9 @@
         for mask in bits[:1]:
             vectors = vectors + swap_dp(vectors, mask, "vectors")
         attend.land()
-        first_one, first_two, vectors = gate(attend, first_one, first_two, vectors)
+        first_one, first_two, vectors, feed_sum = gate(
+            attend, first_one, first_two, vectors, feed_sum
+        )
         for mask in bits[1:]:
             vectors = vectors + swap_dp(vectors, mask, "vectors")
         vectors = vectors + swap_z(vectors, 2, "vectors")

time: 226 us -> 218 us (0.965)
  waiting for transfers between devices: 82.3 us -> 60.8 us
  starting transfers between devices: 45.1 us -> 60.5 us
  other arithmetic: 20.8 us -> 18.5 us
    ppermute x39, waiting for transfers between devices: 82.3 us -> 60.7 us  [send(): return lax.ppermute(value, AXES, pairs)]
    ppermute x39, starting transfers between devices: 45.1 us -> 60.5 us  [send(): return lax.ppermute(value, AXES, pairs)]
    pallas_call x3 -> x4, Pallas kernels: 26.5 us -> 26.7 us  [call_kernel(): pl.pallas_call(kernel, grid=(1,), in_specs=[pl.BlockSpec(memory_space=plt...]
    unnamed x96 -> x114, local copies, waits for them, and re-layouts: 15 us -> 15.2 us
  transfers between devices with their start and end apart: 41 -> 41, of which waited for: 22 -> 19; matrix products, arithmetic and copies ran while one was open for 14% -> 12% of each run, Pallas kernels for 12% -> 17%
where the time goes in v4:
time: 218 us; the launch traced here: 217 us
  waiting for transfers between devices  60.8 us (28%)
  starting transfers between devices  60.5 us (28%)
  Pallas kernels  36 us (17%)
  local copies, waits for them, and re-layouts  21.6 us (10%)
  other arithmetic  18.5 us (8%)
  between operations  15.1 us (7%)
  matrix products  4.75 us (2%)
    ppermute x39, waiting for transfers between devices, send(): return lax.ppermute(value, AXES, pairs)  60.7 us
    ppermute x39, starting transfers between devices, send(): return lax.ppermute(value, AXES, pairs)  60.5 us
    pallas_call x4, Pallas kernels, call_kernel(): pl.pallas_call(kernel, grid=(1,), in_specs=[pl.BlockSpec(memory_space=plt...  26.7 us
    unnamed x114, local copies, waits for them, and re-layouts  15.2 us
    pallas_call x2, Pallas kernels, weight_grads(): pl.pallas_call(functools.partial(grads_kernel, steps, [len(group) for gro...  9.26 us
  transfers between devices with their start and end apart: 41, of which 19 were waited for; matrix products, arithmetic and copies ran while one was open for 12% of the time, Pallas kernels for 17%

profile of v4, /device:TPU:0, one launch (start us, length us, event | category | flops | bytes accessed | tf_op | source)
XLA Modules:
  0.0 217.2 jit_solution(11304113467776993731)
XLA Ops:
  7.2 3.1 %collective-permute-start.2 = (bf16[128,1024]{1,0:T(8,128)(2,1)}, bf16[128,1024]{1,0:T(8,128)(2,1)S(1)}, u32[]{:S(2)}, u32[]{:S(2)}) collective-permute-start(bf16[128,1024]{1,0:T(8,128)(2,1)} %refs_9_.1), channel_id=1, source_target_pairs={{0,1},{1,0},{2,3},{3,2},{4,5},{5,4},{6,7},{7,6},{8,9},{9,8},{10,11... | collective-permute-start | bytes 786440 | tf_op jit(solution)/shard_map/rows_z1/ppermute | solution.py:300
  10.3 2.6 %collective-permute-start.3 = (bf16[128,1024]{1,0:T(8,128)(2,1)}, bf16[128,1024]{1,0:T(8,128)(2,1)S(1)}, u32[]{:S(2)}, u32[]{:S(2)}) collective-permute-start(bf16[128,1024]{1,0:T(8,128)(2,1)} %refs_9_.1), channel_id=1, source_target_pairs={{0,2},{1,3},{2,0},{3,1},{4,6},{5,7},{6,4},{7,5},{8,10},{9,11},{10,... | collective-permute-start | bytes 786440 | tf_op jit(solution)/shard_map/rows_z2/ppermute | solution.py:300
  22.3 2.5 %collective-permute-done.3.refs_8_.refs_11_ = bf16[128,1024]{1,0:T(8,128)(2,1)S(1)} collective-permute-done((bf16[128,1024]{1,0:T(8,128)(2,1)}, bf16[128,1024]{1,0:T(8,128)(2,1)S(1)}, u32[]{:S(2)}, u32[]{:S(2)}) %collective-permute-start.3) | collective-permute-done | bytes 262176 | tf_op jit(solution)/shard_map/rows_z2/ppermute | solution.py:300
  28.3 2.9 %collective-permute-done.4 = bf16[2,1,1,128,512]{3,4,2,1,0:T(8,128)(2,1)S(1)} collective-permute-done((bf16[2,1,1,128,512]{3,4,2,1,0:T(8,128)(2,1)S(1)}, bf16[2,1,1,128,512]{3,4,2,1,0:T(8,128)(2,1)S(1)}, u32[]{:S(2)}, u32[]{:S(2)}) %collective-permute-start.4) | collective-permute-done | bytes 262176 | tf_op jit(solution)/shard_map/att_a_d2/ppermute | solution.py:300
  36.8 2.4 %collective-permute-start.10 = (bf16[128,1024]{1,0:T(8,128)(2,1)S(1)}, bf16[128,1024]{1,0:T(8,128)(2,1)S(1)}, u32[]{:S(2)}, u32[]{:S(2)}) collective-permute-start(bf16[128,1024]{1,0:T(8,128)(2,1)S(1)} %copy-done.7), channel_id=1, source_target_pairs={{0,2},{1,3},{2,0},{3,1},{4,6},{5,7},{6,4},{7,5},{8,10},{9,11},{10,... | collective-permute-start | bytes 786440 | tf_op jit(solution)/shard_map/tops_z2/ppermute | solution.py:300
  41.0 6.6 %shard_map.245 = (bf16[512,1024]{1,0:T(8,128)(2,1)S(1)}, bf16[512,768]{1,0:T(8,128)(2,1)S(1)}, bf16[512,256]{1,0:T(8,128)(2,1)S(1)}, f32[4,512]{1,0:T(4,128)S(1)...) custom-call(f32[4]{0:T(128)S(1)} %multiply_exponential_fusion.refs_0, ...), custom_call_target="tpu_custom_call" | custom-call | flops 1342177280 | bytes 6573056 | tf_op jit(solution)/shard_map/pallas_call | solution.py:200
  51.9 1.9 collective-permute-start.8
  53.8 7.2 %collective-permute-done.11 = bf16[128,1024]{1,0:T(8,128)(2,1)S(1)} collective-permute-done((bf16[128,1024]{1,0:T(8,128)(2,1)S(1)}, bf16[128,1024]{1,0:T(8,128)(2,1)S(1)}, u32[]{:S(2)}, u32[]{:S(2)}) %collective-permute-start.11) | collective-permute-done | bytes 262176 | tf_op jit(solution)/shard_map/branch_far_z1/ppermute | solution.py:300
  62.1 5.4 %collective-permute-done.8 = bf16[128,1024]{1,0:T(8,128)(2,1)S(1)} collective-permute-done((bf16[128,1024]{1,0:T(8,128)(2,1)S(1)}, bf16[128,1024]{1,0:T(8,128)(2,1)S(1)}, u32[]{:S(2)}, u32[]{:S(2)}) %collective-permute-start.8) | collective-permute-done | bytes 262176 | tf_op jit(solution)/shard_map/branch_z1/ppermute | solution.py:300
  67.5 6.2 %collective-permute-done.12 = bf16[128,1024]{1,0:T(8,128)(2,1)S(1)} collective-permute-done((bf16[128,1024]{1,0:T(8,128)(2,1)S(1)}, bf16[128,1024]{1,0:T(8,128)(2,1)S(1)}, u32[]{:S(2)}, u32[]{:S(2)}) %collective-permute-start.12) | collective-permute-done | bytes 262176 | tf_op jit(solution)/shard_map/branch_z2/ppermute | solution.py:300
  75.0 2.6 %collective-permute-start.17 = (bf16[128,1024]{1,0:T(8,128)(2,1)S(1)}, bf16[128,1024]{1,0:T(8,128)(2,1)S(1)}, u32[]{:S(2)}, u32[]{:S(2)}) collective-permute-start(bf16[128,1024]{1,0:T(8,128)(2,1)S(1)} %copy-done.16), channel_id=1, source_target_pairs={{0,1},{1,0},{2,3},{3,2},{4,5},{5,4},{6,7},{7,6},{8,9},{9,8},{10,11... | collective-permute-start | bytes 786440 | tf_op jit(solution)/shard_map/tops_far_z1/ppermute | solution.py:300
  77.6 8.1 %collective-permute-done.14.refs_6_.refs_2_ = bf16[128,1024]{1,0:T(8,128)(2,1)S(1)} collective-permute-done((bf16[128,1024]{1,0:T(8,128)(2,1)S(1)}, bf16[128,1024]{1,0:T(8,128)(2,1)S(1)}, u32[]{:S(2)}, u32[]{:S(2)}) %collective-permute-start.14) | collective-permute-done | bytes 262176 | tf_op jit(solution)/shard_map/second_z2/ppermute | solution.py:300
  87.8 7.2 %collective-permute-done.16.refs_0_.refs_3_ = bf16[128,1024]{1,0:T(8,128)(2,1)S(1)} collective-permute-done((bf16[128,1024]{1,0:T(8,128)(2,1)S(1)}, bf16[128,1024]{1,0:T(8,128)(2,1)S(1)}, u32[]{:S(2)}, u32[]{:S(2)}) %collective-permute-start.16) | collective-permute-done | bytes 262176 | tf_op jit(solution)/shard_map/second_far_z1/ppermute | solution.py:300
  95.0 2.2 %copy-done = bf16[1024,2048]{1,0:T(8,128)(2,1)S(1)} copy-done((bf16[1024,2048]{1,0:T(8,128)(2,1)S(1)}, bf16[1024,2048]{1,0:T(8,128)(2,1)}, u32[]{:S(2)}) %copy-start) | copy-done | bytes 4194328
  97.2 2.3 %shard_map.247 = (bf16[128,1024]{1,0:T(8,128)(2,1)S(1)}, bf16[128,1024]{1,0:T(8,128)(2,1)S(1)}, bf16[128,1024]{1,0:T(8,128)(2,1)S(1)}, f32[1,1024]{1,0:T(1,128)S(1)}) custom-call(bf16[128,1024]{1,0:T(8,128)(2,1)S(1)} %collective-permute-done.16.refs_0_.refs_3_, bf16[1024,2048]{1,0:T(8,128)(2,1)S(1)} %copy-done, f32[1,1024]{1,0:T(1,128)S(1)} %bitcast.65, ...), custom_call_target="tpu_custom_call" | custom-call | flops 805306368 | bytes 5513216 | tf_op jit(solution)/shard_map/pallas_call | solution.py:200
  100.0 6.3 %shard_map.246 = (bf16[384,1024]{1,0:T(8,128)(2,1)S(1)}, bf16[384,1024]{1,0:T(8,128)(2,1)S(1)}, f32[128,1024]{1,0:T(8,128)S(1)}, bf16[128,1024]{1,0:T(8,128)(2,1...) custom-call(bf16[128,1024]{1,0:T(8,128)(2,1)S(1)} %add_convert_fusion.6.refs_0_, ...), custom_call_target="tpu_custom_call" | custom-call | flops 2415919104 | bytes 8396800 | tf_op jit(solution)/shard_map/pallas_call | solution.py:200
  108.1 2.0 collective-permute-start.19
  110.0 6.4 %shard_map.248 = (bf16[1024,1024]{1,0:T(8,128)(2,1)S(1)}, bf16[1024,1024]{1,0:T(8,128)(2,1)S(1)}) custom-call(bf16[128,1024]{1,0:T(8,128)(2,1)S(1)} %add_convert_fusion.6.refs_0_, bf16[128,1024]{1,0:T(8,128)(2,1)S(1)} %collective-permute-done.13.refs_4_.refs_1_, bf16[128,1024]{1,0:T(8,128)(2,1)S(1)} %collective-permute-done.14.refs_6_.refs_2_, ...), custom_call_target="tpu_custom_call" | custom-call | flops 2147483648 | bytes 6291456 | tf_op jit(solution)/shard_map/pallas_call | solution.py:270
  117.7 2.5 %pad_maximum_fusion = bf16[1024,2048]{1,0:T(8,128)(2,1)} fusion(bf16[1024,1024]{1,0:T(8,128)(2,1)S(1)} %get-tuple-element.177, bf16[1024,1024]{1,0:T(8,128)(2,1)S(1)} %get-tuple-element.176), kind=kLoop, calls=%fused_computation | loop fusion | flops 8388608 | bytes 8388608 | tf_op jit(solution)/shard_map/concatenate | solution.py:531
  121.6 3.4 %collective-permute-start.20 = (bf16[128,1024]{1,0:T(8,128)(2,1)S(1)}, bf16[128,1024]{1,0:T(8,128)(2,1)S(1)}, u32[]{:S(2)}, u32[]{:S(2)}) collective-permute-start(bf16[128,1024]{1,0:T(8,128)(2,1)S(1)} %convert_element_type.182.refs_2_), channel_id=1, source_target_pairs={{0,1},{1,0},{2,3},{3,2},{4,5},{5,4},{6,7},{7,6},{8,9},{9,8},{10,11... | collective-permute-start | bytes 786440 | tf_op jit(solution)/shard_map/middle_z1/ppermute | solution.py:300
  125.0 2.8 %collective-permute-start.21 = (bf16[128,1024]{1,0:T(8,128)(2,1)S(1)}, bf16[128,1024]{1,0:T(8,128)(2,1)S(1)}, u32[]{:S(2)}, u32[]{:S(2)}) collective-permute-start(bf16[128,1024]{1,0:T(8,128)(2,1)S(1)} %convert_element_type.182.refs_2_), channel_id=1, source_target_pairs={{0,2},{1,3},{2,0},{3,1},{4,6},{5,7},{6,4},{7,5},{8,10},{9,11},{10,... | collective-permute-start | bytes 786440 | tf_op jit(solution)/shard_map/middle_z2/ppermute | solution.py:300
  127.9 4.2 %collective-permute-done.20.refs_4_.refs_3_ = bf16[128,1024]{1,0:T(8,128)(2,1)S(1)} collective-permute-done((bf16[128,1024]{1,0:T(8,128)(2,1)S(1)}, bf16[128,1024]{1,0:T(8,128)(2,1)S(1)}, u32[]{:S(2)}, u32[]{:S(2)}) %collective-permute-start.20) | collective-permute-done | bytes 262176 | tf_op jit(solution)/shard_map/middle_z1/ppermute | solution.py:300
  134.0 3.1 %collective-permute-start.22 = (bf16[128,1024]{1,0:T(8,128)(2,1)S(1)}, bf16[128,1024]{1,0:T(8,128)(2,1)S(1)}, u32[]{:S(2)}, u32[]{:S(2)}) collective-permute-start(bf16[128,1024]{1,0:T(8,128)(2,1)S(1)} %collective-permute-done.21.refs_5_.refs_4_), channel_id=1, source_target_pairs={{0,1},{1,0},{2,3},{3,2},{4,5},{5,4},{6,7},{7,6},{8,9},{9,8},{10,11... | collective-permute-start | bytes 786440 | tf_op jit(solution)/shard_map/middle_far_z1/ppermute | solution.py:300
  137.1 3.9 %fusion.33 = (bf16[384,1024]{1,0:T(8,128)(2,1)S(1)}, f32[384,1024]{1,0:T(8,128)}) fusion(bf16[384,1024]{1,0:T(8,128)(2,1)S(1)} %copy-done.26, bf16[1024,2048]{1,0:T(8,128)(2,1)} %all-gather.2.cloned.1.call-done.refs_1_), kind=kOutput, calls=%fused_computation.100 | convolution fusion | flops 805699584 | bytes 5242880 | tf_op jit(solution)/shard_map/sf,df->sd/dot_general | solution.py:542
  145.5 11.4 %shard_map.249 = (bf16[512,768]{1,0:T(8,128)(2,1)}, f32[128,1024]{1,0:T(8,128)}, bf16[128,1024]{1,0:T(8,128)(2,1)}, bf16[128,1024]{1,0:T(8,128)(2,1)}, bf16[128,...) custom-call(f32[4]{0:T(128)} %copy-done.24, s32[4]{0:T(128)} %copy-done.23, bf16[128,1024]{1,0:T(8,128)(2,1)} %copy-done.5, ...), custom_call_target="tpu_custom_call" | custom-call | flops 1744830464 | bytes 7097344 | tf_op jit(solution)/shard_map/pallas_call | solution.py:200
  161.7 2.9 %collective-permute-start.27 = (bf16[128,1024]{1,0:T(8,128)(2,1)S(1)}, bf16[128,1024]{1,0:T(8,128)(2,1)S(1)}, u32[]{:S(2)}, u32[]{:S(2)}) collective-permute-start(bf16[128,1024]{1,0:T(8,128)(2,1)S(1)} %add_convert_fusion.4), channel_id=1, source_target_pairs={{0,2},{1,3},{2,0},{3,1},{4,6},{5,7},{6,4},{7,5},{8,10},{9,11},{10,... | collective-permute-start | bytes 786440 | tf_op jit(solution)/shard_map/shrunk_z2/ppermute | solution.py:300
  166.8 2.9 %shard_map.250 = (bf16[1024,768]{1,0:T(8,128)(2,1)S(1)}, bf16[1024,256]{1,0:T(8,128)(2,1)S(1)}) custom-call(bf16[512,1024]{1,0:T(8,128)(2,1)S(1)} %copy-done.28, bf16[512,768]{1,0:T(8,128)(2,1)S(1)} %copy-done.29, bf16[128,1024]{1,0:T(8,128)(2,1)S(1)} %copy-done.6, bf16[128,1024]{1,0:T(8,128)(2,1)S(1)} %copy-done.18, bf16[128,1024]{1,0:T(8,128)(2,1)S(1)} %copy-done.20, ...), custom_call_target="tpu_custom_call" | custom-call | flops 1073741824 | bytes 4194304 | tf_op jit(solution)/shard_map/pallas_call | solution.py:270
  174.2 2.3 %collective-permute-start.32 = (bf16[128,1024]{1,0:T(8,128)(2,1)}, bf16[128,1024]{1,0:T(8,128)(2,1)}, u32[]{:S(2)}, u32[]{:S(2)}) collective-permute-start(bf16[128,1024]{1,0:T(8,128)(2,1)} %get-tuple-element.173), channel_id=1, source_target_pairs={{0,1},{1,0},{2,3},{3,2},{4,5},{5,4},{6,7},{7,6},{8,9},{9,8},{10,11... | collective-permute-start | bytes 786440 | tf_op jit(solution)/shard_map/first_grad_z1/ppermute | solution.py:300
  180.2 5.6 %collective-permute-start.30 = (bf16[2,1,128,512]{2,3,1,0:T(8,128)(2,1)S(1)}, bf16[2,1,128,512]{2,3,1,0:T(8,128)(2,1)S(1)}, u32[]{:S(2)}, u32[]{:S(2)}) collective-permute-start(bf16[2,1,128,512]{2,3,1,0:T(8,128)(2,1)S(1)} %constant_dynamic-slice_fusion.5), channel_id=1, source_target_pairs={{0,8},{1,9},{2,10},{3,11},{4,12},{5,13},{6,14},{7,15},{8,0},{9,1},... | collective-permute-start | bytes 786440 | tf_op jit(solution)/shard_map/att_grad_a_d2/ppermute | solution.py:300
  187.6 1.9 fusion.22
  189.6 3.7 %collective-permute-done.34 = f32[12,1024]{1,0:T(8,128)S(1)} collective-permute-done((f32[12,1024]{1,0:T(8,128)S(1)}, f32[12,1024]{1,0:T(8,128)S(1)}, u32[]{:S(2)}, u32[]{:S(2)}) %collective-permute-start.34) | collective-permute-done | bytes 49184 | tf_op jit(solution)/shard_map/vectors_d2/ppermute | solution.py:300
  204.1 2.7 %collective-permute-done.36 = f32[12,1024]{1,0:T(8,128)S(1)} collective-permute-done((f32[12,1024]{1,0:T(8,128)S(1)}, f32[12,1024]{1,0:T(8,128)S(1)}, u32[]{:S(2)}, u32[]{:S(2)}) %collective-permute-start.36) | collective-permute-done | bytes 49184 | tf_op jit(solution)/shard_map/vectors_z2/ppermute | solution.py:300
  (264 shorter events, 70.8 us)
Async XLA Ops:
  7.2 66.5 %all-gather.2.cloned.1.call-start = ((), (), s32[]{:S(2)}) async-start(), calls=%async_computation.1 | async-start | bytes 4718592 | tf_op jit(solution)/shard_map/all_gather | solution.py:464
  7.2 15.1 %collective-permute-start.2 = (bf16[128,1024]{1,0:T(8,128)(2,1)}, bf16[128,1024]{1,0:T(8,128)(2,1)S(1)}, u32[]{:S(2)}, u32[]{:S(2)}) collective-permute-start(bf16[128,1024]{1,0:T(8,128)(2,1)} %refs_9_.1), channel_id=1, source_target_pairs={{0,1},{1,0},{2,3},{3,2},{4,5},{5,4},{6,7},{7,6},{8,9},{9,8},{10,11... | collective-permute-start | bytes 786440 | tf_op jit(solution)/shard_map/rows_z1/ppermute | solution.py:300
  10.3 14.6 %collective-permute-start.3 = (bf16[128,1024]{1,0:T(8,128)(2,1)}, bf16[128,1024]{1,0:T(8,128)(2,1)S(1)}, u32[]{:S(2)}, u32[]{:S(2)}) collective-permute-start(bf16[128,1024]{1,0:T(8,128)(2,1)} %refs_9_.1), channel_id=1, source_target_pairs={{0,2},{1,3},{2,0},{3,1},{4,6},{5,7},{6,4},{7,5},{8,10},{9,11},{10,... | collective-permute-start | bytes 786440 | tf_op jit(solution)/shard_map/rows_z2/ppermute | solution.py:300
  14.0 6.9 %collective-permute-start = (bf16[1,1,1,128,512]{3,4,2,1,0:T(8,128)(2,1)S(1)}, bf16[1,1,1,128,512]{3,4,2,1,0:T(8,128)(2,1)S(1)}, u32[]{:S(2)}, u32[]{:S(2)}) collective-permute-start(bf16[1,1,1,128,512]{3,4,2,1,0:T(8,128)(2,1)S(1)} %slice_bitcast_fusion.1), channel_id=1, source_target_pairs={{0,16},{1,17},{2,18},{3,19},{4,20},{5,21},{6,22},{7,23},{8,24},{9,... | collective-permute-start | bytes 393224 | tf_op jit(solution)/shard_map/att_a_d4/ppermute | solution.py:300
  34.3 159.1 %reduce-scatter.2.cloned.1.call-start = ((), (), s32[]{:S(2)}) async-start(), calls=%async_computation.2 | async-start | bytes 4718592 | tf_op jit(solution)/shard_map/reduce_scatter | solution.py:532
  36.1 13.9 %collective-permute-start.9 = (bf16[128,1024]{1,0:T(8,128)(2,1)S(1)}, bf16[128,1024]{1,0:T(8,128)(2,1)S(1)}, u32[]{:S(2)}, u32[]{:S(2)}) collective-permute-start(bf16[128,1024]{1,0:T(8,128)(2,1)S(1)} %copy-done.7), channel_id=1, source_target_pairs={{0,1},{1,0},{2,3},{3,2},{4,5},{5,4},{6,7},{7,6},{8,9},{9,8},{10,11... | collective-permute-start | bytes 786440 | tf_op jit(solution)/shard_map/tops_z1/ppermute | solution.py:300
  36.8 15.0 %collective-permute-start.10 = (bf16[128,1024]{1,0:T(8,128)(2,1)S(1)}, bf16[128,1024]{1,0:T(8,128)(2,1)S(1)}, u32[]{:S(2)}, u32[]{:S(2)}) collective-permute-start(bf16[128,1024]{1,0:T(8,128)(2,1)S(1)} %copy-done.7), channel_id=1, source_target_pairs={{0,2},{1,3},{2,0},{3,1},{4,6},{5,7},{6,4},{7,5},{8,10},{9,11},{10,... | collective-permute-start | bytes 786440 | tf_op jit(solution)/shard_map/tops_z2/ppermute | solution.py:300
  51.8 9.3 %collective-permute-start.11 = (bf16[128,1024]{1,0:T(8,128)(2,1)S(1)}, bf16[128,1024]{1,0:T(8,128)(2,1)S(1)}, u32[]{:S(2)}, u32[]{:S(2)}) collective-permute-start(bf16[128,1024]{1,0:T(8,128)(2,1)S(1)} %get-tuple-element.115), channel_id=1, source_target_pairs={{0,1},{1,0},{2,3},{3,2},{4,5},{5,4},{6,7},{7,6},{8,9},{9,8},{10,11... | collective-permute-start | bytes 786440 | tf_op jit(solution)/shard_map/branch_far_z1/ppermute | solution.py:300
  51.9 15.5 %collective-permute-start.8 = (bf16[128,1024]{1,0:T(8,128)(2,1)S(1)}, bf16[128,1024]{1,0:T(8,128)(2,1)S(1)}, u32[]{:S(2)}, u32[]{:S(2)}) collective-permute-start(bf16[128,1024]{1,0:T(8,128)(2,1)S(1)} %get-tuple-element.111), channel_id=1, source_target_pairs={{0,1},{1,0},{2,3},{3,2},{4,5},{5,4},{6,7},{7,6},{8,9},{9,8},{10,11... | collective-permute-start | bytes 786440 | tf_op jit(solution)/shard_map/branch_z1/ppermute | solution.py:300
  61.1 12.5 %collective-permute-start.12 = (bf16[128,1024]{1,0:T(8,128)(2,1)S(1)}, bf16[128,1024]{1,0:T(8,128)(2,1)S(1)}, u32[]{:S(2)}, u32[]{:S(2)}) collective-permute-start(bf16[128,1024]{1,0:T(8,128)(2,1)S(1)} %add_convert_fusion.7), channel_id=1, source_target_pairs={{0,2},{1,3},{2,0},{3,1},{4,6},{5,7},{6,4},{7,5},{8,10},{9,11},{10,... | collective-permute-start | bytes 786440 | tf_op jit(solution)/shard_map/branch_z2/ppermute | solution.py:300
  74.9 10.8 %collective-permute-start.14 = (bf16[128,1024]{1,0:T(8,128)(2,1)S(1)}, bf16[128,1024]{1,0:T(8,128)(2,1)S(1)}, u32[]{:S(2)}, u32[]{:S(2)}) collective-permute-start(bf16[128,1024]{1,0:T(8,128)(2,1)S(1)} %add_convert_fusion.6.refs_0_), channel_id=1, source_target_pairs={{0,2},{1,3},{2,0},{3,1},{4,6},{5,7},{6,4},{7,5},{8,10},{9,11},{10,... | collective-permute-start | bytes 786440 | tf_op jit(solution)/shard_map/second_z2/ppermute | solution.py:300
  75.0 12.8 %collective-permute-start.17 = (bf16[128,1024]{1,0:T(8,128)(2,1)S(1)}, bf16[128,1024]{1,0:T(8,128)(2,1)S(1)}, u32[]{:S(2)}, u32[]{:S(2)}) collective-permute-start(bf16[128,1024]{1,0:T(8,128)(2,1)S(1)} %copy-done.16), channel_id=1, source_target_pairs={{0,1},{1,0},{2,3},{3,2},{4,5},{5,4},{6,7},{7,6},{8,9},{9,8},{10,11... | collective-permute-start | bytes 786440 | tf_op jit(solution)/shard_map/tops_far_z1/ppermute | solution.py:300
  85.7 9.2 %collective-permute-start.16 = (bf16[128,1024]{1,0:T(8,128)(2,1)S(1)}, bf16[128,1024]{1,0:T(8,128)(2,1)S(1)}, u32[]{:S(2)}, u32[]{:S(2)}) collective-permute-start(bf16[128,1024]{1,0:T(8,128)(2,1)S(1)} %collective-permute-done.14.refs_6_.refs_2_), channel_id=1, source_target_pairs={{0,1},{1,0},{2,3},{3,2},{4,5},{5,4},{6,7},{7,6},{8,9},{9,8},{10,11... | collective-permute-start | bytes 786440 | tf_op jit(solution)/shard_map/second_far_z1/ppermute | solution.py:300
  86.2 13.8 %collective-permute-start.13 = (bf16[128,1024]{1,0:T(8,128)(2,1)S(1)}, bf16[128,1024]{1,0:T(8,128)(2,1)S(1)}, u32[]{:S(2)}, u32[]{:S(2)}) collective-permute-start(bf16[128,1024]{1,0:T(8,128)(2,1)S(1)} %add_convert_fusion.6.refs_0_), channel_id=1, source_target_pairs={{0,1},{1,0},{2,3},{3,2},{4,5},{5,4},{6,7},{7,6},{8,9},{9,8},{10,11... | collective-permute-start | bytes 786440 | tf_op jit(solution)/shard_map/second_z1/ppermute | solution.py:300
  99.5 8.5 %collective-permute-start.18 = (bf16[128,1024]{1,0:T(8,128)(2,1)S(1)}, bf16[128,1024]{1,0:T(8,128)(2,1)S(1)}, u32[]{:S(2)}, u32[]{:S(2)}) collective-permute-start(bf16[128,1024]{1,0:T(8,128)(2,1)S(1)} %get-tuple-element.126), channel_id=1, source_target_pairs={{0,1},{1,0},{2,3},{3,2},{4,5},{5,4},{6,7},{7,6},{8,9},{9,8},{10,11... | collective-permute-start | bytes 786440 | tf_op jit(solution)/shard_map/second_grad_far_z1/ppermute | solution.py:300
  106.4 10.1 %collective-permute-start.15 = (bf16[128,1024]{1,0:T(8,128)(2,1)S(1)}, bf16[128,1024]{1,0:T(8,128)(2,1)S(1)}, u32[]{:S(2)}, u32[]{:S(2)}) collective-permute-start(bf16[128,1024]{1,0:T(8,128)(2,1)S(1)} %get-tuple-element.124), channel_id=1, source_target_pairs={{0,1},{1,0},{2,3},{3,2},{4,5},{5,4},{6,7},{7,6},{8,9},{9,8},{10,11... | collective-permute-start | bytes 786440 | tf_op jit(solution)/shard_map/second_grad_z1/ppermute | solution.py:300
  108.1 9.3 %collective-permute-start.19 = (bf16[128,1024]{1,0:T(8,128)(2,1)S(1)}, bf16[128,1024]{1,0:T(8,128)(2,1)S(1)}, u32[]{:S(2)}, u32[]{:S(2)}) collective-permute-start(bf16[128,1024]{1,0:T(8,128)(2,1)S(1)} %add_convert_fusion.5), channel_id=1, source_target_pairs={{0,2},{1,3},{2,0},{3,1},{4,6},{5,7},{6,4},{7,5},{8,10},{9,11},{10,... | collective-permute-start | bytes 786440 | tf_op jit(solution)/shard_map/second_grad_z2/ppermute | solution.py:300
  121.6 10.6 %collective-permute-start.20 = (bf16[128,1024]{1,0:T(8,128)(2,1)S(1)}, bf16[128,1024]{1,0:T(8,128)(2,1)S(1)}, u32[]{:S(2)}, u32[]{:S(2)}) collective-permute-start(bf16[128,1024]{1,0:T(8,128)(2,1)S(1)} %convert_element_type.182.refs_2_), channel_id=1, source_target_pairs={{0,1},{1,0},{2,3},{3,2},{4,5},{5,4},{6,7},{7,6},{8,9},{9,8},{10,11... | collective-permute-start | bytes 786440 | tf_op jit(solution)/shard_map/middle_z1/ppermute | solution.py:300
  125.0 9.0 %collective-permute-start.21 = (bf16[128,1024]{1,0:T(8,128)(2,1)S(1)}, bf16[128,1024]{1,0:T(8,128)(2,1)S(1)}, u32[]{:S(2)}, u32[]{:S(2)}) collective-permute-start(bf16[128,1024]{1,0:T(8,128)(2,1)S(1)} %convert_element_type.182.refs_2_), channel_id=1, source_target_pairs={{0,2},{1,3},{2,0},{3,1},{4,6},{5,7},{6,4},{7,5},{8,10},{9,11},{10,... | collective-permute-start | bytes 786440 | tf_op jit(solution)/shard_map/middle_z2/ppermute | solution.py:300
  134.0 9.9 %collective-permute-start.22 = (bf16[128,1024]{1,0:T(8,128)(2,1)S(1)}, bf16[128,1024]{1,0:T(8,128)(2,1)S(1)}, u32[]{:S(2)}, u32[]{:S(2)}) collective-permute-start(bf16[128,1024]{1,0:T(8,128)(2,1)S(1)} %collective-permute-done.21.refs_5_.refs_4_), channel_id=1, source_target_pairs={{0,1},{1,0},{2,3},{3,2},{4,5},{5,4},{6,7},{7,6},{8,9},{9,8},{10,11... | collective-permute-start | bytes 786440 | tf_op jit(solution)/shard_map/middle_far_z1/ppermute | solution.py:300
  143.9 14.7 %collective-permute-start.23 = (bf16[128,1024]{1,0:T(8,128)(2,1)S(1)}, bf16[128,1024]{1,0:T(8,128)(2,1)S(1)}, u32[]{:S(2)}, u32[]{:S(2)}) collective-permute-start(bf16[128,1024]{1,0:T(8,128)(2,1)S(1)} %fusion.4), channel_id=1, source_target_pairs={{0,1},{1,0},{2,3},{3,2},{4,5},{5,4},{6,7},{7,6},{8,9},{9,8},{10,11... | collective-permute-start | bytes 786440 | tf_op jit(solution)/shard_map/shrunk_far_z1/ppermute | solution.py:300
  158.7 11.5 %collective-permute-start.24 = (bf16[128,1024]{1,0:T(8,128)(2,1)}, bf16[128,1024]{1,0:T(8,128)(2,1)S(1)}, u32[]{:S(2)}, u32[]{:S(2)}) collective-permute-start(bf16[128,1024]{1,0:T(8,128)(2,1)} %get-tuple-element.157), channel_id=1, source_target_pairs={{0,1},{1,0},{2,3},{3,2},{4,5},{5,4},{6,7},{7,6},{8,9},{9,8},{10,11... | collective-permute-start | bytes 786440 | tf_op jit(solution)/shard_map/first_grad_far_z1/ppermute | solution.py:300
  159.7 10.4 %collective-permute-start.25 = (f32[12,1024]{1,0:T(8,128)S(1)}, f32[12,1024]{1,0:T(8,128)S(1)}, u32[]{:S(2)}, u32[]{:S(2)}) collective-permute-start(f32[12,1024]{1,0:T(8,128)S(1)} %concatenate.44), channel_id=1, source_target_pairs={{0,1},{1,0},{2,3},{3,2},{4,5},{5,4},{6,7},{7,6},{8,9},{9,8},{10,11... | collective-permute-start | bytes 147464 | tf_op jit(solution)/shard_map/vectors_z1/ppermute | solution.py:300
  160.7 10.9 %collective-permute-start.26 = (bf16[128,1024]{1,0:T(8,128)(2,1)}, bf16[128,1024]{1,0:T(8,128)(2,1)S(1)}, u32[]{:S(2)}, u32[]{:S(2)}) collective-permute-start(bf16[128,1024]{1,0:T(8,128)(2,1)} %get-tuple-element.164), channel_id=1, source_target_pairs={{0,1},{1,0},{2,3},{3,2},{4,5},{5,4},{6,7},{7,6},{8,9},{9,8},{10,11... | collective-permute-start | bytes 786440 | tf_op jit(solution)/shard_map/shrunk_z1/ppermute | solution.py:300
  161.7 10.6 %collective-permute-start.27 = (bf16[128,1024]{1,0:T(8,128)(2,1)S(1)}, bf16[128,1024]{1,0:T(8,128)(2,1)S(1)}, u32[]{:S(2)}, u32[]{:S(2)}) collective-permute-start(bf16[128,1024]{1,0:T(8,128)(2,1)S(1)} %add_convert_fusion.4), channel_id=1, source_target_pairs={{0,2},{1,3},{2,0},{3,1},{4,6},{5,7},{6,4},{7,5},{8,10},{9,11},{10,... | collective-permute-start | bytes 786440 | tf_op jit(solution)/shard_map/shrunk_z2/ppermute | solution.py:300
  174.2 20.5 %collective-permute-start.32 = (bf16[128,1024]{1,0:T(8,128)(2,1)}, bf16[128,1024]{1,0:T(8,128)(2,1)}, u32[]{:S(2)}, u32[]{:S(2)}) collective-permute-start(bf16[128,1024]{1,0:T(8,128)(2,1)} %get-tuple-element.173), channel_id=1, source_target_pairs={{0,1},{1,0},{2,3},{3,2},{4,5},{5,4},{6,7},{7,6},{8,9},{9,8},{10,11... | collective-permute-start | bytes 786440 | tf_op jit(solution)/shard_map/first_grad_z1/ppermute | solution.py:300
  176.5 18.2 %collective-permute-start.33 = (bf16[128,1024]{1,0:T(8,128)(2,1)S(1)}, bf16[128,1024]{1,0:T(8,128)(2,1)}, u32[]{:S(2)}, u32[]{:S(2)}) collective-permute-start(bf16[128,1024]{1,0:T(8,128)(2,1)S(1)} %add_convert_fusion.3), channel_id=1, source_target_pairs={{0,2},{1,3},{2,0},{3,1},{4,6},{5,7},{6,4},{7,5},{8,10},{9,11},{10,... | collective-permute-start | bytes 786440 | tf_op jit(solution)/shard_map/first_grad_z2/ppermute | solution.py:300
  180.2 13.0 %collective-permute-start.30 = (bf16[2,1,128,512]{2,3,1,0:T(8,128)(2,1)S(1)}, bf16[2,1,128,512]{2,3,1,0:T(8,128)(2,1)S(1)}, u32[]{:S(2)}, u32[]{:S(2)}) collective-permute-start(bf16[2,1,128,512]{2,3,1,0:T(8,128)(2,1)S(1)} %constant_dynamic-slice_fusion.5), channel_id=1, source_target_pairs={{0,8},{1,9},{2,10},{3,11},{4,12},{5,13},{6,14},{7,15},{8,0},{9,1},... | collective-permute-start | bytes 786440 | tf_op jit(solution)/shard_map/att_grad_a_d2/ppermute | solution.py:300
  185.8 7.5 %collective-permute-start.31 = (bf16[1,2,128,512]{2,3,1,0:T(8,128)(2,1)S(1)}, bf16[1,2,128,512]{2,3,1,0:T(8,128)(2,1)S(1)}, u32[]{:S(2)}, u32[]{:S(2)}) collective-permute-start(bf16[1,2,128,512]{2,3,1,0:T(8,128)(2,1)S(1)} %constant_dynamic-slice_fusion.4), channel_id=1, source_target_pairs={{0,16},{1,17},{2,18},{3,19},{4,20},{5,21},{6,22},{7,23},{8,24},{9,... | collective-permute-start | bytes 786440 | tf_op jit(solution)/shard_map/att_grad_b_d4/ppermute | solution.py:300
  186.4 6.9 %collective-permute-start.34 = (f32[12,1024]{1,0:T(8,128)S(1)}, f32[12,1024]{1,0:T(8,128)S(1)}, u32[]{:S(2)}, u32[]{:S(2)}) collective-permute-start(f32[12,1024]{1,0:T(8,128)S(1)} %add.212), channel_id=1, source_target_pairs={{0,8},{1,9},{2,10},{3,11},{4,12},{5,13},{6,14},{7,15},{8,0},{9,1},... | collective-permute-start | bytes 147464 | tf_op jit(solution)/shard_map/vectors_d2/ppermute | solution.py:300
  197.7 11.0 %collective-permute-start.37 = (bf16[1,1,128,512]{2,3,1,0:T(8,128)(2,1)S(1)}, bf16[1,1,128,512]{2,3,1,0:T(8,128)(2,1)S(1)}, u32[]{:S(2)}, u32[]{:S(2)}) collective-permute-start(bf16[1,1,128,512]{2,3,1,0:T(8,128)(2,1)S(1)} %constant_dynamic-slice_fusion.3), channel_id=1, source_target_pairs={{0,16},{1,17},{2,18},{3,19},{4,20},{5,21},{6,22},{7,23},{8,24},{9,... | collective-permute-start | bytes 393224 | tf_op jit(solution)/shard_map/att_grad_a_d4/ppermute | solution.py:300
  198.2 10.5 %collective-permute-start.38 = (bf16[1,1,128,512]{2,3,1,0:T(8,128)(2,1)S(1)}, bf16[1,1,128,512]{2,3,1,0:T(8,128)(2,1)S(1)}, u32[]{:S(2)}, u32[]{:S(2)}) collective-permute-start(bf16[1,1,128,512]{2,3,1,0:T(8,128)(2,1)S(1)} %constant_dynamic-slice_fusion.2), channel_id=1, source_target_pairs={{0,8},{1,9},{2,10},{3,11},{4,12},{5,13},{6,14},{7,15},{8,0},{9,1},... | collective-permute-start | bytes 393224 | tf_op jit(solution)/shard_map/att_grad_b_d2/ppermute | solution.py:300
  (63 other events, 548.9 us)
Sparse Core Ops, SparseCore 0:
  34.4 34.9 all-gather.1
  120.3 54.3 reduce-scatter.1
